TPU v7x, 32 devices: a whole 2x2x4 slice. The times are simulated.
32 devices in a mesh: cls: 4 (over x, core), dom: 8 (over z, y).
Axes of the slice: x: 2, y: 2, z: 4, core: 2. Of those that a mesh axis runs over, the one named last changes fastest.
Arguments:
- particles: bfloat16 [128, 36864], P(('cls', 'dom')), may hold values from -6 to 6
- references: bfloat16 [200, 36864], P('cls'), may hold values from -0.03125 to 0.03125
- candidates: int32 [128, 8], P(('cls', 'dom')), may hold values from 0 to 199, as said below
- offsets: int32 [128, 2], P(('cls', 'dom')), may hold values from -7 to 7
Outputs:
- class_average: bfloat16 [200, 36864], P('cls')
Inputs may be any that keep to these rules, and one draw needn't show every extreme that they name: `candidates`: each particle lists 8 distinct classes, 4 of them with each of two class owners, the owner of class c being c // (200 / number of cls groups). Of the 4 particles of one device at most 2 list classes of one owner, and on every device some owner is listed by exactly 2.
All inputs are finite; a program needn't handle non-finite values.
Results may differ from a plain program's by a relative error of at most 0.0074.
Values may be sent and summed in bfloat16 or wider, within the bound.
No kernel may reach another device: no remote copies, remote signals or barrier semaphores. Data moves between devices by JAX's collectives and lax.ppermute only.
A program may use at most 128 MiB of HBM per device.

v0:
```python
import functools
import math

import jax
import jax.numpy as jnp
import numpy as np
from jax import lax
from jax.experimental import pallas as pl
from jax.experimental.pallas import tpu as pltpu
from jax.sharding import PartitionSpec as P

CYCLES = 128
ANGLES = 144
ROT = 36
SHIFTS = 5
BOX = 256
LANES = 128
SPAN = 40
STEP_ANGLES = ANGLES // ROT
PIECES = 2 * STEP_ANGLES
IMAGE_ROWS = PIECES * SPAN
REACH = 7

SOFTMAX_WARMTH = 2.0
PRIOR_MASS = 1.0
NEGATIVE = -1e30
META_ROWS = 16
VMEM_LIMIT = 60 * 1024 * 1024
DOM, OWNER, SLOT, CLASS = 0, 1, 3, 5
FILLED, OTHER, OTHER_SLOT = 0, 1, 2


def trig_tables():
    theta = 2.0 * np.pi * np.arange(ANGLES) / ANGLES
    radius = np.arange(1, CYCLES + 1)
    out = np.zeros((4, REACH + 1, STEP_ANGLES, SPAN, CYCLES), np.float32)
    for axis, direction in enumerate((np.cos(theta), np.sin(theta))):
        for t in range(REACH + 1):
            phase = 2.0 * np.pi / BOX * t * direction[:, None] * radius[None, :]
            for part, fn in enumerate((np.cos, np.sin)):
                table = fn(phase).reshape(ROT, STEP_ANGLES, CYCLES).transpose(1, 0, 2)
                out[2 * axis + part, t, :, :ROT] = table[:, ::-1]
    return out.reshape(4, REACH + 1, STEP_ANGLES * SPAN, CYCLES)


def axis_phase(table_ref, axis, step, move):
    size = jnp.abs(move)
    sign = jnp.where(move < 0, -1.0, 1.0).astype(jnp.float32)
    at = pl.ds(step * SPAN, SPAN)
    return table_ref[2 * axis, size, at, :], table_ref[2 * axis + 1, size, at, :] * sign


def prep_kernel(local, place_ref, near_ref, far_ref, image_near, image_far, table_ref, mine_ref, rest_ref, raw):
    count = near_ref.shape[0]
    listed = near_ref.shape[1] - 2
    rows = image_near.shape[1]
    half = listed // 2
    share = count // 2
    my_cls, my_dom = place_ref[0], place_ref[1]
    core = lax.rem(my_cls, 2)
    raw[...] = jnp.zeros_like(raw)
    lane = lax.broadcasted_iota(jnp.int32, (META_ROWS, LANES), 1)
    for far in range(2):
        record, image_ref = (far_ref, image_far) if far else (near_ref, image_near)
        source_core = 1 - core if far else core
        source = my_cls - core + source_core
        cand = [[record[u, k] for k in range(listed)] for u in range(count)]
        owner = [[lax.div(c, local) for c in row] for row in cand]
        pair = []
        for u in range(count):
            first = owner[u][0]
            second = first
            for k in range(1, listed):
                second = jnp.where(owner[u][k] != first, owner[u][k], second)
            pair.append((first, second))
        for u in range(count):
            entries = [my_dom, pair[u][0], pair[u][1]]
            for side in range(2):
                value = source * (count // 2)
                for v in range(u):
                    lists = (pair[v][0] == pair[u][side]) | (pair[v][1] == pair[u][side])
                    value = value + jnp.where(lists, 1, 0)
                entries.append(value)
            for side in range(2):
                classes = [jnp.int32(0)] * half
                seen = jnp.int32(0)
                for k in range(listed):
                    hit = owner[u][k] == pair[u][side]
                    for j in range(half):
                        classes[j] = jnp.where(hit & (seen == j), cand[u][k] - pair[u][side] * local, classes[j])
                    seen = seen + jnp.where(hit, 1, 0)
                entries += classes
            tile = jnp.zeros((META_ROWS, LANES), jnp.int32)
            for k, value in enumerate(entries):
                tile = jnp.where(lane == k, value, tile)
            values = image_ref[u].astype(jnp.float32)
            for block in range(rows // PIECES):
                at = rows - (block + 1) * PIECES
                raw[at : at + PIECES, :] = values[block * PIECES : (block + 1) * PIECES]
            moved = []
            for step in range(STEP_ANGLES):
                re = raw[pl.ds(2 * step, SPAN, stride=PIECES), :]
                im = raw[pl.ds(2 * step + 1, SPAN, stride=PIECES), :]
                cx, sx = axis_phase(table_ref, 0, step, record[u, listed])
                cy, sy = axis_phase(table_ref, 1, step, record[u, listed + 1])
                cosine = cx * cy - sx * sy
                sine = sx * cy + cx * sy
                moved += [re * cosine + im * sine, im * cosine - re * sine]
            moved = jnp.concatenate(moved, axis=0).astype(mine_ref.dtype)
            tile = tile.astype(jnp.float32).astype(mine_ref.dtype)
            at = source_core * share + u % share
            role = u // share

            @pl.when(core == role)
            def _():
                mine_ref[at, :IMAGE_ROWS, :] = moved
                mine_ref[at, IMAGE_ROWS:, :] = tile

            @pl.when(core != role)
            def _():
                rest_ref[at, :IMAGE_ROWS, :] = moved
                rest_ref[at, IMAGE_ROWS:, :] = tile


SMEM_SPEC = pl.BlockSpec(memory_space=pltpu.SMEM)
VMEM_SPEC = pl.BlockSpec(memory_space=pltpu.VMEM)
HBM_SPEC = pl.BlockSpec(memory_space=pl.ANY)


def prepare(place, near, far, image_near, image_far, tables, local):
    count = near.shape[0]
    shape = jax.ShapeDtypeStruct((count, IMAGE_ROWS + META_ROWS, LANES), image_near.dtype)
    return pl.pallas_call(
        functools.partial(prep_kernel, local),
        out_shape=(shape, shape),
        in_specs=[SMEM_SPEC] * 3 + [VMEM_SPEC] * 3,
        out_specs=(VMEM_SPEC, VMEM_SPEC),
        scratch_shapes=[pltpu.VMEM((IMAGE_ROWS, LANES), jnp.float32)],
        compiler_params=pltpu.CompilerParams(vmem_limit_bytes=VMEM_LIMIT),
        name="prepare",
    )(place, near, far, image_near, image_far, tables)


def read_meta(source, meta_vmem, row):
    meta_vmem[pl.ds(row, 1), :] = source.astype(jnp.float32)[0:1, :].astype(jnp.int32)


def move_metas(meta_vmem, meta, sem):
    copy = pltpu.make_async_copy(meta_vmem, meta, sem)
    copy.start()
    copy.wait()


def side_of(meta, i, my_cls):
    return jnp.where(meta[i, OWNER] == my_cls, 0, 1)


def collect(meta, active, total, my_cls, my_dom=None):
    def look(i, n):
        mine = (meta[i, OWNER] == my_cls) | (meta[i, OWNER + 1] == my_cls)
        if my_dom is not None:
            mine = mine & (meta[i, DOM] == my_dom)
        active[n] = i
        return n + jnp.where(mine, 1, 0)

    return lax.fori_loop(0, total, look, jnp.int32(0), unroll=4)


def step_pieces(values, table_ref, step):
    re = values[2 * step * SPAN : (2 * step + 1) * SPAN]
    im = values[(2 * step + 1) * SPAN : (2 * step + 2) * SPAN]
    at = pl.ds(step * SPAN, SPAN)
    return re, im, [table_ref[k, at, :] for k in range(4)]


def store_moved(moved, step, part, blocks):
    at = pl.ds((2 * step + part) * LANES, LANES)
    pad = jnp.zeros((8, LANES), jnp.float32)
    moved[:LANES, at] = jnp.concatenate([*blocks[:3], pad], axis=0).astype(jnp.bfloat16)
    moved[LANES : LANES + 2 * SPAN, at] = jnp.concatenate(blocks[3:], axis=0).astype(jnp.bfloat16)


def score_kernel(count, place_ref, *refs):
    image_refs = refs[:count]
    (
        refs_ref, table_ref, weight_ref, stat_ref, partner_ref,
        images, moved_a, moved_b, picked_a, picked_b, sums_a, sums_b, meta_vmem, meta, active, image_sem, sem,
    ) = refs[count:]
    total = images.shape[0]
    slots = weight_ref.shape[0]
    classes = picked_a.shape[0] // 48
    my_cls, my_dom = place_ref[0], place_ref[1]
    copies, at = [], 0
    for b, ref in enumerate(image_refs):
        copies.append(pltpu.make_async_copy(ref, images.at[pl.ds(at, ref.shape[0])], image_sem.at[b]))
        at += ref.shape[0]
    for copy in copies:
        copy.start()
    for ref in (moved_a, moved_b, picked_a, picked_b, sums_a, sums_b, weight_ref, stat_ref):
        ref[...] = jnp.zeros_like(ref)
    for slot in range(slots):
        for k in range(3):
            partner_ref[slot, k] = 0
    for copy in copies:
        copy.wait()
    for i in range(total):
        read_meta(images[i, IMAGE_ROWS:, :], meta_vmem, i)
    move_metas(meta_vmem, meta, sem)
    number = collect(meta, active, total, my_cls, my_dom)
    lane = lax.broadcasted_iota(jnp.int32, (SPAN, LANES), 1)

    def one(at, moved, picked, sums):
        index = active[jnp.minimum(at, number - 1)]
        side = side_of(meta, index, my_cls)
        slot = meta[index, SLOT + side]
        partner_ref[slot, FILLED] = 1
        partner_ref[slot, OTHER] = meta[index, OWNER + 1 - side]
        partner_ref[slot, OTHER_SLOT] = meta[index, SLOT + 1 - side]
        for j in range(classes):
            picked[j * 48 : j * 48 + ROT, :] = refs_ref[meta[index, CLASS + side * classes + j]]
        values = images[index, :IMAGE_ROWS, :].astype(jnp.float32)
        for step in range(STEP_ANGLES):
            re, im, (c1, s1, c2, s2) = step_pieces(values, table_ref, step)
            a1, b1, d1, e1 = re * c1, im * s1, im * c1, re * s1
            a2, b2, d2, e2 = re * c2, im * s2, im * c2, re * s2
            store_moved(moved, step, 0, [re, a1 + b1, a1 - b1, a2 + b2, a2 - b2])
            store_moved(moved, step, 1, [im, d1 - e1, d1 + e1, d2 - e2, d2 + e2])
        pairs = lax.dot_general(
            picked[...], moved[...], (((1,), (1,)), ((), ())), preferred_element_type=jnp.float32
        )
        for s in range(SHIFTS):
            half, k = divmod(s, 3)
            for j in range(classes):
                part = pairs[j * 48 : j * 48 + SPAN, half * LANES : (half + 1) * LANES]
                part = jnp.where((lane >= k * SPAN) & (lane < (k + 1) * SPAN), part, 0.0)
                turned = pltpu.roll(part, 0, 1, stride=1, stride_axis=0)
                sums[k, pl.ds(half * classes + j, 1), :] = jnp.sum(turned, axis=0, keepdims=True)
        found = []
        for k in range(3):
            plain = pltpu.roll(sums[k], (LANES - k * SPAN) % LANES, 1) if k else sums[k]
            found.append(SOFTMAX_WARMTH * (plain + pltpu.roll(plain, LANES - ROT, 1)))
        lanes = lax.broadcasted_iota(jnp.int32, found[0].shape, 1)
        lines = lax.broadcasted_iota(jnp.int32, found[0].shape, 0)
        valid = [lanes < ROT, lanes < ROT, (lanes < ROT) & (lines < classes)]
        found = [jnp.where(v, f, NEGATIVE) for v, f in zip(valid, found)]
        peak = jnp.maximum(jnp.maximum(found[0], found[1]), found[2])
        peak = jnp.max(jnp.max(peak, axis=0, keepdims=True), axis=1, keepdims=True)
        w = [jnp.where(v, jnp.exp(f - peak), 0.0) for v, f in zip(valid, found)]
        total = w[0] + w[1] + w[2]
        total = jnp.sum(jnp.sum(total, axis=0, keepdims=True), axis=1, keepdims=True)
        stat_ref[pl.ds(2 * slot, 1), :] = jnp.broadcast_to(peak, (1, LANES))
        stat_ref[pl.ds(2 * slot + 1, 1), :] = jnp.broadcast_to(total, (1, LANES))
        upper = lines < classes
        first = jnp.where(upper, w[0], w[0] + w[1])
        second = jnp.where(upper, w[1] + w[2], w[0] - w[1])
        third = w[1] - w[2]
        third = jnp.where(upper, third, 0.0)
        weight_ref[slot] = first + pltpu.roll(second, SPAN, 1) + pltpu.roll(third, 2 * SPAN, 1)

    def two(step, carry):
        one(2 * step, moved_a, picked_a, sums_a)
        one(2 * step + 1, moved_b, picked_b, sums_b)
        return carry

    lax.fori_loop(0, lax.div(number + 1, 2), two, 0)


def score(place, buffers, refs, tables, slots, classes):
    count, total = len(buffers), sum(buffer.shape[0] for buffer in buffers)
    width = refs.shape[2]
    return pl.pallas_call(
        functools.partial(score_kernel, count),
        out_shape=(
            jax.ShapeDtypeStruct((slots, 2 * classes, LANES), jnp.float32),
            jax.ShapeDtypeStruct((2 * slots, LANES), jnp.float32),
            jax.ShapeDtypeStruct((slots, 3), jnp.int32),
        ),
        in_specs=[SMEM_SPEC] + [HBM_SPEC] * count + [VMEM_SPEC] * 2,
        out_specs=(VMEM_SPEC, VMEM_SPEC, SMEM_SPEC),
        scratch_shapes=[
            pltpu.VMEM((total, IMAGE_ROWS + META_ROWS, LANES), jnp.bfloat16),
            *[pltpu.VMEM((2 * LANES, width), jnp.bfloat16)] * 2,
            *[pltpu.VMEM((48 * classes, width), jnp.bfloat16)] * 2,
            *[pltpu.VMEM((3, 2 * classes, LANES), jnp.float32)] * 2,
            pltpu.VMEM((total, LANES), jnp.int32),
            pltpu.SMEM((total, LANES), jnp.int32),
            pltpu.SMEM((total + 1,), jnp.int32),
            pltpu.SemaphoreType.DMA((count,)),
            pltpu.SemaphoreType.DMA,
        ],
        compiler_params=pltpu.CompilerParams(vmem_limit_bytes=VMEM_LIMIT),
        cost_estimate=pl.CostEstimate(flops=10**10, bytes_accessed=10**7, transcendentals=0),
        name="score",
    )(place, *buffers, refs, tables)


def weight_kernel(flip, place_ref, partner_ref, weight_ref, *refs):
    stat_refs, out_ref = refs[:-1], refs[-1]
    slots, lines, _ = weight_ref.shape
    my_cls = place_ref[0]
    done = []
    for slot in range(slots):
        other, other_slot = partner_ref[slot, OTHER], partner_ref[slot, OTHER_SLOT]
        at = pl.ds(2 * other_slot, 2)
        if flip:
            mine = stat_refs[0][2 * slot : 2 * slot + 2, :]
            theirs = mine
            for k in range(1, len(stat_refs)):
                theirs = jnp.where(jnp.bitwise_xor(other, my_cls) == k, stat_refs[k][at, :], theirs)
        else:
            mine = stat_refs[0][my_cls, 2 * slot : 2 * slot + 2, :]
            theirs = stat_refs[0][other, at, :]
        peak = jnp.maximum(mine[0:1], theirs[0:1])
        gain = jnp.exp(mine[0:1] - peak)
        mass = mine[1:2] * gain + theirs[1:2] * jnp.exp(theirs[0:1] - peak)
        factor = gain / jnp.where(partner_ref[slot, FILLED] > 0, mass, 1.0)
        done.append(weight_ref[slot] * factor)
    out_ref[...] = jnp.concatenate(done, axis=0).astype(out_ref.dtype)


def normalise(flip, place, partners, weights, stats):
    slots, lines, _ = weights.shape
    return pl.pallas_call(
        functools.partial(weight_kernel, flip),
        out_shape=jax.ShapeDtypeStruct((slots * lines, LANES), jnp.bfloat16),
        in_specs=[SMEM_SPEC] * 2 + [VMEM_SPEC] * (1 + len(stats)),
        out_specs=VMEM_SPEC,
        name="normalise",
    )(place, partners, weights, *stats)


def sum_kernel(weight_rows, relative, z_size, y_size, lines, local, width, count, n_weights, first, last, place_ref, *refs):
    refs = list(refs)
    image_refs = [refs.pop(0) for _ in range(count)]
    weight_refs = [refs.pop(0) for _ in range(n_weights)]
    table_ref = refs.pop(0)
    given = None if first else [refs.pop(0), refs.pop(0)]
    out_ref = refs.pop(0) if last else None
    if not last:
        totals, mass = refs.pop(0), refs.pop(0)
    images, weights, moved_a, moved_b, spread_a, spread_b, meta_vmem, meta, active, image_sem, meta_sem = refs[:11]
    if last:
        totals, mass = refs[11:13]
    given_sem = refs[-1]
    depth, wave = images.shape[0], images.shape[1]
    per_row = weight_rows
    chunk = weight_refs[0].shape[0]
    classes = lines // 2
    waves = sum(ref.shape[0] for ref in image_refs) // wave

    def copies(w):
        out, at = [], 0
        for b, ref in enumerate(image_refs):
            size = ref.shape[0]
            low, high = max(at, w * wave), min(at + size, (w + 1) * wave)
            if low < high:
                source = ref.at[pl.ds(low - at, high - low)]
                target = images.at[w % depth, pl.ds(low - w * wave, high - low)]
                out.append(pltpu.make_async_copy(source, target, image_sem.at[w % depth, b]))
            at += size
        return out

    for w in range(min(depth, waves)):
        for copy in copies(w):
            copy.start()
    if first:
        mass[...] = jnp.zeros_like(mass)
        totals[...] = jnp.zeros_like(totals)
    else:
        held = [pltpu.make_async_copy(g, t, given_sem.at[k]) for k, (g, t) in enumerate(zip(given, (totals, mass)))]
        for copy in held:
            copy.start()
    moved_a[...] = jnp.zeros_like(moved_a)
    moved_b[...] = jnp.zeros_like(moved_b)
    for b in range(n_weights):
        weights[b * chunk : (b + 1) * chunk, :] = weight_refs[b][...].astype(jnp.float32)
    my_cls, my_dom = place_ref[0], place_ref[1]
    my_z, my_y = lax.div(my_dom, y_size), lax.rem(my_dom, y_size)
    lane = lax.broadcasted_iota(jnp.int32, (lines, LANES), 1)
    lane_wide = lax.broadcasted_iota(jnp.int32, (SPAN, LANES), 1)

    for w in range(waves):
        for copy in copies(w):
            copy.wait()
        here = images.at[w % depth]
        for i in range(wave):
            read_meta(here[i, IMAGE_ROWS:, :], meta_vmem, i)
        move_metas(meta_vmem, meta, meta_sem)
        number = collect(meta, active, wave, my_cls)
        if w == 0 and not first:
            for copy in held:
                copy.wait()

        def prepare_one(at, moved, spread):
            i = active[jnp.minimum(at, number - 1)]
            share = jnp.where(at < number, 1.0, 0.0).astype(jnp.float32)
            side = side_of(meta, i, my_cls)
            q = meta[i, DOM]
            if relative:
                d_z = lax.rem(my_z - lax.div(q, y_size) + z_size, z_size)
                d_y = lax.rem(my_y - lax.rem(q, y_size) + y_size, y_size)
                q = d_y * z_size + d_z
            at = pl.multiple_of(q * per_row + meta[i, SLOT + side] * lines, lines)
            mine = weights[pl.ds(at, lines), :] * share
            values = here[i, :IMAGE_ROWS, :].astype(jnp.float32)
            for step in range(STEP_ANGLES):
                re, im, (c1, s1, c2, s2) = step_pieces(values, table_ref, step)
                store_moved(moved, step, 0, [re, re * c1, im * s1, re * c2, im * s2])
                store_moved(moved, step, 1, [im, im * c1, -re * s1, im * c2, -re * s2])
            parts = []
            for k in range(3):
                part = jnp.where((lane >= k * SPAN) & (lane < (k + 1) * SPAN), mine, 0.0)
                parts.append(part + pltpu.roll(part, LANES - ROT, 1))
            blocks = []
            for j in range(classes):
                line = []
                for half in range(2):
                    at = half * classes + j
                    turned = [
                        pltpu.roll(
                            jnp.broadcast_to(parts[k][at : at + 1], (SPAN, LANES)), 1, 1, stride=1, stride_axis=0
                        )
                        for k in range(3 - half)
                    ]
                    tile = jnp.where(lane_wide < SPAN, turned[0], turned[1])
                    if half == 0:
                        tile = jnp.where(lane_wide < 2 * SPAN, tile, turned[2])
                    line.append(tile)
                blocks.append(jnp.concatenate(line, axis=1))
            spread[...] = jnp.concatenate(blocks, axis=0).astype(jnp.bfloat16)
            plain = jnp.where(lane < 2 * SPAN, mine, 0.0)
            plain_high = jnp.where(lane < SPAN, mine, 0.0)
            for j in range(classes):
                c = meta[i, CLASS + side * classes + j]
                mass[pl.ds(c, 1), :] += plain[j : j + 1] + plain_high[classes + j : classes + j + 1]

        def add_one(at, added):
            i = active[jnp.minimum(at, number - 1)]
            side = side_of(meta, i, my_cls)
            for j in range(classes):
                c = meta[i, CLASS + side * classes + j]
                for tile in range(width // LANES):
                    to = pl.ds(pl.multiple_of(tile * local * SPAN + c * SPAN, 8), SPAN)
                    totals[to, :] += added[j * SPAN : (j + 1) * SPAN, tile * LANES : (tile + 1) * LANES]

        def two(step, carry):
            at = 2 * step
            added = jnp.dot(spread_a[...], moved_a[...], preferred_element_type=jnp.float32)
            prepare_one(at + 1, moved_b, spread_b)
            add_one(at, added)
            added = jnp.dot(spread_b[...], moved_b[...], preferred_element_type=jnp.float32)
            prepare_one(at + 2, moved_a, spread_a)
            add_one(at + 1, added)
            return carry

        @pl.when(number > 0)
        def _():
            prepare_one(0, moved_a, spread_a)

        lax.fori_loop(0, lax.div(number + 1, 2), two, 0)
        if w + depth < waves:
            for copy in copies(w + depth):
                copy.start()

    if not last:
        return
    scale = 1.0 / (jnp.sum(mass[:local, :], axis=1, keepdims=True) + PRIOR_MASS)
    for turn in range(ROT):
        for tile in range(width // LANES):
            line = totals[pl.ds(tile * local * SPAN + ROT - 1 - turn, local, stride=SPAN), :]
            out_ref[:, pl.ds(turn * width + tile * LANES, LANES)] = (line * scale).astype(out_ref.dtype)


def class_sum(place, buffers, weights, tables, given, last, relative, z_size, y_size, local, width, lines, weight_rows):
    count = len(buffers)
    total = sum(buffer.shape[0] for buffer in buffers)
    wave = total if total <= 128 else math.gcd(total, 128)
    depth = min(2, total // wave)
    totals = (width // LANES * local * SPAN, LANES)
    mass = (-(-local // 8) * 8, LANES)
    first = given is None
    out = jax.ShapeDtypeStruct((local, ROT * width), jnp.bfloat16)
    held = tuple(jax.ShapeDtypeStruct(shape, jnp.float32) for shape in (totals, mass))
    scratch = [
        pltpu.VMEM((depth, wave, IMAGE_ROWS + META_ROWS, LANES), jnp.bfloat16),
        pltpu.VMEM((len(weights) * weights[0].shape[0], LANES), jnp.float32),
        pltpu.VMEM((2 * LANES, width), jnp.bfloat16),
        pltpu.VMEM((2 * LANES, width), jnp.bfloat16),
        pltpu.VMEM((lines // 2 * SPAN, 2 * LANES), jnp.bfloat16),
        pltpu.VMEM((lines // 2 * SPAN, 2 * LANES), jnp.bfloat16),
        pltpu.VMEM((wave, LANES), jnp.int32),
        pltpu.SMEM((wave, LANES), jnp.int32),
        pltpu.SMEM((wave + 1,), jnp.int32),
        pltpu.SemaphoreType.DMA((depth, count)),
        pltpu.SemaphoreType.DMA,
    ]
    if last:
        scratch += [pltpu.VMEM(totals, jnp.float32), pltpu.VMEM(mass, jnp.float32)]
    scratch += [pltpu.SemaphoreType.DMA((2,))]
    return pl.pallas_call(
        functools.partial(
            sum_kernel, weight_rows, relative, z_size, y_size, lines, local, width, count, len(weights), first, last
        ),
        out_shape=out if last else held,
        in_specs=[SMEM_SPEC]
        + [HBM_SPEC] * count
        + [VMEM_SPEC] * (len(weights) + 1)
        + ([] if first else [HBM_SPEC] * 2),
        out_specs=VMEM_SPEC if last else (VMEM_SPEC, VMEM_SPEC),
        scratch_shapes=scratch,
        compiler_params=pltpu.CompilerParams(vmem_limit_bytes=VMEM_LIMIT),
        cost_estimate=pl.CostEstimate(flops=total * 2 * 10**8, bytes_accessed=10**7, transcendentals=0),
        name="class_sum",
    )(place, *buffers, *weights, tables, *([] if first else given))


def shards(x_size, y_size, z_size, particles, references, candidates, offsets):
    groups = lax.axis_size("cls")
    doms = lax.axis_size("dom")
    count, width = particles.shape
    local = references.shape[0]
    classes = candidates.shape[1] // 2
    block_width = width // ROT
    slots = groups * (count // 2)
    tables = trig_tables()
    place = jnp.stack([lax.axis_index("cls"), lax.axis_index("dom")]).astype(jnp.int32)

    def moves(goal):
        out = []
        for cls in range(groups):
            for dom in range(doms):
                x, core, z, y = goal(cls // 2, cls % 2, dom // y_size, dom % y_size)
                to = ((x % x_size) * 2 + core) * doms + (z % z_size) * y_size + y % y_size
                out.append((cls * doms + dom, to))
        return out

    def send(value, goal):
        return lax.ppermute(value, ("cls", "dom"), moves(goal))

    swap = functools.partial(send, goal=lambda x, c, z, y: (x, 1 - c, z, y))
    along_z = functools.partial(send, goal=lambda x, c, z, y: (x, c, z + 1, y))
    back_z = functools.partial(send, goal=lambda x, c, z, y: (x, c, z - 1, y))
    early = functools.partial(send, goal=lambda x, c, z, y: (x + 1 - c, c, z, y + c))
    late = functools.partial(send, goal=lambda x, c, z, y: (x + c, c, z, y + 1 - c))

    images = particles.reshape(count, width // LANES, LANES)
    record = jnp.concatenate([candidates, offsets], axis=1)
    mine, rest = prepare(place, record, swap(record), images, swap(images), jnp.asarray(tables), local)
    refs = lax.optimization_barrier((references, mine))[0].reshape(local, ROT, block_width)
    steps = jnp.asarray(tables[:, 1])
    tuned = x_size == 2 and y_size == 2 and z_size == 4
    if tuned:
        e0, l0, z1, z3 = early(mine), late(mine), along_z(mine), back_z(mine)
        e0, l0, z1, z3, refs = lax.optimization_barrier((e0, l0, z1, z3, refs))
        near = jnp.concatenate([e0, l0])
        row = [mine, rest, near, swap(near)]
        e1, l1, z2, f0 = early(z1), late(z1), along_z(z1), late(e0)
        weights, stats, partners = score(place, row, refs, steps, slots, classes)
        stats = [
            stats,
            swap(stats),
            send(stats, lambda x, c, z, y: (x + 1, c, z, y)),
            send(stats, lambda x, c, z, y: (x + 1, 1 - c, z, y)),
        ]
        z2, z3, e1, l1, f0, *_ = lax.optimization_barrier((z2, z3, e1, l1, f0, *stats))
        z23 = jnp.concatenate([z2, z3])
        f1, e23 = late(e1), early(z23)
        weights = normalise(tuned, place, partners, weights, stats)
        weights = [weights] + [send(weights, lambda x, c, z, y, dz=dz: (x, c, z + dz, y)) for dz in range(1, z_size)]
        weights = jnp.concatenate(weights)
        weights = [weights, send(weights, lambda x, c, z, y: (x, c, z, y + 1))]
        z23, e23, f1, *weights = lax.optimization_barrier((z23, e23, f1, *weights))
        l23, f23 = late(z23), late(e23)
        first = jnp.concatenate([z1, z23, e1, l1, f0])
        second = jnp.concatenate([f1, e23])
        parts = [[*row, first, second], [swap(first), swap(second), l23, f23]]
    else:
        row = lax.all_gather(mine, "cls", axis=0, tiled=True)
        parts = [[lax.all_gather(row, "dom", axis=0, tiled=True)]]
        weights, stats, partners = score(place, [row], refs, steps, slots, classes)
        stats = [lax.all_gather(stats, "cls", axis=0, tiled=False)]
        weights = normalise(tuned, place, partners, weights, stats)
        weights = [lax.all_gather(weights, "dom", axis=0, tiled=True)]
    held = None
    for k, part in enumerate(parts):
        if k:
            *end, _ = lax.optimization_barrier((*part[2:], held[1]))
            part = part[:2] + end + [swap(block) for block in end]
        held = class_sum(
            place, part, weights, steps, held, k == len(parts) - 1, tuned, z_size, y_size, local, block_width, 2 * classes, slots * 2 * classes
        )
    return held


def solution(mesh):
    coords = [device.coords for device in mesh.devices.flat]
    sizes = [len({c[axis] for c in coords}) for axis in range(3)]
    in_specs = (
        P(("cls", "dom"), None),
        P("cls", None),
        P(("cls", "dom"), None),
        P(("cls", "dom"), None),
    )
    out_specs = P("cls", None)
    return jax.shard_map(
        functools.partial(shards, *sizes),
        mesh=mesh,
        in_specs=in_specs,
        out_specs=out_specs,
        check_vma=False,
    )
```

profile of v0, /device:TPU:0, one launch (start us, length us, event | category | flops | bytes accessed | tf_op | source)
XLA Modules:
  0.0 114.4 jit_solution(15026746872543509180)
XLA Ops:
  0.0 1.0 copy.10
  5.5 4.1 %prepare.1 = (bf16[4,336,128]{2,1,0:T(8,128)(2,1)}, bf16[4,336,128]{2,1,0:T(8,128)(2,1)}) custom-call(s32[2]{0:T(128)} %pad_add_fusion.1.place_ref, s32[4,10]{1,0:T(4,128)} %copy-done.8, s32[4,10]{1,0:T(4,128)} %copy-done.9, bf16[4,288,128]{2,1,0:T(8,128)(2,1)} %bitcast.7, bf16[4,288,128]{2,1,0:T(8,128)(2,1)} %copy-done.1, ...), custom_call_target="tpu_custom_call" | custom-call | tf_op jit(solution)/shard_map/prepare/pallas_call | solution.py:133
  9.6 4.8 %collective-permute-start.5 = (bf16[4,336,128]{2,1,0:T(8,128)(2,1)}, bf16[4,336,128]{2,1,0:T(8,128)(2,1)S(1)}, u32[]{:S(2)}, u32[]{:S(2)}) collective-permute-start(bf16[4,336,128]{2,1,0:T(8,128)(2,1)} %get-tuple-element.30.refs_0_), channel_id=1, source_target_pairs={{0,6},{1,7},{2,0},{3,1},{4,2},{5,3},{6,4},{7,5},{8,14},{9,15},{10,... | collective-permute-start | bytes 1032200 | tf_op jit(solution)/shard_map/ppermute | solution.py:538
  14.4 1.5 %collective-permute-start.3 = (bf16[4,336,128]{2,1,0:T(8,128)(2,1)}, bf16[4,336,128]{2,1,0:T(8,128)(2,1)S(1)}, u32[]{:S(2)}, u32[]{:S(2)}) collective-permute-start(bf16[4,336,128]{2,1,0:T(8,128)(2,1)} %get-tuple-element.30.refs_0_), channel_id=1, source_target_pairs={{0,1},{1,0},{2,3},{3,2},{4,5},{5,4},{6,7},{7,6},{8,24},{9,25},{10,... | collective-permute-start | bytes 1032200 | tf_op jit(solution)/shard_map/ppermute | solution.py:538
  15.9 1.5 %collective-permute-start.2 = (bf16[4,336,128]{2,1,0:T(8,128)(2,1)}, bf16[4,336,128]{2,1,0:T(8,128)(2,1)S(1)}, u32[]{:S(2)}, u32[]{:S(2)}) collective-permute-start(bf16[4,336,128]{2,1,0:T(8,128)(2,1)} %get-tuple-element.30.refs_0_), channel_id=1, source_target_pairs={{0,16},{1,17},{2,18},{3,19},{4,20},{5,21},{6,22},{7,23},{8,9},{9,8... | collective-permute-start | bytes 1032200 | tf_op jit(solution)/shard_map/ppermute | solution.py:538
  17.4 7.1 %reshape.7.refs_4_ = bf16[50,36,1024]{2,1,0:T(8,128)(2,1)} reshape(bf16[50,36864]{1,0:T(8,128)(2,1)} %param.7) | data formatting | bytes 7372800 | tf_op jit(solution)/shard_map/reshape | solution.py:549
  24.5 6.2 %collective-permute-done.4 = bf16[4,336,128]{2,1,0:T(8,128)(2,1)S(1)} collective-permute-done((bf16[4,336,128]{2,1,0:T(8,128)(2,1)}, bf16[4,336,128]{2,1,0:T(8,128)(2,1)S(1)}, u32[]{:S(2)}, u32[]{:S(2)}) %collective-permute-start.4) | collective-permute-done | bytes 344096 | tf_op jit(solution)/shard_map/ppermute | solution.py:538
  30.9 1.6 %collective-permute-start.9 = (bf16[4,336,128]{2,1,0:T(8,128)(2,1)S(1)}, bf16[4,336,128]{2,1,0:T(8,128)(2,1)S(1)}, u32[]{:S(2)}, u32[]{:S(2)}) collective-permute-start(bf16[4,336,128]{2,1,0:T(8,128)(2,1)S(1)} %collective-permute-done.2), channel_id=1, source_target_pairs={{0,1},{1,0},{2,3},{3,2},{4,5},{5,4},{6,7},{7,6},{8,24},{9,25},{10,... | collective-permute-start | bytes 1032200 | tf_op jit(solution)/shard_map/ppermute | solution.py:538
  33.0 1.5 %collective-permute-start.7 = (bf16[4,336,128]{2,1,0:T(8,128)(2,1)S(1)}, bf16[4,336,128]{2,1,0:T(8,128)(2,1)S(1)}, u32[]{:S(2)}, u32[]{:S(2)}) collective-permute-start(bf16[4,336,128]{2,1,0:T(8,128)(2,1)S(1)} %collective-permute-done.4), channel_id=1, source_target_pairs={{0,16},{1,17},{2,18},{3,19},{4,20},{5,21},{6,22},{7,23},{8,9},{9,8... | collective-permute-start | bytes 1032200 | tf_op jit(solution)/shard_map/ppermute | solution.py:538
  34.5 1.6 %collective-permute-start.6 = (bf16[4,336,128]{2,1,0:T(8,128)(2,1)S(1)}, bf16[4,336,128]{2,1,0:T(8,128)(2,1)S(1)}, u32[]{:S(2)}, u32[]{:S(2)}) collective-permute-start(bf16[4,336,128]{2,1,0:T(8,128)(2,1)S(1)} %collective-permute-done.4), channel_id=1, source_target_pairs={{0,2},{1,3},{2,4},{3,5},{4,6},{5,7},{6,0},{7,1},{8,10},{9,11},{10,... | collective-permute-start | bytes 1032200 | tf_op jit(solution)/shard_map/ppermute | solution.py:538
  36.1 0.9 copy-done.11
  37.0 9.8 %score.1 = (f32[8,8,128]{2,1,0:T(8,128)}, f32[16,128]{1,0:T(8,128)}, s32[8,3]{1,0:T(8,128)}) custom-call(s32[2]{0:T(128)} %pad_add_fusion.1.place_ref, bf16[4,336,128]{2,1,0:T(8,128)(2,1)} %get-tuple-element.30.refs_0_, bf16[4,336,128]{2,1,0:T(8,128)(2,1)} %get-tuple-element.35.refs_1_, bf16[8,336,128]{2,1,0:T(8,128)(2,1)} %copy-done.2, ...), custom_call_target="tpu_custom_call" | custom-call | flops 10000000000 | bytes 10000000 | tf_op jit(solution)/shard_map/score/pallas_call | solution.py:271
  47.8 0.9 collective-permute-start.11
  48.8 1.4 %collective-permute-done.13.refs_3_ = f32[16,128]{1,0:T(8,128)S(1)} collective-permute-done((f32[16,128]{1,0:T(8,128)}, f32[16,128]{1,0:T(8,128)S(1)}, u32[]{:S(2)}, u32[]{:S(2)}) %collective-permute-start.13) | collective-permute-done | bytes 8224 | tf_op jit(solution)/shard_map/ppermute | solution.py:538
  50.2 1.0 collective-permute-done.12.refs_2_
  51.9 1.2 %collective-permute-start.15 = (bf16[4,336,128]{2,1,0:T(8,128)(2,1)S(1)}, bf16[4,336,128]{2,1,0:T(8,128)(2,1)S(1)}, u32[]{:S(2)}, u32[]{:S(2)}) collective-permute-start(bf16[4,336,128]{2,1,0:T(8,128)(2,1)S(1)} %collective-permute-done.7), channel_id=1, source_target_pairs={{0,1},{1,0},{2,3},{3,2},{4,5},{5,4},{6,7},{7,6},{8,24},{9,25},{10,... | collective-permute-start | bytes 1032200 | tf_op jit(solution)/shard_map/ppermute | solution.py:538
  53.0 1.5 %normalise.1 = bf16[64,128]{1,0:T(8,128)(2,1)} custom-call(s32[2]{0:T(128)} %pad_add_fusion.1.place_ref, s32[8,3]{1,0:T(8,128)} %get-tuple-element.42.partner_ref, f32[8,8,128]{2,1,0:T(8,128)} %get-tuple-element.43.weight_ref, f32[16,128]{1,0:T(8,128)} %get-tuple-element.38.refs_0_, f32[16,128]{1,0:T(8,128)} %copy-done.7, f32[16,128]{1,0:T(8,128)} %copy-done.6, ...), custom_call_target="tpu_custom_call" | custom-call | tf_op jit(solution)/shard_map/normalise/pallas_call | solution.py:323
  54.6 2.2 %collective-permute-start.18 = (bf16[64,128]{1,0:T(8,128)(2,1)}, bf16[64,128]{1,0:T(8,128)(2,1)S(1)}, u32[]{:S(2)}, u32[]{:S(2)}) collective-permute-start(bf16[64,128]{1,0:T(8,128)(2,1)} %normalise.1), channel_id=1, source_target_pairs={{0,6},{1,7},{2,0},{3,1},{4,2},{5,3},{6,4},{7,5},{8,14},{9,15},{10,... | collective-permute-start | bytes 49160 | tf_op jit(solution)/shard_map/ppermute | solution.py:538
  57.4 1.2 %collective-permute-done.18 = bf16[64,128]{1,0:T(8,128)(2,1)S(1)} collective-permute-done((bf16[64,128]{1,0:T(8,128)(2,1)}, bf16[64,128]{1,0:T(8,128)(2,1)S(1)}, u32[]{:S(2)}, u32[]{:S(2)}) %collective-permute-start.18) | collective-permute-done | bytes 16416 | tf_op jit(solution)/shard_map/ppermute | solution.py:538
  58.5 3.1 %collective-permute-done.17 = bf16[64,128]{1,0:T(8,128)(2,1)S(1)} collective-permute-done((bf16[64,128]{1,0:T(8,128)(2,1)}, bf16[64,128]{1,0:T(8,128)(2,1)S(1)}, u32[]{:S(2)}, u32[]{:S(2)}) %collective-permute-start.17) | collective-permute-done | bytes 16416 | tf_op jit(solution)/shard_map/ppermute | solution.py:538
  61.6 0.9 collective-permute-done.16
  63.3 0.8 collective-permute-start.19
  64.9 2.7 %collective-permute-done.19.refs_7_ = bf16[256,128]{1,0:T(8,128)(2,1)S(1)} collective-permute-done((bf16[256,128]{1,0:T(8,128)(2,1)S(1)}, bf16[256,128]{1,0:T(8,128)(2,1)S(1)}, u32[]{:S(2)}, u32[]{:S(2)}) %collective-permute-start.19) | collective-permute-done | bytes 65568 | tf_op jit(solution)/shard_map/ppermute | solution.py:538
  67.6 0.9 constant_dynamic-update-slice_fusion.7
  70.7 0.8 collective-permute-start.22
  71.6 1.2 %collective-permute-start.23 = (bf16[8,336,128]{2,1,0:T(8,128)(2,1)S(1)}, bf16[8,336,128]{2,1,0:T(8,128)(2,1)}, u32[]{:S(2)}, u32[]{:S(2)}) collective-permute-start(bf16[8,336,128]{2,1,0:T(8,128)(2,1)S(1)} %collective-permute-done.14), channel_id=1, source_target_pairs={{0,1},{1,0},{2,3},{3,2},{4,5},{5,4},{6,7},{7,6},{8,24},{9,25},{10,... | collective-permute-start | bytes 2064392 | tf_op jit(solution)/shard_map/ppermute | solution.py:538
  73.0 0.9 copy-done.3
  73.8 16.5 %class_sum.2 = (f32[16000,128]{1,0:T(8,128)}, f32[56,128]{1,0:T(8,128)}) custom-call(s32[2]{0:T(128)} %pad_add_fusion.1.place_ref, bf16[4,336,128]{2,1,0:T(8,128)(2,1)} %get-tuple-element.30.refs_0_, bf16[4,336,128]{2,1,0:T(8,128)(2,1)} %get-tuple-element.35.refs_1_, bf16[8,336,128]{2,1,0:T(8,128)(2,1)} %copy-done.2, bf16[8,336,128]{2,1,0:T(8,128)(2,1)} %copy-done.11, ...), custom_call_target="tpu_custom_call" | custom-call | flops 12000000000 | bytes 10000000 | tf_op jit(solution)/shard_map/class_sum/pallas_call | solution.py:500
  91.0 1.8 %collective-permute-done.24.refs_4_ = bf16[8,336,128]{2,1,0:T(8,128)(2,1)S(1)} collective-permute-done((bf16[8,336,128]{2,1,0:T(8,128)(2,1)}, bf16[8,336,128]{2,1,0:T(8,128)(2,1)S(1)}, u32[]{:S(2)}, u32[]{:S(2)}) %collective-permute-start.24) | collective-permute-done | bytes 688160 | tf_op jit(solution)/shard_map/ppermute | solution.py:538
  92.8 1.0 collective-permute-done.25.refs_5_
  93.8 0.9 copy-done.13
  94.7 19.7 %class_sum.3 = bf16[50,36864]{1,0:T(8,128)(2,1)} custom-call(s32[2]{0:T(128)} %pad_add_fusion.1.place_ref, bf16[24,336,128]{2,1,0:T(8,128)(2,1)} %collective-permute-done.20.refs_0_, bf16[12,336,128]{2,1,0:T(8,128)(2,1)} %copy-done.10, bf16[8,336,128]{2,1,0:T(8,128)(2,1)} %collective-permute-done.22.refs_2_, ...), custom_call_target="tpu_custom_call" | custom-call | flops 13600000000 | bytes 10000000 | tf_op jit(solution)/shard_map/class_sum/pallas_call | solution.py:500
  (72 shorter events, 12.0 us)
Async XLA Ops:
  1.0 3.2 %copy-start = (bf16[1,4,288,128]{3,2,1,0:T(8,128)(2,1)}, bf16[1,4,288,128]{3,2,1,0:T(8,128)(2,1)S(1)}, u32[]{:S(2)}) copy-start(bf16[1,4,288,128]{3,2,1,0:T(8,128)(2,1)S(1)} %copy.10) | copy-start | bytes 884740
  1.0 3.2 %collective-permute-start.1 = (bf16[4,288,128]{2,1,0:T(8,128)(2,1)S(1)}, bf16[4,288,128]{2,1,0:T(8,128)(2,1)S(1)}, u32[]{:S(2)}, u32[]{:S(2)}) collective-permute-start(bf16[4,288,128]{2,1,0:T(8,128)(2,1)S(1)} %bitcast.6), channel_id=1, source_target_pairs={{0,8},{1,9},{2,10},{3,11},{4,12},{5,13},{6,14},{7,15},{8,0},{9,1},... | collective-permute-start | bytes 884744 | tf_op jit(solution)/shard_map/ppermute | solution.py:538
  3.1 1.2 %collective-permute-start = (s32[4,10]{1,0:T(4,128)S(1)}, s32[4,10]{1,0:T(4,128)S(1)}, u32[]{:S(2)}, u32[]{:S(2)}) collective-permute-start(s32[4,10]{1,0:T(4,128)S(1)} %pad_add_fusion.near_ref), channel_id=1, source_target_pairs={{0,8},{1,9},{2,10},{3,11},{4,12},{5,13},{6,14},{7,15},{8,0},{9,1},... | collective-permute-start | bytes 488 | tf_op jit(solution)/shard_map/ppermute | solution.py:538
  9.6 14.9 %collective-permute-start.5 = (bf16[4,336,128]{2,1,0:T(8,128)(2,1)}, bf16[4,336,128]{2,1,0:T(8,128)(2,1)S(1)}, u32[]{:S(2)}, u32[]{:S(2)}) collective-permute-start(bf16[4,336,128]{2,1,0:T(8,128)(2,1)} %get-tuple-element.30.refs_0_), channel_id=1, source_target_pairs={{0,6},{1,7},{2,0},{3,1},{4,2},{5,3},{6,4},{7,5},{8,14},{9,15},{10,... | collective-permute-start | bytes 1032200 | tf_op jit(solution)/shard_map/ppermute | solution.py:538
  14.4 16.3 %collective-permute-start.4 = (bf16[4,336,128]{2,1,0:T(8,128)(2,1)}, bf16[4,336,128]{2,1,0:T(8,128)(2,1)S(1)}, u32[]{:S(2)}, u32[]{:S(2)}) collective-permute-start(bf16[4,336,128]{2,1,0:T(8,128)(2,1)} %get-tuple-element.30.refs_0_), channel_id=1, source_target_pairs={{0,2},{1,3},{2,4},{3,5},{4,6},{5,7},{6,0},{7,1},{8,10},{9,11},{10,... | collective-permute-start | bytes 1032200 | tf_op jit(solution)/shard_map/ppermute | solution.py:538
  14.4 16.3 %collective-permute-start.3 = (bf16[4,336,128]{2,1,0:T(8,128)(2,1)}, bf16[4,336,128]{2,1,0:T(8,128)(2,1)S(1)}, u32[]{:S(2)}, u32[]{:S(2)}) collective-permute-start(bf16[4,336,128]{2,1,0:T(8,128)(2,1)} %get-tuple-element.30.refs_0_), channel_id=1, source_target_pairs={{0,1},{1,0},{2,3},{3,2},{4,5},{5,4},{6,7},{7,6},{8,24},{9,25},{10,... | collective-permute-start | bytes 1032200 | tf_op jit(solution)/shard_map/ppermute | solution.py:538
  15.9 14.8 %collective-permute-start.2 = (bf16[4,336,128]{2,1,0:T(8,128)(2,1)}, bf16[4,336,128]{2,1,0:T(8,128)(2,1)S(1)}, u32[]{:S(2)}, u32[]{:S(2)}) collective-permute-start(bf16[4,336,128]{2,1,0:T(8,128)(2,1)} %get-tuple-element.30.refs_0_), channel_id=1, source_target_pairs={{0,16},{1,17},{2,18},{3,19},{4,20},{5,21},{6,22},{7,23},{8,9},{9,8... | collective-permute-start | bytes 1032200 | tf_op jit(solution)/shard_map/ppermute | solution.py:538
  30.8 5.3 %copy-start.2 = (bf16[8,336,128]{2,1,0:T(8,128)(2,1)}, bf16[8,336,128]{2,1,0:T(8,128)(2,1)S(1)}, u32[]{:S(2)}) copy-start(bf16[8,336,128]{2,1,0:T(8,128)(2,1)S(1)} %constant_dynamic-update-slice_fusion.refs_2_) | copy-start | bytes 2064388
  30.8 5.3 %collective-permute-start.10 = (bf16[8,336,128]{2,1,0:T(8,128)(2,1)S(1)}, bf16[8,336,128]{2,1,0:T(8,128)(2,1)S(1)}, u32[]{:S(2)}, u32[]{:S(2)}) collective-permute-start(bf16[8,336,128]{2,1,0:T(8,128)(2,1)S(1)} %constant_dynamic-update-slice_fusion.refs_2_), channel_id=1, source_target_pairs={{0,8},{1,9},{2,10},{3,11},{4,12},{5,13},{6,14},{7,15},{8,0},{9,1},... | collective-permute-start | bytes 2064392 | tf_op jit(solution)/shard_map/ppermute | solution.py:538
  30.9 16.4 %collective-permute-start.9 = (bf16[4,336,128]{2,1,0:T(8,128)(2,1)S(1)}, bf16[4,336,128]{2,1,0:T(8,128)(2,1)S(1)}, u32[]{:S(2)}, u32[]{:S(2)}) collective-permute-start(bf16[4,336,128]{2,1,0:T(8,128)(2,1)S(1)} %collective-permute-done.2), channel_id=1, source_target_pairs={{0,1},{1,0},{2,3},{3,2},{4,5},{5,4},{6,7},{7,6},{8,24},{9,25},{10,... | collective-permute-start | bytes 1032200 | tf_op jit(solution)/shard_map/ppermute | solution.py:538
  32.5 15.4 %collective-permute-start.8 = (bf16[4,336,128]{2,1,0:T(8,128)(2,1)S(1)}, bf16[4,336,128]{2,1,0:T(8,128)(2,1)S(1)}, u32[]{:S(2)}, u32[]{:S(2)}) collective-permute-start(bf16[4,336,128]{2,1,0:T(8,128)(2,1)S(1)} %collective-permute-done.4), channel_id=1, source_target_pairs={{0,1},{1,0},{2,3},{3,2},{4,5},{5,4},{6,7},{7,6},{8,24},{9,25},{10,... | collective-permute-start | bytes 1032200 | tf_op jit(solution)/shard_map/ppermute | solution.py:538
  33.0 15.8 %collective-permute-start.7 = (bf16[4,336,128]{2,1,0:T(8,128)(2,1)S(1)}, bf16[4,336,128]{2,1,0:T(8,128)(2,1)S(1)}, u32[]{:S(2)}, u32[]{:S(2)}) collective-permute-start(bf16[4,336,128]{2,1,0:T(8,128)(2,1)S(1)} %collective-permute-done.4), channel_id=1, source_target_pairs={{0,16},{1,17},{2,18},{3,19},{4,20},{5,21},{6,22},{7,23},{8,9},{9,8... | collective-permute-start | bytes 1032200 | tf_op jit(solution)/shard_map/ppermute | solution.py:538
  34.5 14.3 %collective-permute-start.6 = (bf16[4,336,128]{2,1,0:T(8,128)(2,1)S(1)}, bf16[4,336,128]{2,1,0:T(8,128)(2,1)S(1)}, u32[]{:S(2)}, u32[]{:S(2)}) collective-permute-start(bf16[4,336,128]{2,1,0:T(8,128)(2,1)S(1)} %collective-permute-done.4), channel_id=1, source_target_pairs={{0,2},{1,3},{2,4},{3,5},{4,6},{5,7},{6,0},{7,1},{8,10},{9,11},{10,... | collective-permute-start | bytes 1032200 | tf_op jit(solution)/shard_map/ppermute | solution.py:538
  46.8 3.4 %collective-permute-start.13 = (f32[16,128]{1,0:T(8,128)}, f32[16,128]{1,0:T(8,128)S(1)}, u32[]{:S(2)}, u32[]{:S(2)}) collective-permute-start(f32[16,128]{1,0:T(8,128)} %get-tuple-element.38.refs_0_), channel_id=1, source_target_pairs={{0,24},{1,25},{2,26},{3,27},{4,28},{5,29},{6,30},{7,31},{8,16},{9,... | collective-permute-start | bytes 24584 | tf_op jit(solution)/shard_map/ppermute | solution.py:538
  47.3 3.9 %collective-permute-start.12 = (f32[16,128]{1,0:T(8,128)}, f32[16,128]{1,0:T(8,128)S(1)}, u32[]{:S(2)}, u32[]{:S(2)}) collective-permute-start(f32[16,128]{1,0:T(8,128)} %get-tuple-element.38.refs_0_), channel_id=1, source_target_pairs={{0,16},{1,17},{2,18},{3,19},{4,20},{5,21},{6,22},{7,23},{8,24},{9,... | collective-permute-start | bytes 24584 | tf_op jit(solution)/shard_map/ppermute | solution.py:538
  47.8 3.3 %collective-permute-start.11 = (f32[16,128]{1,0:T(8,128)}, f32[16,128]{1,0:T(8,128)S(1)}, u32[]{:S(2)}, u32[]{:S(2)}) collective-permute-start(f32[16,128]{1,0:T(8,128)} %get-tuple-element.38.refs_0_), channel_id=1, source_target_pairs={{0,8},{1,9},{2,10},{3,11},{4,12},{5,13},{6,14},{7,15},{8,0},{9,1},... | collective-permute-start | bytes 24584 | tf_op jit(solution)/shard_map/ppermute | solution.py:538
  50.2 2.9 %copy-start.5 = (f32[16,128]{1,0:T(8,128)}, f32[16,128]{1,0:T(8,128)S(1)}, u32[]{:S(2)}) copy-start(f32[16,128]{1,0:T(8,128)S(1)} %collective-permute-done.13.refs_3_) | copy-start | bytes 24580
  51.3 16.3 %collective-permute-start.14 = (bf16[8,336,128]{2,1,0:T(8,128)(2,1)S(1)}, bf16[8,336,128]{2,1,0:T(8,128)(2,1)S(1)}, u32[]{:S(2)}, u32[]{:S(2)}) collective-permute-start(bf16[8,336,128]{2,1,0:T(8,128)(2,1)S(1)} %constant_dynamic-update-slice_fusion.2), channel_id=1, source_target_pairs={{0,16},{1,17},{2,18},{3,19},{4,20},{5,21},{6,22},{7,23},{8,9},{9,8... | collective-permute-start | bytes 2064392 | tf_op jit(solution)/shard_map/ppermute | solution.py:538
  51.9 15.7 %collective-permute-start.15 = (bf16[4,336,128]{2,1,0:T(8,128)(2,1)S(1)}, bf16[4,336,128]{2,1,0:T(8,128)(2,1)S(1)}, u32[]{:S(2)}, u32[]{:S(2)}) collective-permute-start(bf16[4,336,128]{2,1,0:T(8,128)(2,1)S(1)} %collective-permute-done.7), channel_id=1, source_target_pairs={{0,1},{1,0},{2,3},{3,2},{4,5},{5,4},{6,7},{7,6},{8,24},{9,25},{10,... | collective-permute-start | bytes 1032200 | tf_op jit(solution)/shard_map/ppermute | solution.py:538
  54.6 3.9 %collective-permute-start.18 = (bf16[64,128]{1,0:T(8,128)(2,1)}, bf16[64,128]{1,0:T(8,128)(2,1)S(1)}, u32[]{:S(2)}, u32[]{:S(2)}) collective-permute-start(bf16[64,128]{1,0:T(8,128)(2,1)} %normalise.1), channel_id=1, source_target_pairs={{0,6},{1,7},{2,0},{3,1},{4,2},{5,3},{6,4},{7,5},{8,14},{9,15},{10,... | collective-permute-start | bytes 49160 | tf_op jit(solution)/shard_map/ppermute | solution.py:538
  56.8 4.8 %collective-permute-start.17 = (bf16[64,128]{1,0:T(8,128)(2,1)}, bf16[64,128]{1,0:T(8,128)(2,1)S(1)}, u32[]{:S(2)}, u32[]{:S(2)}) collective-permute-start(bf16[64,128]{1,0:T(8,128)(2,1)} %normalise.1), channel_id=1, source_target_pairs={{0,4},{1,5},{2,6},{3,7},{4,0},{5,1},{6,2},{7,3},{8,12},{9,13},{10,... | collective-permute-start | bytes 49160 | tf_op jit(solution)/shard_map/ppermute | solution.py:538
  56.8 5.7 %collective-permute-start.16 = (bf16[64,128]{1,0:T(8,128)(2,1)}, bf16[64,128]{1,0:T(8,128)(2,1)S(1)}, u32[]{:S(2)}, u32[]{:S(2)}) collective-permute-start(bf16[64,128]{1,0:T(8,128)(2,1)} %normalise.1), channel_id=1, source_target_pairs={{0,2},{1,3},{2,4},{3,5},{4,6},{5,7},{6,0},{7,1},{8,10},{9,11},{10,... | collective-permute-start | bytes 49160 | tf_op jit(solution)/shard_map/ppermute | solution.py:538
  63.3 9.5 %copy-start.4 = (bf16[256,128]{1,0:T(8,128)(2,1)}, bf16[256,128]{1,0:T(8,128)(2,1)S(1)}, u32[]{:S(2)}) copy-start(bf16[256,128]{1,0:T(8,128)(2,1)S(1)} %pad_maximum_fusion.refs_6_) | copy-start | bytes 196612
  63.3 4.3 %collective-permute-start.19 = (bf16[256,128]{1,0:T(8,128)(2,1)S(1)}, bf16[256,128]{1,0:T(8,128)(2,1)S(1)}, u32[]{:S(2)}, u32[]{:S(2)}) collective-permute-start(bf16[256,128]{1,0:T(8,128)(2,1)S(1)} %pad_maximum_fusion.refs_6_), channel_id=1, source_target_pairs={{0,1},{1,0},{2,3},{3,2},{4,5},{5,4},{6,7},{7,6},{8,9},{9,8},{10,11... | collective-permute-start | bytes 196616 | tf_op jit(solution)/shard_map/ppermute | solution.py:538
  67.5 5.3 %copy-start.14 = (bf16[256,128]{1,0:T(8,128)(2,1)}, bf16[256,128]{1,0:T(8,128)(2,1)S(1)}, u32[]{:S(2)}) copy-start(bf16[256,128]{1,0:T(8,128)(2,1)S(1)} %collective-permute-done.19.refs_7_) | copy-start | bytes 196612
  70.7 23.1 %collective-permute-start.20 = (bf16[24,336,128]{2,1,0:T(8,128)(2,1)}, bf16[24,336,128]{2,1,0:T(8,128)(2,1)}, u32[]{:S(2)}, u32[]{:S(2)}) collective-permute-start(bf16[24,336,128]{2,1,0:T(8,128)(2,1)} %constant_dynamic-update-slice_fusion.4.refs_4_), channel_id=1, source_target_pairs={{0,8},{1,9},{2,10},{3,11},{4,12},{5,13},{6,14},{7,15},{8,0},{9,1},... | collective-permute-start | bytes 6193160 | tf_op jit(solution)/shard_map/ppermute | solution.py:538
  70.7 19.7 %collective-permute-start.22 = (bf16[8,336,128]{2,1,0:T(8,128)(2,1)S(1)}, bf16[8,336,128]{2,1,0:T(8,128)(2,1)}, u32[]{:S(2)}, u32[]{:S(2)}) collective-permute-start(bf16[8,336,128]{2,1,0:T(8,128)(2,1)S(1)} %constant_dynamic-update-slice_fusion.2), channel_id=1, source_target_pairs={{0,1},{1,0},{2,3},{3,2},{4,5},{5,4},{6,7},{7,6},{8,24},{9,25},{10,... | collective-permute-start | bytes 2064392 | tf_op jit(solution)/shard_map/ppermute | solution.py:538
  71.6 18.8 %collective-permute-start.23 = (bf16[8,336,128]{2,1,0:T(8,128)(2,1)S(1)}, bf16[8,336,128]{2,1,0:T(8,128)(2,1)}, u32[]{:S(2)}, u32[]{:S(2)}) collective-permute-start(bf16[8,336,128]{2,1,0:T(8,128)(2,1)S(1)} %collective-permute-done.14), channel_id=1, source_target_pairs={{0,1},{1,0},{2,3},{3,2},{4,5},{5,4},{6,7},{7,6},{8,24},{9,25},{10,... | collective-permute-start | bytes 2064392 | tf_op jit(solution)/shard_map/ppermute | solution.py:538
  72.9 18.1 %collective-permute-start.21 = (bf16[12,336,128]{2,1,0:T(8,128)(2,1)S(1)}, bf16[12,336,128]{2,1,0:T(8,128)(2,1)S(1)}, u32[]{:S(2)}, u32[]{:S(2)}) collective-permute-start(bf16[12,336,128]{2,1,0:T(8,128)(2,1)S(1)} %constant_dynamic-update-slice_fusion.9.refs_5_), channel_id=1, source_target_pairs={{0,8},{1,9},{2,10},{3,11},{4,12},{5,13},{6,14},{7,15},{8,0},{9,1},... | collective-permute-start | bytes 3096584 | tf_op jit(solution)/shard_map/ppermute | solution.py:538
  90.4 2.4 %collective-permute-start.24 = (bf16[8,336,128]{2,1,0:T(8,128)(2,1)}, bf16[8,336,128]{2,1,0:T(8,128)(2,1)S(1)}, u32[]{:S(2)}, u32[]{:S(2)}) collective-permute-start(bf16[8,336,128]{2,1,0:T(8,128)(2,1)} %collective-permute-done.22.refs_2_), channel_id=1, source_target_pairs={{0,8},{1,9},{2,10},{3,11},{4,12},{5,13},{6,14},{7,15},{8,0},{9,1},... | collective-permute-start | bytes 2064392 | tf_op jit(solution)/shard_map/ppermute | solution.py:538
  90.5 3.3 %collective-permute-start.25 = (bf16[8,336,128]{2,1,0:T(8,128)(2,1)}, bf16[8,336,128]{2,1,0:T(8,128)(2,1)S(1)}, u32[]{:S(2)}, u32[]{:S(2)}) collective-permute-start(bf16[8,336,128]{2,1,0:T(8,128)(2,1)} %collective-permute-done.23.refs_3_), channel_id=1, source_target_pairs={{0,8},{1,9},{2,10},{3,11},{4,12},{5,13},{6,14},{7,15},{8,0},{9,1},... | collective-permute-start | bytes 2064392 | tf_op jit(solution)/shard_map/ppermute | solution.py:538
  91.0 2.8 %copy-start.10 = (bf16[12,336,128]{2,1,0:T(8,128)(2,1)}, bf16[12,336,128]{2,1,0:T(8,128)(2,1)S(1)}, u32[]{:S(2)}) copy-start(bf16[12,336,128]{2,1,0:T(8,128)(2,1)S(1)} %collective-permute-done.21.refs_1_) | copy-start | bytes 3096580
  (9 other events, 10.0 us)
where the time goes:
time: 115 us; the launch traced here: 114 us
  Pallas kernels  51.7 us (45%)
  starting transfers between devices  23.6 us (21%)
  waiting for transfers between devices  19.8 us (17%)
  local copies, waits for them, and re-layouts  17 us (15%)
  other arithmetic  2.07 us (2%)
    pallas_call x2, Pallas kernels, class_sum(): pl.pallas_call(functools.partial(sum_kernel, weight_rows, relative, z_siz...  36.2 us
    ppermute x26, starting transfers between devices, send(): return lax.ppermute(value, ('cls', 'dom'), moves(goal))  23.6 us
    ppermute x26, waiting for transfers between devices, send(): return lax.ppermute(value, ('cls', 'dom'), moves(goal))  19.8 us
    pallas_call x1, Pallas kernels, score(): pl.pallas_call(functools.partial(score_kernel, count), out_shape=(jax.Sha...  9.82 us
    unnamed x39, local copies, waits for them, and re-layouts  8.97 us
    reshape x1, local copies, waits for them, and re-layouts, shards(): lax.optimization_barrier((references, mine))[0]  7.11 us
    pallas_call x1, Pallas kernels, prepare(): pl.pallas_call(functools.partial(prep_kernel, local), out_shape=(shape, s...  4.09 us
  transfers between devices with their start and end apart: 26, of which 10 were waited for; matrix products, arithmetic and copies ran while one was open for 9% of the time, Pallas kernels for 24%

commit v1 on v0

--- a/solution.py
+++ b/solution.py
@@ -166,9 +166,9 @@
     return lax.fori_loop(0, total, look, jnp.int32(0), unroll=4)
 
 
-def step_pieces(values, table_ref, step):
-    re = values[2 * step * SPAN : (2 * step + 1) * SPAN]
-    im = values[(2 * step + 1) * SPAN : (2 * step + 2) * SPAN]
+def step_pieces(images, i, table_ref, step):
+    values = images[i, 2 * step * SPAN : (2 * step + 2) * SPAN, :].astype(jnp.float32)
+    re, im = values[:SPAN], values[SPAN:]
     at = pl.ds(step * SPAN, SPAN)
     return re, im, [table_ref[k, at, :] for k in range(4)]
 
@@ -218,20 +218,23 @@
         partner_ref[slot, OTHER_SLOT] = meta[index, SLOT + 1 - side]
         for j in range(classes):
             picked[j * 48 : j * 48 + ROT, :] = refs_ref[meta[index, CLASS + side * classes + j]]
-        values = images[index, :IMAGE_ROWS, :].astype(jnp.float32)
         for step in range(STEP_ANGLES):
-            re, im, (c1, s1, c2, s2) = step_pieces(values, table_ref, step)
+            re, im, (c1, s1, c2, s2) = step_pieces(images, index, table_ref, step)
             a1, b1, d1, e1 = re * c1, im * s1, im * c1, re * s1
             a2, b2, d2, e2 = re * c2, im * s2, im * c2, re * s2
             store_moved(moved, step, 0, [re, a1 + b1, a1 - b1, a2 + b2, a2 - b2])
             store_moved(moved, step, 1, [im, d1 - e1, d1 + e1, d2 - e2, d2 + e2])
-        pairs = lax.dot_general(
-            picked[...], moved[...], (((1,), (1,)), ((), ())), preferred_element_type=jnp.float32
-        )
         for s in range(SHIFTS):
             half, k = divmod(s, 3)
+            if k == 0:
+                pairs = lax.dot_general(
+                    picked[...],
+                    moved[half * LANES : (half + 1) * LANES, :],
+                    (((1,), (1,)), ((), ())),
+                    preferred_element_type=jnp.float32,
+                )
             for j in range(classes):
-                part = pairs[j * 48 : j * 48 + SPAN, half * LANES : (half + 1) * LANES]
+                part = pairs[j * 48 : j * 48 + SPAN]
                 part = jnp.where((lane >= k * SPAN) & (lane < (k + 1) * SPAN), part, 0.0)
                 turned = pltpu.roll(part, 0, 1, stride=1, stride_axis=0)
                 sums[k, pl.ds(half * classes + j, 1), :] = jnp.sum(turned, axis=0, keepdims=True)
@@ -402,17 +405,12 @@
                 q = d_y * z_size + d_z
             at = pl.multiple_of(q * per_row + meta[i, SLOT + side] * lines, lines)
             mine = weights[pl.ds(at, lines), :] * share
-            values = here[i, :IMAGE_ROWS, :].astype(jnp.float32)
-            for step in range(STEP_ANGLES):
-                re, im, (c1, s1, c2, s2) = step_pieces(values, table_ref, step)
-                store_moved(moved, step, 0, [re, re * c1, im * s1, re * c2, im * s2])
-                store_moved(moved, step, 1, [im, im * c1, -re * s1, im * c2, -re * s2])
             parts = []
             for k in range(3):
                 part = jnp.where((lane >= k * SPAN) & (lane < (k + 1) * SPAN), mine, 0.0)
                 parts.append(part + pltpu.roll(part, LANES - ROT, 1))
-            blocks = []
-            for j in range(classes):
+
+            def circulant(j):
                 line = []
                 for half in range(2):
                     at = half * classes + j
@@ -426,36 +424,49 @@
                     if half == 0:
                         tile = jnp.where(lane_wide < 2 * SPAN, tile, turned[2])
                     line.append(tile)
-                blocks.append(jnp.concatenate(line, axis=1))
-            spread[...] = jnp.concatenate(blocks, axis=0).astype(jnp.bfloat16)
-            plain = jnp.where(lane < 2 * SPAN, mine, 0.0)
-            plain_high = jnp.where(lane < SPAN, mine, 0.0)
-            for j in range(classes):
-                c = meta[i, CLASS + side * classes + j]
-                mass[pl.ds(c, 1), :] += plain[j : j + 1] + plain_high[classes + j : classes + j + 1]
-
-        def add_one(at, added):
+                return jnp.concatenate(line, axis=1)
+
+            def one_step(step):
+                re, im, (c1, s1, c2, s2) = step_pieces(here, i, table_ref, step)
+                store_moved(moved, step, 0, [re, re * c1, im * s1, re * c2, im * s2])
+                store_moved(moved, step, 1, [im, im * c1, -re * s1, im * c2, -re * s2])
+                for j in range(step * 2, min(step * 2 + 2, classes), 2):
+                    both = jnp.concatenate([circulant(j), circulant(j + 1)], axis=0)
+                    spread[j * SPAN : (j + 2) * SPAN, :] = both.astype(jnp.bfloat16)
+                if step == STEP_ANGLES - 1:
+                    plain = jnp.where(lane < 2 * SPAN, mine, 0.0)
+                    plain_high = jnp.where(lane < SPAN, mine, 0.0)
+                    for j in range(classes):
+                        c = meta[i, CLASS + side * classes + j]
+                        mass[pl.ds(c, 1), :] += plain[j : j + 1] + plain_high[classes + j : classes + j + 1]
+
+            return one_step
+
+        def add_one(at, moved, spread, one_step):
             i = active[jnp.minimum(at, number - 1)]
             side = side_of(meta, i, my_cls)
-            for j in range(classes):
-                c = meta[i, CLASS + side * classes + j]
-                for tile in range(width // LANES):
-                    to = pl.ds(pl.multiple_of(tile * local * SPAN + c * SPAN, 8), SPAN)
-                    totals[to, :] += added[j * SPAN : (j + 1) * SPAN, tile * LANES : (tile + 1) * LANES]
+            chosen = [meta[i, CLASS + side * classes + j] for j in range(classes)]
+            for step in range(STEP_ANGLES):
+                columns = pl.ds(2 * step * LANES, 2 * LANES)
+                added = jnp.dot(spread[...], moved[:, columns], preferred_element_type=jnp.float32)
+                one_step(step)
+                for part in range(2):
+                    for j in range(classes):
+                        start = (2 * step + part) * local * SPAN
+                        to = pl.ds(pl.multiple_of(start + chosen[j] * SPAN, 8), SPAN)
+                        totals[to, :] += added[j * SPAN : (j + 1) * SPAN, part * LANES : (part + 1) * LANES]
 
         def two(step, carry):
             at = 2 * step
-            added = jnp.dot(spread_a[...], moved_a[...], preferred_element_type=jnp.float32)
-            prepare_one(at + 1, moved_b, spread_b)
-            add_one(at, added)
-            added = jnp.dot(spread_b[...], moved_b[...], preferred_element_type=jnp.float32)
-            prepare_one(at + 2, moved_a, spread_a)
-            add_one(at + 1, added)
+            add_one(at, moved_a, spread_a, prepare_one(at + 1, moved_b, spread_b))
+            add_one(at + 1, moved_b, spread_b, prepare_one(at + 2, moved_a, spread_a))
             return carry
 
         @pl.when(number > 0)
         def _():
-            prepare_one(0, moved_a, spread_a)
+            start = prepare_one(0, moved_a, spread_a)
+            for step in range(STEP_ANGLES):
+                start(step)
 
         lax.fori_loop(0, lax.div(number + 1, 2), two, 0)
         if w + depth < waves:

time: 115 us -> 118 us (1.026)
  Pallas kernels: 51.7 us -> 54.3 us
    pallas_call x2, Pallas kernels: 36.2 us -> 39.2 us  [class_sum(): pl.pallas_call(functools.partial(sum_kernel, weight_rows, relative, z_siz...]
  transfers between devices with their start and end apart: 26 -> 26, of which waited for: 10 -> 10; matrix products, arithmetic and copies ran while one was open for 9% -> 9% of each run, Pallas kernels for 24% -> 25%
where the time goes in v1:
time: 118 us; the launch traced here: 117 us
  Pallas kernels  54.3 us (46%)
  starting transfers between devices  23.7 us (20%)
  waiting for transfers between devices  19.9 us (17%)
  local copies, waits for them, and re-layouts  17 us (14%)
  other arithmetic  2.07 us (2%)
    pallas_call x2, Pallas kernels, class_sum(): pl.pallas_call(functools.partial(sum_kernel, weight_rows, relative, z_siz...  39.2 us
    ppermute x26, starting transfers between devices, send(): return lax.ppermute(value, ('cls', 'dom'), moves(goal))  23.7 us
    ppermute x26, waiting for transfers between devices, send(): return lax.ppermute(value, ('cls', 'dom'), moves(goal))  19.9 us
    pallas_call x1, Pallas kernels, score(): pl.pallas_call(functools.partial(score_kernel, count), out_shape=(jax.Sha...  9.51 us
    unnamed x39, local copies, waits for them, and re-layouts  8.97 us
    reshape x1, local copies, waits for them, and re-layouts, shards(): lax.optimization_barrier((references, mine))[0]  7.11 us
    pallas_call x1, Pallas kernels, prepare(): pl.pallas_call(functools.partial(prep_kernel, local), out_shape=(shape, s...  4.09 us
  transfers between devices with their start and end apart: 26, of which 10 were waited for; matrix products, arithmetic and copies ran while one was open for 9% of the time, Pallas kernels for 25%

profile of v1, /device:TPU:0, one launch (start us, length us, event | category | flops | bytes accessed | tf_op | source)
XLA Modules:
  0.0 117.2 jit_solution(16167286844933672131)
XLA Ops:
  0.0 1.0 copy.10
  5.5 4.1 %prepare.1 = (bf16[4,336,128]{2,1,0:T(8,128)(2,1)}, bf16[4,336,128]{2,1,0:T(8,128)(2,1)}) custom-call(s32[2]{0:T(128)} %pad_add_fusion.1.place_ref, s32[4,10]{1,0:T(4,128)} %copy-done.8, s32[4,10]{1,0:T(4,128)} %copy-done.9, bf16[4,288,128]{2,1,0:T(8,128)(2,1)} %bitcast.7, bf16[4,288,128]{2,1,0:T(8,128)(2,1)} %copy-done.1, ...), custom_call_target="tpu_custom_call" | custom-call | tf_op jit(solution)/shard_map/prepare/pallas_call | solution.py:133
  9.6 4.8 %collective-permute-start.5 = (bf16[4,336,128]{2,1,0:T(8,128)(2,1)}, bf16[4,336,128]{2,1,0:T(8,128)(2,1)S(1)}, u32[]{:S(2)}, u32[]{:S(2)}) collective-permute-start(bf16[4,336,128]{2,1,0:T(8,128)(2,1)} %get-tuple-element.30.refs_0_), channel_id=1, source_target_pairs={{0,6},{1,7},{2,0},{3,1},{4,2},{5,3},{6,4},{7,5},{8,14},{9,15},{10,... | collective-permute-start | bytes 1032200 | tf_op jit(solution)/shard_map/ppermute | solution.py:549
  14.4 1.5 %collective-permute-start.3 = (bf16[4,336,128]{2,1,0:T(8,128)(2,1)}, bf16[4,336,128]{2,1,0:T(8,128)(2,1)S(1)}, u32[]{:S(2)}, u32[]{:S(2)}) collective-permute-start(bf16[4,336,128]{2,1,0:T(8,128)(2,1)} %get-tuple-element.30.refs_0_), channel_id=1, source_target_pairs={{0,1},{1,0},{2,3},{3,2},{4,5},{5,4},{6,7},{7,6},{8,24},{9,25},{10,... | collective-permute-start | bytes 1032200 | tf_op jit(solution)/shard_map/ppermute | solution.py:549
  15.9 1.5 %collective-permute-start.2 = (bf16[4,336,128]{2,1,0:T(8,128)(2,1)}, bf16[4,336,128]{2,1,0:T(8,128)(2,1)S(1)}, u32[]{:S(2)}, u32[]{:S(2)}) collective-permute-start(bf16[4,336,128]{2,1,0:T(8,128)(2,1)} %get-tuple-element.30.refs_0_), channel_id=1, source_target_pairs={{0,16},{1,17},{2,18},{3,19},{4,20},{5,21},{6,22},{7,23},{8,9},{9,8... | collective-permute-start | bytes 1032200 | tf_op jit(solution)/shard_map/ppermute | solution.py:549
  17.4 7.1 %reshape.7.refs_4_ = bf16[50,36,1024]{2,1,0:T(8,128)(2,1)} reshape(bf16[50,36864]{1,0:T(8,128)(2,1)} %param.7) | data formatting | bytes 7372800 | tf_op jit(solution)/shard_map/reshape | solution.py:560
  24.5 6.2 %collective-permute-done.4 = bf16[4,336,128]{2,1,0:T(8,128)(2,1)S(1)} collective-permute-done((bf16[4,336,128]{2,1,0:T(8,128)(2,1)}, bf16[4,336,128]{2,1,0:T(8,128)(2,1)S(1)}, u32[]{:S(2)}, u32[]{:S(2)}) %collective-permute-start.4) | collective-permute-done | bytes 344096 | tf_op jit(solution)/shard_map/ppermute | solution.py:549
  30.9 1.6 %collective-permute-start.9 = (bf16[4,336,128]{2,1,0:T(8,128)(2,1)S(1)}, bf16[4,336,128]{2,1,0:T(8,128)(2,1)S(1)}, u32[]{:S(2)}, u32[]{:S(2)}) collective-permute-start(bf16[4,336,128]{2,1,0:T(8,128)(2,1)S(1)} %collective-permute-done.2), channel_id=1, source_target_pairs={{0,1},{1,0},{2,3},{3,2},{4,5},{5,4},{6,7},{7,6},{8,24},{9,25},{10,... | collective-permute-start | bytes 1032200 | tf_op jit(solution)/shard_map/ppermute | solution.py:549
  33.0 1.5 %collective-permute-start.7 = (bf16[4,336,128]{2,1,0:T(8,128)(2,1)S(1)}, bf16[4,336,128]{2,1,0:T(8,128)(2,1)S(1)}, u32[]{:S(2)}, u32[]{:S(2)}) collective-permute-start(bf16[4,336,128]{2,1,0:T(8,128)(2,1)S(1)} %collective-permute-done.4), channel_id=1, source_target_pairs={{0,16},{1,17},{2,18},{3,19},{4,20},{5,21},{6,22},{7,23},{8,9},{9,8... | collective-permute-start | bytes 1032200 | tf_op jit(solution)/shard_map/ppermute | solution.py:549
  34.5 1.6 %collective-permute-start.6 = (bf16[4,336,128]{2,1,0:T(8,128)(2,1)S(1)}, bf16[4,336,128]{2,1,0:T(8,128)(2,1)S(1)}, u32[]{:S(2)}, u32[]{:S(2)}) collective-permute-start(bf16[4,336,128]{2,1,0:T(8,128)(2,1)S(1)} %collective-permute-done.4), channel_id=1, source_target_pairs={{0,2},{1,3},{2,4},{3,5},{4,6},{5,7},{6,0},{7,1},{8,10},{9,11},{10,... | collective-permute-start | bytes 1032200 | tf_op jit(solution)/shard_map/ppermute | solution.py:549
  36.1 0.9 copy-done.11
  37.0 9.5 %score.1 = (f32[8,8,128]{2,1,0:T(8,128)}, f32[16,128]{1,0:T(8,128)}, s32[8,3]{1,0:T(8,128)}) custom-call(s32[2]{0:T(128)} %pad_add_fusion.1.place_ref, bf16[4,336,128]{2,1,0:T(8,128)(2,1)} %get-tuple-element.30.refs_0_, bf16[4,336,128]{2,1,0:T(8,128)(2,1)} %get-tuple-element.35.refs_1_, bf16[8,336,128]{2,1,0:T(8,128)(2,1)} %copy-done.2, ...), custom_call_target="tpu_custom_call" | custom-call | flops 10000000000 | bytes 10000000 | tf_op jit(solution)/shard_map/score/pallas_call | solution.py:274
  47.5 0.9 collective-permute-start.11
  48.4 1.4 %collective-permute-done.13.refs_3_ = f32[16,128]{1,0:T(8,128)S(1)} collective-permute-done((f32[16,128]{1,0:T(8,128)}, f32[16,128]{1,0:T(8,128)S(1)}, u32[]{:S(2)}, u32[]{:S(2)}) %collective-permute-start.13) | collective-permute-done | bytes 8224 | tf_op jit(solution)/shard_map/ppermute | solution.py:549
  49.9 1.0 collective-permute-done.12.refs_2_
  51.6 1.2 %collective-permute-start.15 = (bf16[4,336,128]{2,1,0:T(8,128)(2,1)S(1)}, bf16[4,336,128]{2,1,0:T(8,128)(2,1)S(1)}, u32[]{:S(2)}, u32[]{:S(2)}) collective-permute-start(bf16[4,336,128]{2,1,0:T(8,128)(2,1)S(1)} %collective-permute-done.7), channel_id=1, source_target_pairs={{0,1},{1,0},{2,3},{3,2},{4,5},{5,4},{6,7},{7,6},{8,24},{9,25},{10,... | collective-permute-start | bytes 1032200 | tf_op jit(solution)/shard_map/ppermute | solution.py:549
  52.7 1.5 %normalise.1 = bf16[64,128]{1,0:T(8,128)(2,1)} custom-call(s32[2]{0:T(128)} %pad_add_fusion.1.place_ref, s32[8,3]{1,0:T(8,128)} %get-tuple-element.42.partner_ref, f32[8,8,128]{2,1,0:T(8,128)} %get-tuple-element.43.weight_ref, f32[16,128]{1,0:T(8,128)} %get-tuple-element.38.refs_0_, f32[16,128]{1,0:T(8,128)} %copy-done.7, f32[16,128]{1,0:T(8,128)} %copy-done.6, ...), custom_call_target="tpu_custom_call" | custom-call | tf_op jit(solution)/shard_map/normalise/pallas_call | solution.py:326
  54.3 2.2 %collective-permute-start.18 = (bf16[64,128]{1,0:T(8,128)(2,1)}, bf16[64,128]{1,0:T(8,128)(2,1)S(1)}, u32[]{:S(2)}, u32[]{:S(2)}) collective-permute-start(bf16[64,128]{1,0:T(8,128)(2,1)} %normalise.1), channel_id=1, source_target_pairs={{0,6},{1,7},{2,0},{3,1},{4,2},{5,3},{6,4},{7,5},{8,14},{9,15},{10,... | collective-permute-start | bytes 49160 | tf_op jit(solution)/shard_map/ppermute | solution.py:549
  57.1 1.2 %collective-permute-done.18 = bf16[64,128]{1,0:T(8,128)(2,1)S(1)} collective-permute-done((bf16[64,128]{1,0:T(8,128)(2,1)}, bf16[64,128]{1,0:T(8,128)(2,1)S(1)}, u32[]{:S(2)}, u32[]{:S(2)}) %collective-permute-start.18) | collective-permute-done | bytes 16416 | tf_op jit(solution)/shard_map/ppermute | solution.py:549
  58.2 3.1 %collective-permute-done.17 = bf16[64,128]{1,0:T(8,128)(2,1)S(1)} collective-permute-done((bf16[64,128]{1,0:T(8,128)(2,1)}, bf16[64,128]{1,0:T(8,128)(2,1)S(1)}, u32[]{:S(2)}, u32[]{:S(2)}) %collective-permute-start.17) | collective-permute-done | bytes 16416 | tf_op jit(solution)/shard_map/ppermute | solution.py:549
  61.3 0.9 collective-permute-done.16
  63.0 0.8 collective-permute-start.19
  64.6 2.7 %collective-permute-done.19.refs_7_ = bf16[256,128]{1,0:T(8,128)(2,1)S(1)} collective-permute-done((bf16[256,128]{1,0:T(8,128)(2,1)S(1)}, bf16[256,128]{1,0:T(8,128)(2,1)S(1)}, u32[]{:S(2)}, u32[]{:S(2)}) %collective-permute-start.19) | collective-permute-done | bytes 65568 | tf_op jit(solution)/shard_map/ppermute | solution.py:549
  67.3 0.9 constant_dynamic-update-slice_fusion.7
  70.4 0.8 collective-permute-start.22
  71.3 1.2 %collective-permute-start.23 = (bf16[8,336,128]{2,1,0:T(8,128)(2,1)S(1)}, bf16[8,336,128]{2,1,0:T(8,128)(2,1)}, u32[]{:S(2)}, u32[]{:S(2)}) collective-permute-start(bf16[8,336,128]{2,1,0:T(8,128)(2,1)S(1)} %collective-permute-done.14), channel_id=1, source_target_pairs={{0,1},{1,0},{2,3},{3,2},{4,5},{5,4},{6,7},{7,6},{8,24},{9,25},{10,... | collective-permute-start | bytes 2064392 | tf_op jit(solution)/shard_map/ppermute | solution.py:549
  72.7 0.9 copy-done.3
  73.5 17.7 %class_sum.2 = (f32[16000,128]{1,0:T(8,128)}, f32[56,128]{1,0:T(8,128)}) custom-call(s32[2]{0:T(128)} %pad_add_fusion.1.place_ref, bf16[4,336,128]{2,1,0:T(8,128)(2,1)} %get-tuple-element.30.refs_0_, bf16[4,336,128]{2,1,0:T(8,128)(2,1)} %get-tuple-element.35.refs_1_, bf16[8,336,128]{2,1,0:T(8,128)(2,1)} %copy-done.2, bf16[8,336,128]{2,1,0:T(8,128)(2,1)} %copy-done.11, ...), custom_call_target="tpu_custom_call" | custom-call | flops 12000000000 | bytes 10000000 | tf_op jit(solution)/shard_map/class_sum/pallas_call | solution.py:511
  92.0 1.9 %collective-permute-done.24.refs_4_ = bf16[8,336,128]{2,1,0:T(8,128)(2,1)S(1)} collective-permute-done((bf16[8,336,128]{2,1,0:T(8,128)(2,1)}, bf16[8,336,128]{2,1,0:T(8,128)(2,1)S(1)}, u32[]{:S(2)}, u32[]{:S(2)}) %collective-permute-start.24) | collective-permute-done | bytes 688160 | tf_op jit(solution)/shard_map/ppermute | solution.py:549
  93.9 1.0 collective-permute-done.25.refs_5_
  94.9 0.9 copy-done.13
  95.8 21.4 %class_sum.3 = bf16[50,36864]{1,0:T(8,128)(2,1)} custom-call(s32[2]{0:T(128)} %pad_add_fusion.1.place_ref, bf16[24,336,128]{2,1,0:T(8,128)(2,1)} %collective-permute-done.20.refs_0_, bf16[12,336,128]{2,1,0:T(8,128)(2,1)} %copy-done.10, bf16[8,336,128]{2,1,0:T(8,128)(2,1)} %collective-permute-done.22.refs_2_, ...), custom_call_target="tpu_custom_call" | custom-call | flops 13600000000 | bytes 10000000 | tf_op jit(solution)/shard_map/class_sum/pallas_call | solution.py:511
  (72 shorter events, 12.1 us)
Async XLA Ops:
  1.0 3.2 %copy-start = (bf16[1,4,288,128]{3,2,1,0:T(8,128)(2,1)}, bf16[1,4,288,128]{3,2,1,0:T(8,128)(2,1)S(1)}, u32[]{:S(2)}) copy-start(bf16[1,4,288,128]{3,2,1,0:T(8,128)(2,1)S(1)} %copy.10) | copy-start | bytes 884740
  1.0 3.2 %collective-permute-start.1 = (bf16[4,288,128]{2,1,0:T(8,128)(2,1)S(1)}, bf16[4,288,128]{2,1,0:T(8,128)(2,1)S(1)}, u32[]{:S(2)}, u32[]{:S(2)}) collective-permute-start(bf16[4,288,128]{2,1,0:T(8,128)(2,1)S(1)} %bitcast.6), channel_id=1, source_target_pairs={{0,8},{1,9},{2,10},{3,11},{4,12},{5,13},{6,14},{7,15},{8,0},{9,1},... | collective-permute-start | bytes 884744 | tf_op jit(solution)/shard_map/ppermute | solution.py:549
  3.1 1.2 collective-permute-start
  9.6 14.9 %collective-permute-start.5 = (bf16[4,336,128]{2,1,0:T(8,128)(2,1)}, bf16[4,336,128]{2,1,0:T(8,128)(2,1)S(1)}, u32[]{:S(2)}, u32[]{:S(2)}) collective-permute-start(bf16[4,336,128]{2,1,0:T(8,128)(2,1)} %get-tuple-element.30.refs_0_), channel_id=1, source_target_pairs={{0,6},{1,7},{2,0},{3,1},{4,2},{5,3},{6,4},{7,5},{8,14},{9,15},{10,... | collective-permute-start | bytes 1032200 | tf_op jit(solution)/shard_map/ppermute | solution.py:549
  14.4 16.3 %collective-permute-start.4 = (bf16[4,336,128]{2,1,0:T(8,128)(2,1)}, bf16[4,336,128]{2,1,0:T(8,128)(2,1)S(1)}, u32[]{:S(2)}, u32[]{:S(2)}) collective-permute-start(bf16[4,336,128]{2,1,0:T(8,128)(2,1)} %get-tuple-element.30.refs_0_), channel_id=1, source_target_pairs={{0,2},{1,3},{2,4},{3,5},{4,6},{5,7},{6,0},{7,1},{8,10},{9,11},{10,... | collective-permute-start | bytes 1032200 | tf_op jit(solution)/shard_map/ppermute | solution.py:549
  14.4 16.3 %collective-permute-start.3 = (bf16[4,336,128]{2,1,0:T(8,128)(2,1)}, bf16[4,336,128]{2,1,0:T(8,128)(2,1)S(1)}, u32[]{:S(2)}, u32[]{:S(2)}) collective-permute-start(bf16[4,336,128]{2,1,0:T(8,128)(2,1)} %get-tuple-element.30.refs_0_), channel_id=1, source_target_pairs={{0,1},{1,0},{2,3},{3,2},{4,5},{5,4},{6,7},{7,6},{8,24},{9,25},{10,... | collective-permute-start | bytes 1032200 | tf_op jit(solution)/shard_map/ppermute | solution.py:549
  15.9 14.8 %collective-permute-start.2 = (bf16[4,336,128]{2,1,0:T(8,128)(2,1)}, bf16[4,336,128]{2,1,0:T(8,128)(2,1)S(1)}, u32[]{:S(2)}, u32[]{:S(2)}) collective-permute-start(bf16[4,336,128]{2,1,0:T(8,128)(2,1)} %get-tuple-element.30.refs_0_), channel_id=1, source_target_pairs={{0,16},{1,17},{2,18},{3,19},{4,20},{5,21},{6,22},{7,23},{8,9},{9,8... | collective-permute-start | bytes 1032200 | tf_op jit(solution)/shard_map/ppermute | solution.py:549
  30.8 5.3 %copy-start.2 = (bf16[8,336,128]{2,1,0:T(8,128)(2,1)}, bf16[8,336,128]{2,1,0:T(8,128)(2,1)S(1)}, u32[]{:S(2)}) copy-start(bf16[8,336,128]{2,1,0:T(8,128)(2,1)S(1)} %constant_dynamic-update-slice_fusion.refs_2_) | copy-start | bytes 2064388
  30.8 5.3 %collective-permute-start.10 = (bf16[8,336,128]{2,1,0:T(8,128)(2,1)S(1)}, bf16[8,336,128]{2,1,0:T(8,128)(2,1)S(1)}, u32[]{:S(2)}, u32[]{:S(2)}) collective-permute-start(bf16[8,336,128]{2,1,0:T(8,128)(2,1)S(1)} %constant_dynamic-update-slice_fusion.refs_2_), channel_id=1, source_target_pairs={{0,8},{1,9},{2,10},{3,11},{4,12},{5,13},{6,14},{7,15},{8,0},{9,1},... | collective-permute-start | bytes 2064392 | tf_op jit(solution)/shard_map/ppermute | solution.py:549
  30.9 16.1 %collective-permute-start.9 = (bf16[4,336,128]{2,1,0:T(8,128)(2,1)S(1)}, bf16[4,336,128]{2,1,0:T(8,128)(2,1)S(1)}, u32[]{:S(2)}, u32[]{:S(2)}) collective-permute-start(bf16[4,336,128]{2,1,0:T(8,128)(2,1)S(1)} %collective-permute-done.2), channel_id=1, source_target_pairs={{0,1},{1,0},{2,3},{3,2},{4,5},{5,4},{6,7},{7,6},{8,24},{9,25},{10,... | collective-permute-start | bytes 1032200 | tf_op jit(solution)/shard_map/ppermute | solution.py:549
  32.5 15.1 %collective-permute-start.8 = (bf16[4,336,128]{2,1,0:T(8,128)(2,1)S(1)}, bf16[4,336,128]{2,1,0:T(8,128)(2,1)S(1)}, u32[]{:S(2)}, u32[]{:S(2)}) collective-permute-start(bf16[4,336,128]{2,1,0:T(8,128)(2,1)S(1)} %collective-permute-done.4), channel_id=1, source_target_pairs={{0,1},{1,0},{2,3},{3,2},{4,5},{5,4},{6,7},{7,6},{8,24},{9,25},{10,... | collective-permute-start | bytes 1032200 | tf_op jit(solution)/shard_map/ppermute | solution.py:549
  33.0 15.5 %collective-permute-start.7 = (bf16[4,336,128]{2,1,0:T(8,128)(2,1)S(1)}, bf16[4,336,128]{2,1,0:T(8,128)(2,1)S(1)}, u32[]{:S(2)}, u32[]{:S(2)}) collective-permute-start(bf16[4,336,128]{2,1,0:T(8,128)(2,1)S(1)} %collective-permute-done.4), channel_id=1, source_target_pairs={{0,16},{1,17},{2,18},{3,19},{4,20},{5,21},{6,22},{7,23},{8,9},{9,8... | collective-permute-start | bytes 1032200 | tf_op jit(solution)/shard_map/ppermute | solution.py:549
  34.5 14.0 %collective-permute-start.6 = (bf16[4,336,128]{2,1,0:T(8,128)(2,1)S(1)}, bf16[4,336,128]{2,1,0:T(8,128)(2,1)S(1)}, u32[]{:S(2)}, u32[]{:S(2)}) collective-permute-start(bf16[4,336,128]{2,1,0:T(8,128)(2,1)S(1)} %collective-permute-done.4), channel_id=1, source_target_pairs={{0,2},{1,3},{2,4},{3,5},{4,6},{5,7},{6,0},{7,1},{8,10},{9,11},{10,... | collective-permute-start | bytes 1032200 | tf_op jit(solution)/shard_map/ppermute | solution.py:549
  46.5 3.4 %collective-permute-start.13 = (f32[16,128]{1,0:T(8,128)}, f32[16,128]{1,0:T(8,128)S(1)}, u32[]{:S(2)}, u32[]{:S(2)}) collective-permute-start(f32[16,128]{1,0:T(8,128)} %get-tuple-element.38.refs_0_), channel_id=1, source_target_pairs={{0,24},{1,25},{2,26},{3,27},{4,28},{5,29},{6,30},{7,31},{8,16},{9,... | collective-permute-start | bytes 24584 | tf_op jit(solution)/shard_map/ppermute | solution.py:549
  47.0 3.9 %collective-permute-start.12 = (f32[16,128]{1,0:T(8,128)}, f32[16,128]{1,0:T(8,128)S(1)}, u32[]{:S(2)}, u32[]{:S(2)}) collective-permute-start(f32[16,128]{1,0:T(8,128)} %get-tuple-element.38.refs_0_), channel_id=1, source_target_pairs={{0,16},{1,17},{2,18},{3,19},{4,20},{5,21},{6,22},{7,23},{8,24},{9,... | collective-permute-start | bytes 24584 | tf_op jit(solution)/shard_map/ppermute | solution.py:549
  47.5 3.3 %collective-permute-start.11 = (f32[16,128]{1,0:T(8,128)}, f32[16,128]{1,0:T(8,128)S(1)}, u32[]{:S(2)}, u32[]{:S(2)}) collective-permute-start(f32[16,128]{1,0:T(8,128)} %get-tuple-element.38.refs_0_), channel_id=1, source_target_pairs={{0,8},{1,9},{2,10},{3,11},{4,12},{5,13},{6,14},{7,15},{8,0},{9,1},... | collective-permute-start | bytes 24584 | tf_op jit(solution)/shard_map/ppermute | solution.py:549
  49.8 2.9 %copy-start.5 = (f32[16,128]{1,0:T(8,128)}, f32[16,128]{1,0:T(8,128)S(1)}, u32[]{:S(2)}) copy-start(f32[16,128]{1,0:T(8,128)S(1)} %collective-permute-done.13.refs_3_) | copy-start | bytes 24580
  51.0 16.3 %collective-permute-start.14 = (bf16[8,336,128]{2,1,0:T(8,128)(2,1)S(1)}, bf16[8,336,128]{2,1,0:T(8,128)(2,1)S(1)}, u32[]{:S(2)}, u32[]{:S(2)}) collective-permute-start(bf16[8,336,128]{2,1,0:T(8,128)(2,1)S(1)} %constant_dynamic-update-slice_fusion.2), channel_id=1, source_target_pairs={{0,16},{1,17},{2,18},{3,19},{4,20},{5,21},{6,22},{7,23},{8,9},{9,8... | collective-permute-start | bytes 2064392 | tf_op jit(solution)/shard_map/ppermute | solution.py:549
  51.6 15.7 %collective-permute-start.15 = (bf16[4,336,128]{2,1,0:T(8,128)(2,1)S(1)}, bf16[4,336,128]{2,1,0:T(8,128)(2,1)S(1)}, u32[]{:S(2)}, u32[]{:S(2)}) collective-permute-start(bf16[4,336,128]{2,1,0:T(8,128)(2,1)S(1)} %collective-permute-done.7), channel_id=1, source_target_pairs={{0,1},{1,0},{2,3},{3,2},{4,5},{5,4},{6,7},{7,6},{8,24},{9,25},{10,... | collective-permute-start | bytes 1032200 | tf_op jit(solution)/shard_map/ppermute | solution.py:549
  54.3 3.9 %collective-permute-start.18 = (bf16[64,128]{1,0:T(8,128)(2,1)}, bf16[64,128]{1,0:T(8,128)(2,1)S(1)}, u32[]{:S(2)}, u32[]{:S(2)}) collective-permute-start(bf16[64,128]{1,0:T(8,128)(2,1)} %normalise.1), channel_id=1, source_target_pairs={{0,6},{1,7},{2,0},{3,1},{4,2},{5,3},{6,4},{7,5},{8,14},{9,15},{10,... | collective-permute-start | bytes 49160 | tf_op jit(solution)/shard_map/ppermute | solution.py:549
  56.5 4.8 %collective-permute-start.17 = (bf16[64,128]{1,0:T(8,128)(2,1)}, bf16[64,128]{1,0:T(8,128)(2,1)S(1)}, u32[]{:S(2)}, u32[]{:S(2)}) collective-permute-start(bf16[64,128]{1,0:T(8,128)(2,1)} %normalise.1), channel_id=1, source_target_pairs={{0,4},{1,5},{2,6},{3,7},{4,0},{5,1},{6,2},{7,3},{8,12},{9,13},{10,... | collective-permute-start | bytes 49160 | tf_op jit(solution)/shard_map/ppermute | solution.py:549
  56.5 5.7 %collective-permute-start.16 = (bf16[64,128]{1,0:T(8,128)(2,1)}, bf16[64,128]{1,0:T(8,128)(2,1)S(1)}, u32[]{:S(2)}, u32[]{:S(2)}) collective-permute-start(bf16[64,128]{1,0:T(8,128)(2,1)} %normalise.1), channel_id=1, source_target_pairs={{0,2},{1,3},{2,4},{3,5},{4,6},{5,7},{6,0},{7,1},{8,10},{9,11},{10,... | collective-permute-start | bytes 49160 | tf_op jit(solution)/shard_map/ppermute | solution.py:549
  63.0 9.5 %copy-start.4 = (bf16[256,128]{1,0:T(8,128)(2,1)}, bf16[256,128]{1,0:T(8,128)(2,1)S(1)}, u32[]{:S(2)}) copy-start(bf16[256,128]{1,0:T(8,128)(2,1)S(1)} %pad_maximum_fusion.refs_6_) | copy-start | bytes 196612
  63.0 4.3 %collective-permute-start.19 = (bf16[256,128]{1,0:T(8,128)(2,1)S(1)}, bf16[256,128]{1,0:T(8,128)(2,1)S(1)}, u32[]{:S(2)}, u32[]{:S(2)}) collective-permute-start(bf16[256,128]{1,0:T(8,128)(2,1)S(1)} %pad_maximum_fusion.refs_6_), channel_id=1, source_target_pairs={{0,1},{1,0},{2,3},{3,2},{4,5},{5,4},{6,7},{7,6},{8,9},{9,8},{10,11... | collective-permute-start | bytes 196616 | tf_op jit(solution)/shard_map/ppermute | solution.py:549
  67.2 5.3 %copy-start.14 = (bf16[256,128]{1,0:T(8,128)(2,1)}, bf16[256,128]{1,0:T(8,128)(2,1)S(1)}, u32[]{:S(2)}) copy-start(bf16[256,128]{1,0:T(8,128)(2,1)S(1)} %collective-permute-done.19.refs_7_) | copy-start | bytes 196612
  70.4 24.5 %collective-permute-start.20 = (bf16[24,336,128]{2,1,0:T(8,128)(2,1)}, bf16[24,336,128]{2,1,0:T(8,128)(2,1)}, u32[]{:S(2)}, u32[]{:S(2)}) collective-permute-start(bf16[24,336,128]{2,1,0:T(8,128)(2,1)} %constant_dynamic-update-slice_fusion.4.refs_4_), channel_id=1, source_target_pairs={{0,8},{1,9},{2,10},{3,11},{4,12},{5,13},{6,14},{7,15},{8,0},{9,1},... | collective-permute-start | bytes 6193160 | tf_op jit(solution)/shard_map/ppermute | solution.py:549
  70.4 20.9 %collective-permute-start.22 = (bf16[8,336,128]{2,1,0:T(8,128)(2,1)S(1)}, bf16[8,336,128]{2,1,0:T(8,128)(2,1)}, u32[]{:S(2)}, u32[]{:S(2)}) collective-permute-start(bf16[8,336,128]{2,1,0:T(8,128)(2,1)S(1)} %constant_dynamic-update-slice_fusion.2), channel_id=1, source_target_pairs={{0,1},{1,0},{2,3},{3,2},{4,5},{5,4},{6,7},{7,6},{8,24},{9,25},{10,... | collective-permute-start | bytes 2064392 | tf_op jit(solution)/shard_map/ppermute | solution.py:549
  71.3 20.0 %collective-permute-start.23 = (bf16[8,336,128]{2,1,0:T(8,128)(2,1)S(1)}, bf16[8,336,128]{2,1,0:T(8,128)(2,1)}, u32[]{:S(2)}, u32[]{:S(2)}) collective-permute-start(bf16[8,336,128]{2,1,0:T(8,128)(2,1)S(1)} %collective-permute-done.14), channel_id=1, source_target_pairs={{0,1},{1,0},{2,3},{3,2},{4,5},{5,4},{6,7},{7,6},{8,24},{9,25},{10,... | collective-permute-start | bytes 2064392 | tf_op jit(solution)/shard_map/ppermute | solution.py:549
  72.6 19.4 %collective-permute-start.21 = (bf16[12,336,128]{2,1,0:T(8,128)(2,1)S(1)}, bf16[12,336,128]{2,1,0:T(8,128)(2,1)S(1)}, u32[]{:S(2)}, u32[]{:S(2)}) collective-permute-start(bf16[12,336,128]{2,1,0:T(8,128)(2,1)S(1)} %constant_dynamic-update-slice_fusion.9.refs_5_), channel_id=1, source_target_pairs={{0,8},{1,9},{2,10},{3,11},{4,12},{5,13},{6,14},{7,15},{8,0},{9,1},... | collective-permute-start | bytes 3096584 | tf_op jit(solution)/shard_map/ppermute | solution.py:549
  91.3 2.6 %collective-permute-start.24 = (bf16[8,336,128]{2,1,0:T(8,128)(2,1)}, bf16[8,336,128]{2,1,0:T(8,128)(2,1)S(1)}, u32[]{:S(2)}, u32[]{:S(2)}) collective-permute-start(bf16[8,336,128]{2,1,0:T(8,128)(2,1)} %collective-permute-done.22.refs_2_), channel_id=1, source_target_pairs={{0,8},{1,9},{2,10},{3,11},{4,12},{5,13},{6,14},{7,15},{8,0},{9,1},... | collective-permute-start | bytes 2064392 | tf_op jit(solution)/shard_map/ppermute | solution.py:549
  91.9 3.0 %collective-permute-start.25 = (bf16[8,336,128]{2,1,0:T(8,128)(2,1)}, bf16[8,336,128]{2,1,0:T(8,128)(2,1)S(1)}, u32[]{:S(2)}, u32[]{:S(2)}) collective-permute-start(bf16[8,336,128]{2,1,0:T(8,128)(2,1)} %collective-permute-done.23.refs_3_), channel_id=1, source_target_pairs={{0,8},{1,9},{2,10},{3,11},{4,12},{5,13},{6,14},{7,15},{8,0},{9,1},... | collective-permute-start | bytes 2064392 | tf_op jit(solution)/shard_map/ppermute | solution.py:549
  92.0 2.9 %copy-start.10 = (bf16[12,336,128]{2,1,0:T(8,128)(2,1)}, bf16[12,336,128]{2,1,0:T(8,128)(2,1)S(1)}, u32[]{:S(2)}) copy-start(bf16[12,336,128]{2,1,0:T(8,128)(2,1)S(1)} %collective-permute-done.21.refs_1_) | copy-start | bytes 3096580
  (9 other events, 10.0 us)

commit v2 on v1

--- a/solution.py
+++ b/solution.py
@@ -151,6 +151,21 @@
     copy.wait()
 
 
+def turned_lanes(offset):
+    lane = lax.broadcasted_iota(jnp.int32, (SPAN, LANES), 1)
+    row = lax.broadcasted_iota(jnp.int32, (SPAN, LANES), 0)
+    base = jnp.where(lane >= SPAN, SPAN, 0) + jnp.where(lane >= 2 * SPAN, SPAN, 0)
+    base = jnp.where(lane >= 3 * SPAN, 0, base)
+    place = jnp.where(lane >= 3 * SPAN, 0, lane - base) - row + offset
+    place = jnp.where(place < 0, place + ROT, place)
+    place = jnp.where(place < 0, place + ROT, place)
+    return base + jnp.minimum(place, ROT - 1)
+
+
+def take_lanes(values, index):
+    return jnp.take_along_axis(values, index, axis=1, mode="promise_in_bounds")
+
+
 def side_of(meta, i, my_cls):
     return jnp.where(meta[i, OWNER] == my_cls, 0, 1)
 
@@ -184,7 +199,7 @@
     image_refs = refs[:count]
     (
         refs_ref, table_ref, weight_ref, stat_ref, partner_ref,
-        images, moved_a, moved_b, picked_a, picked_b, sums_a, sums_b, meta_vmem, meta, active, image_sem, sem,
+        images, moved_a, moved_b, picked_a, picked_b, sums_a, sums_b, index_ref, meta_vmem, meta, active, image_sem, sem,
     ) = refs[count:]
     total = images.shape[0]
     slots = weight_ref.shape[0]
@@ -207,7 +222,7 @@
         read_meta(images[i, IMAGE_ROWS:, :], meta_vmem, i)
     move_metas(meta_vmem, meta, sem)
     number = collect(meta, active, total, my_cls, my_dom)
-    lane = lax.broadcasted_iota(jnp.int32, (SPAN, LANES), 1)
+    index_ref[...] = turned_lanes(0)
 
     def one(at, moved, picked, sums):
         index = active[jnp.minimum(at, number - 1)]
@@ -224,41 +239,36 @@
             a2, b2, d2, e2 = re * c2, im * s2, im * c2, re * s2
             store_moved(moved, step, 0, [re, a1 + b1, a1 - b1, a2 + b2, a2 - b2])
             store_moved(moved, step, 1, [im, d1 - e1, d1 + e1, d2 - e2, d2 + e2])
-        for s in range(SHIFTS):
-            half, k = divmod(s, 3)
-            if k == 0:
-                pairs = lax.dot_general(
-                    picked[...],
-                    moved[half * LANES : (half + 1) * LANES, :],
-                    (((1,), (1,)), ((), ())),
-                    preferred_element_type=jnp.float32,
-                )
+        for half in range(2):
+            pairs = lax.dot_general(
+                picked[...],
+                moved[half * LANES : (half + 1) * LANES, :],
+                (((1,), (1,)), ((), ())),
+                preferred_element_type=jnp.float32,
+            )
             for j in range(classes):
-                part = pairs[j * 48 : j * 48 + SPAN]
-                part = jnp.where((lane >= k * SPAN) & (lane < (k + 1) * SPAN), part, 0.0)
-                turned = pltpu.roll(part, 0, 1, stride=1, stride_axis=0)
-                sums[k, pl.ds(half * classes + j, 1), :] = jnp.sum(turned, axis=0, keepdims=True)
-        found = []
-        for k in range(3):
-            plain = pltpu.roll(sums[k], (LANES - k * SPAN) % LANES, 1) if k else sums[k]
-            found.append(SOFTMAX_WARMTH * (plain + pltpu.roll(plain, LANES - ROT, 1)))
-        lanes = lax.broadcasted_iota(jnp.int32, found[0].shape, 1)
-        lines = lax.broadcasted_iota(jnp.int32, found[0].shape, 0)
-        valid = [lanes < ROT, lanes < ROT, (lanes < ROT) & (lines < classes)]
-        found = [jnp.where(v, f, NEGATIVE) for v, f in zip(valid, found)]
-        peak = jnp.maximum(jnp.maximum(found[0], found[1]), found[2])
-        peak = jnp.max(jnp.max(peak, axis=0, keepdims=True), axis=1, keepdims=True)
-        w = [jnp.where(v, jnp.exp(f - peak), 0.0) for v, f in zip(valid, found)]
-        total = w[0] + w[1] + w[2]
-        total = jnp.sum(jnp.sum(total, axis=0, keepdims=True), axis=1, keepdims=True)
+                total = jnp.zeros((8, LANES), jnp.float32)
+                for group in range(SPAN // 8):
+                    at = j * 48 + group * 8
+                    total = total + take_lanes(pairs[at : at + 8], index_ref[group * 8 : (group + 1) * 8, :])
+                sums[pl.ds(half * classes + j, 1), :] = jnp.sum(total, axis=0, keepdims=True)
+        scores = SOFTMAX_WARMTH * sums[...]
+        lanes = lax.broadcasted_iota(jnp.int32, scores.shape, 1)
+        lines = lax.broadcasted_iota(jnp.int32, scores.shape, 0)
+        upper = lines < classes
+        valid = (lanes < ROT) | ((lanes >= SPAN) & (lanes < SPAN + ROT))
+        valid = valid | (upper & (lanes >= 2 * SPAN) & (lanes < 2 * SPAN + ROT))
+        scores = jnp.where(valid, scores, NEGATIVE)
+        peak = jnp.max(jnp.max(scores, axis=0, keepdims=True), axis=1, keepdims=True)
+        w = jnp.where(valid, jnp.exp(scores - peak), 0.0)
+        total = jnp.sum(jnp.sum(w, axis=0, keepdims=True), axis=1, keepdims=True)
         stat_ref[pl.ds(2 * slot, 1), :] = jnp.broadcast_to(peak, (1, LANES))
         stat_ref[pl.ds(2 * slot + 1, 1), :] = jnp.broadcast_to(total, (1, LANES))
-        upper = lines < classes
-        first = jnp.where(upper, w[0], w[0] + w[1])
-        second = jnp.where(upper, w[1] + w[2], w[0] - w[1])
-        third = w[1] - w[2]
-        third = jnp.where(upper, third, 0.0)
-        weight_ref[slot] = first + pltpu.roll(second, SPAN, 1) + pltpu.roll(third, 2 * SPAN, 1)
+        after, before = pltpu.roll(w, LANES - SPAN, 1), pltpu.roll(w, SPAN, 1)
+        start = jnp.where(upper, SPAN, 0)
+        paired = jnp.where(lanes < start + SPAN, w + after, before - w)
+        paired = jnp.where(lanes < start + 2 * SPAN, paired, 0.0)
+        weight_ref[slot] = jnp.where(lanes < start, w, paired)
 
     def two(step, carry):
         one(2 * step, moved_a, picked_a, sums_a)
@@ -284,7 +294,8 @@
             pltpu.VMEM((total, IMAGE_ROWS + META_ROWS, LANES), jnp.bfloat16),
             *[pltpu.VMEM((2 * LANES, width), jnp.bfloat16)] * 2,
             *[pltpu.VMEM((48 * classes, width), jnp.bfloat16)] * 2,
-            *[pltpu.VMEM((3, 2 * classes, LANES), jnp.float32)] * 2,
+            *[pltpu.VMEM((2 * classes, LANES), jnp.float32)] * 2,
+            pltpu.VMEM((SPAN, LANES), jnp.int32),
             pltpu.VMEM((total, LANES), jnp.int32),
             pltpu.SMEM((total, LANES), jnp.int32),
             pltpu.SMEM((total + 1,), jnp.int32),
@@ -341,9 +352,10 @@
     out_ref = refs.pop(0) if last else None
     if not last:
         totals, mass = refs.pop(0), refs.pop(0)
-    images, weights, moved_a, moved_b, spread_a, spread_b, meta_vmem, meta, active, image_sem, meta_sem = refs[:11]
+    images, weights, moved_a, moved_b, spread_a, spread_b, index_ref, meta_vmem, meta, active = refs[:10]
+    image_sem, meta_sem = refs[10:12]
     if last:
-        totals, mass = refs[11:13]
+        totals, mass = refs[12:14]
     given_sem = refs[-1]
     depth, wave = images.shape[0], images.shape[1]
     per_row = weight_rows
@@ -380,7 +392,7 @@
     my_cls, my_dom = place_ref[0], place_ref[1]
     my_z, my_y = lax.div(my_dom, y_size), lax.rem(my_dom, y_size)
     lane = lax.broadcasted_iota(jnp.int32, (lines, LANES), 1)
-    lane_wide = lax.broadcasted_iota(jnp.int32, (SPAN, LANES), 1)
+    index_ref[...] = turned_lanes(-1)
 
     for w in range(waves):
         for copy in copies(w):
@@ -405,25 +417,13 @@
                 q = d_y * z_size + d_z
             at = pl.multiple_of(q * per_row + meta[i, SLOT + side] * lines, lines)
             mine = weights[pl.ds(at, lines), :] * share
-            parts = []
-            for k in range(3):
-                part = jnp.where((lane >= k * SPAN) & (lane < (k + 1) * SPAN), mine, 0.0)
-                parts.append(part + pltpu.roll(part, LANES - ROT, 1))
-
             def circulant(j):
                 line = []
                 for half in range(2):
                     at = half * classes + j
-                    turned = [
-                        pltpu.roll(
-                            jnp.broadcast_to(parts[k][at : at + 1], (SPAN, LANES)), 1, 1, stride=1, stride_axis=0
-                        )
-                        for k in range(3 - half)
-                    ]
-                    tile = jnp.where(lane_wide < SPAN, turned[0], turned[1])
-                    if half == 0:
-                        tile = jnp.where(lane_wide < 2 * SPAN, tile, turned[2])
-                    line.append(tile)
+                    row = jnp.broadcast_to(mine[at : at + 1], (8, LANES))
+                    tiles = [take_lanes(row, index_ref[g * 8 : (g + 1) * 8, :]) for g in range(SPAN // 8)]
+                    line.append(jnp.concatenate(tiles, axis=0))
                 return jnp.concatenate(line, axis=1)
 
             def one_step(step):
@@ -499,6 +499,7 @@
         pltpu.VMEM((2 * LANES, width), jnp.bfloat16),
         pltpu.VMEM((lines // 2 * SPAN, 2 * LANES), jnp.bfloat16),
         pltpu.VMEM((lines // 2 * SPAN, 2 * LANES), jnp.bfloat16),
+        pltpu.VMEM((SPAN, LANES), jnp.int32),
         pltpu.VMEM((wave, LANES), jnp.int32),
         pltpu.SMEM((wave, LANES), jnp.int32),
         pltpu.SMEM((wave + 1,), jnp.int32),

time: 118 us -> 118 us (level)
  transfers between devices with their start and end apart: 26 -> 26, of which waited for: 10 -> 10; matrix products, arithmetic and copies ran while one was open for 9% -> 9% of each run, Pallas kernels for 25% -> 23%
where the time goes in v2:
time: 118 us; the launch traced here: 117 us
  Pallas kernels  54.1 us (46%)
  starting transfers between devices  23.7 us (20%)
  waiting for transfers between devices  19.9 us (17%)
  local copies, waits for them, and re-layouts  17 us (14%)
  other arithmetic  2.07 us (2%)
    pallas_call x2, Pallas kernels, class_sum(): pl.pallas_call(functools.partial(sum_kernel, weight_rows, relative, z_siz...  39.5 us
    ppermute x26, starting transfers between devices, send(): return lax.ppermute(value, ('cls', 'dom'), moves(goal))  23.7 us
    ppermute x26, waiting for transfers between devices, send(): return lax.ppermute(value, ('cls', 'dom'), moves(goal))  19.9 us
    pallas_call x1, Pallas kernels, score(): pl.pallas_call(functools.partial(score_kernel, count), out_shape=(jax.Sha...  9.04 us
    unnamed x39, local copies, waits for them, and re-layouts  8.97 us
    reshape x1, local copies, waits for them, and re-layouts, shards(): lax.optimization_barrier((references, mine))[0]  7.11 us
    pallas_call x1, Pallas kernels, prepare(): pl.pallas_call(functools.partial(prep_kernel, local), out_shape=(shape, s...  4.09 us
  transfers between devices with their start and end apart: 26, of which 10 were waited for; matrix products, arithmetic and copies ran while one was open for 9% of the time, Pallas kernels for 23%

profile of v2, /device:TPU:0, one launch (start us, length us, event | category | flops | bytes accessed | tf_op | source)
XLA Modules:
  0.0 117.0 jit_solution(17935014819096884495)
XLA Ops:
  0.0 1.0 copy.10
  5.5 4.1 %prepare.1 = (bf16[4,336,128]{2,1,0:T(8,128)(2,1)}, bf16[4,336,128]{2,1,0:T(8,128)(2,1)}) custom-call(s32[2]{0:T(128)} %pad_add_fusion.1.place_ref, s32[4,10]{1,0:T(4,128)} %copy-done.8, s32[4,10]{1,0:T(4,128)} %copy-done.9, bf16[4,288,128]{2,1,0:T(8,128)(2,1)} %bitcast.7, bf16[4,288,128]{2,1,0:T(8,128)(2,1)} %copy-done.1, ...), custom_call_target="tpu_custom_call" | custom-call | tf_op jit(solution)/shard_map/prepare/pallas_call | solution.py:133
  9.6 4.8 %collective-permute-start.5 = (bf16[4,336,128]{2,1,0:T(8,128)(2,1)}, bf16[4,336,128]{2,1,0:T(8,128)(2,1)S(1)}, u32[]{:S(2)}, u32[]{:S(2)}) collective-permute-start(bf16[4,336,128]{2,1,0:T(8,128)(2,1)} %get-tuple-element.30.refs_0_), channel_id=1, source_target_pairs={{0,6},{1,7},{2,0},{3,1},{4,2},{5,3},{6,4},{7,5},{8,14},{9,15},{10,... | collective-permute-start | bytes 1032200 | tf_op jit(solution)/shard_map/ppermute | solution.py:550
  14.4 1.5 %collective-permute-start.3 = (bf16[4,336,128]{2,1,0:T(8,128)(2,1)}, bf16[4,336,128]{2,1,0:T(8,128)(2,1)S(1)}, u32[]{:S(2)}, u32[]{:S(2)}) collective-permute-start(bf16[4,336,128]{2,1,0:T(8,128)(2,1)} %get-tuple-element.30.refs_0_), channel_id=1, source_target_pairs={{0,1},{1,0},{2,3},{3,2},{4,5},{5,4},{6,7},{7,6},{8,24},{9,25},{10,... | collective-permute-start | bytes 1032200 | tf_op jit(solution)/shard_map/ppermute | solution.py:550
  15.9 1.5 %collective-permute-start.2 = (bf16[4,336,128]{2,1,0:T(8,128)(2,1)}, bf16[4,336,128]{2,1,0:T(8,128)(2,1)S(1)}, u32[]{:S(2)}, u32[]{:S(2)}) collective-permute-start(bf16[4,336,128]{2,1,0:T(8,128)(2,1)} %get-tuple-element.30.refs_0_), channel_id=1, source_target_pairs={{0,16},{1,17},{2,18},{3,19},{4,20},{5,21},{6,22},{7,23},{8,9},{9,8... | collective-permute-start | bytes 1032200 | tf_op jit(solution)/shard_map/ppermute | solution.py:550
  17.4 7.1 %reshape.7.refs_4_ = bf16[50,36,1024]{2,1,0:T(8,128)(2,1)} reshape(bf16[50,36864]{1,0:T(8,128)(2,1)} %param.7) | data formatting | bytes 7372800 | tf_op jit(solution)/shard_map/reshape | solution.py:561
  24.5 6.2 %collective-permute-done.4 = bf16[4,336,128]{2,1,0:T(8,128)(2,1)S(1)} collective-permute-done((bf16[4,336,128]{2,1,0:T(8,128)(2,1)}, bf16[4,336,128]{2,1,0:T(8,128)(2,1)S(1)}, u32[]{:S(2)}, u32[]{:S(2)}) %collective-permute-start.4) | collective-permute-done | bytes 344096 | tf_op jit(solution)/shard_map/ppermute | solution.py:550
  30.9 1.6 %collective-permute-start.9 = (bf16[4,336,128]{2,1,0:T(8,128)(2,1)S(1)}, bf16[4,336,128]{2,1,0:T(8,128)(2,1)S(1)}, u32[]{:S(2)}, u32[]{:S(2)}) collective-permute-start(bf16[4,336,128]{2,1,0:T(8,128)(2,1)S(1)} %collective-permute-done.2), channel_id=1, source_target_pairs={{0,1},{1,0},{2,3},{3,2},{4,5},{5,4},{6,7},{7,6},{8,24},{9,25},{10,... | collective-permute-start | bytes 1032200 | tf_op jit(solution)/shard_map/ppermute | solution.py:550
  33.0 1.5 %collective-permute-start.7 = (bf16[4,336,128]{2,1,0:T(8,128)(2,1)S(1)}, bf16[4,336,128]{2,1,0:T(8,128)(2,1)S(1)}, u32[]{:S(2)}, u32[]{:S(2)}) collective-permute-start(bf16[4,336,128]{2,1,0:T(8,128)(2,1)S(1)} %collective-permute-done.4), channel_id=1, source_target_pairs={{0,16},{1,17},{2,18},{3,19},{4,20},{5,21},{6,22},{7,23},{8,9},{9,8... | collective-permute-start | bytes 1032200 | tf_op jit(solution)/shard_map/ppermute | solution.py:550
  34.5 1.6 %collective-permute-start.6 = (bf16[4,336,128]{2,1,0:T(8,128)(2,1)S(1)}, bf16[4,336,128]{2,1,0:T(8,128)(2,1)S(1)}, u32[]{:S(2)}, u32[]{:S(2)}) collective-permute-start(bf16[4,336,128]{2,1,0:T(8,128)(2,1)S(1)} %collective-permute-done.4), channel_id=1, source_target_pairs={{0,2},{1,3},{2,4},{3,5},{4,6},{5,7},{6,0},{7,1},{8,10},{9,11},{10,... | collective-permute-start | bytes 1032200 | tf_op jit(solution)/shard_map/ppermute | solution.py:550
  36.1 0.9 copy-done.11
  37.0 9.0 %score.1 = (f32[8,8,128]{2,1,0:T(8,128)}, f32[16,128]{1,0:T(8,128)}, s32[8,3]{1,0:T(8,128)}) custom-call(s32[2]{0:T(128)} %pad_add_fusion.1.place_ref, bf16[4,336,128]{2,1,0:T(8,128)(2,1)} %get-tuple-element.30.refs_0_, bf16[4,336,128]{2,1,0:T(8,128)(2,1)} %get-tuple-element.35.refs_1_, bf16[8,336,128]{2,1,0:T(8,128)(2,1)} %copy-done.2, ...), custom_call_target="tpu_custom_call" | custom-call | flops 10000000000 | bytes 10000000 | tf_op jit(solution)/shard_map/score/pallas_call | solution.py:284
  47.1 0.9 collective-permute-start.11
  48.0 1.4 %collective-permute-done.13.refs_3_ = f32[16,128]{1,0:T(8,128)S(1)} collective-permute-done((f32[16,128]{1,0:T(8,128)}, f32[16,128]{1,0:T(8,128)S(1)}, u32[]{:S(2)}, u32[]{:S(2)}) %collective-permute-start.13) | collective-permute-done | bytes 8224 | tf_op jit(solution)/shard_map/ppermute | solution.py:550
  49.4 1.0 collective-permute-done.12.refs_2_
  51.1 1.2 %collective-permute-start.15 = (bf16[4,336,128]{2,1,0:T(8,128)(2,1)S(1)}, bf16[4,336,128]{2,1,0:T(8,128)(2,1)S(1)}, u32[]{:S(2)}, u32[]{:S(2)}) collective-permute-start(bf16[4,336,128]{2,1,0:T(8,128)(2,1)S(1)} %collective-permute-done.7), channel_id=1, source_target_pairs={{0,1},{1,0},{2,3},{3,2},{4,5},{5,4},{6,7},{7,6},{8,24},{9,25},{10,... | collective-permute-start | bytes 1032200 | tf_op jit(solution)/shard_map/ppermute | solution.py:550
  52.3 1.5 %normalise.1 = bf16[64,128]{1,0:T(8,128)(2,1)} custom-call(s32[2]{0:T(128)} %pad_add_fusion.1.place_ref, s32[8,3]{1,0:T(8,128)} %get-tuple-element.42.partner_ref, f32[8,8,128]{2,1,0:T(8,128)} %get-tuple-element.43.weight_ref, f32[16,128]{1,0:T(8,128)} %get-tuple-element.38.refs_0_, f32[16,128]{1,0:T(8,128)} %copy-done.7, f32[16,128]{1,0:T(8,128)} %copy-done.6, ...), custom_call_target="tpu_custom_call" | custom-call | tf_op jit(solution)/shard_map/normalise/pallas_call | solution.py:337
  53.8 2.2 %collective-permute-start.18 = (bf16[64,128]{1,0:T(8,128)(2,1)}, bf16[64,128]{1,0:T(8,128)(2,1)S(1)}, u32[]{:S(2)}, u32[]{:S(2)}) collective-permute-start(bf16[64,128]{1,0:T(8,128)(2,1)} %normalise.1), channel_id=1, source_target_pairs={{0,6},{1,7},{2,0},{3,1},{4,2},{5,3},{6,4},{7,5},{8,14},{9,15},{10,... | collective-permute-start | bytes 49160 | tf_op jit(solution)/shard_map/ppermute | solution.py:550
  56.6 1.2 %collective-permute-done.18 = bf16[64,128]{1,0:T(8,128)(2,1)S(1)} collective-permute-done((bf16[64,128]{1,0:T(8,128)(2,1)}, bf16[64,128]{1,0:T(8,128)(2,1)S(1)}, u32[]{:S(2)}, u32[]{:S(2)}) %collective-permute-start.18) | collective-permute-done | bytes 16416 | tf_op jit(solution)/shard_map/ppermute | solution.py:550
  57.8 3.1 %collective-permute-done.17 = bf16[64,128]{1,0:T(8,128)(2,1)S(1)} collective-permute-done((bf16[64,128]{1,0:T(8,128)(2,1)}, bf16[64,128]{1,0:T(8,128)(2,1)S(1)}, u32[]{:S(2)}, u32[]{:S(2)}) %collective-permute-start.17) | collective-permute-done | bytes 16416 | tf_op jit(solution)/shard_map/ppermute | solution.py:550
  60.9 0.9 collective-permute-done.16
  62.5 0.8 collective-permute-start.19
  64.1 2.7 %collective-permute-done.19.refs_7_ = bf16[256,128]{1,0:T(8,128)(2,1)S(1)} collective-permute-done((bf16[256,128]{1,0:T(8,128)(2,1)S(1)}, bf16[256,128]{1,0:T(8,128)(2,1)S(1)}, u32[]{:S(2)}, u32[]{:S(2)}) %collective-permute-start.19) | collective-permute-done | bytes 65568 | tf_op jit(solution)/shard_map/ppermute | solution.py:550
  66.8 0.9 constant_dynamic-update-slice_fusion.7
  69.9 0.8 collective-permute-start.22
  70.8 1.2 %collective-permute-start.23 = (bf16[8,336,128]{2,1,0:T(8,128)(2,1)S(1)}, bf16[8,336,128]{2,1,0:T(8,128)(2,1)}, u32[]{:S(2)}, u32[]{:S(2)}) collective-permute-start(bf16[8,336,128]{2,1,0:T(8,128)(2,1)S(1)} %collective-permute-done.14), channel_id=1, source_target_pairs={{0,1},{1,0},{2,3},{3,2},{4,5},{5,4},{6,7},{7,6},{8,24},{9,25},{10,... | collective-permute-start | bytes 2064392 | tf_op jit(solution)/shard_map/ppermute | solution.py:550
  72.2 0.9 copy-done.3
  73.1 16.7 %class_sum.2 = (f32[16000,128]{1,0:T(8,128)}, f32[56,128]{1,0:T(8,128)}) custom-call(s32[2]{0:T(128)} %pad_add_fusion.1.place_ref, bf16[4,336,128]{2,1,0:T(8,128)(2,1)} %get-tuple-element.30.refs_0_, bf16[4,336,128]{2,1,0:T(8,128)(2,1)} %get-tuple-element.35.refs_1_, bf16[8,336,128]{2,1,0:T(8,128)(2,1)} %copy-done.2, bf16[8,336,128]{2,1,0:T(8,128)(2,1)} %copy-done.11, ...), custom_call_target="tpu_custom_call" | custom-call | flops 12000000000 | bytes 10000000 | tf_op jit(solution)/shard_map/class_sum/pallas_call | solution.py:512
  90.4 1.9 %collective-permute-done.24.refs_4_ = bf16[8,336,128]{2,1,0:T(8,128)(2,1)S(1)} collective-permute-done((bf16[8,336,128]{2,1,0:T(8,128)(2,1)}, bf16[8,336,128]{2,1,0:T(8,128)(2,1)S(1)}, u32[]{:S(2)}, u32[]{:S(2)}) %collective-permute-start.24) | collective-permute-done | bytes 688160 | tf_op jit(solution)/shard_map/ppermute | solution.py:550
  92.3 1.0 collective-permute-done.25.refs_5_
  93.3 0.9 copy-done.13
  94.2 22.8 %class_sum.3 = bf16[50,36864]{1,0:T(8,128)(2,1)} custom-call(s32[2]{0:T(128)} %pad_add_fusion.1.place_ref, bf16[24,336,128]{2,1,0:T(8,128)(2,1)} %collective-permute-done.20.refs_0_, bf16[12,336,128]{2,1,0:T(8,128)(2,1)} %copy-done.10, bf16[8,336,128]{2,1,0:T(8,128)(2,1)} %collective-permute-done.22.refs_2_, ...), custom_call_target="tpu_custom_call" | custom-call | flops 13600000000 | bytes 10000000 | tf_op jit(solution)/shard_map/class_sum/pallas_call | solution.py:512
  (72 shorter events, 12.1 us)
Async XLA Ops:
  1.0 3.2 %copy-start = (bf16[1,4,288,128]{3,2,1,0:T(8,128)(2,1)}, bf16[1,4,288,128]{3,2,1,0:T(8,128)(2,1)S(1)}, u32[]{:S(2)}) copy-start(bf16[1,4,288,128]{3,2,1,0:T(8,128)(2,1)S(1)} %copy.10) | copy-start | bytes 884740
  1.0 3.2 %collective-permute-start.1 = (bf16[4,288,128]{2,1,0:T(8,128)(2,1)S(1)}, bf16[4,288,128]{2,1,0:T(8,128)(2,1)S(1)}, u32[]{:S(2)}, u32[]{:S(2)}) collective-permute-start(bf16[4,288,128]{2,1,0:T(8,128)(2,1)S(1)} %bitcast.6), channel_id=1, source_target_pairs={{0,8},{1,9},{2,10},{3,11},{4,12},{5,13},{6,14},{7,15},{8,0},{9,1},... | collective-permute-start | bytes 884744 | tf_op jit(solution)/shard_map/ppermute | solution.py:550
  3.1 1.2 collective-permute-start
  9.6 14.9 %collective-permute-start.5 = (bf16[4,336,128]{2,1,0:T(8,128)(2,1)}, bf16[4,336,128]{2,1,0:T(8,128)(2,1)S(1)}, u32[]{:S(2)}, u32[]{:S(2)}) collective-permute-start(bf16[4,336,128]{2,1,0:T(8,128)(2,1)} %get-tuple-element.30.refs_0_), channel_id=1, source_target_pairs={{0,6},{1,7},{2,0},{3,1},{4,2},{5,3},{6,4},{7,5},{8,14},{9,15},{10,... | collective-permute-start | bytes 1032200 | tf_op jit(solution)/shard_map/ppermute | solution.py:550
  14.4 16.3 %collective-permute-start.4 = (bf16[4,336,128]{2,1,0:T(8,128)(2,1)}, bf16[4,336,128]{2,1,0:T(8,128)(2,1)S(1)}, u32[]{:S(2)}, u32[]{:S(2)}) collective-permute-start(bf16[4,336,128]{2,1,0:T(8,128)(2,1)} %get-tuple-element.30.refs_0_), channel_id=1, source_target_pairs={{0,2},{1,3},{2,4},{3,5},{4,6},{5,7},{6,0},{7,1},{8,10},{9,11},{10,... | collective-permute-start | bytes 1032200 | tf_op jit(solution)/shard_map/ppermute | solution.py:550
  14.4 16.3 %collective-permute-start.3 = (bf16[4,336,128]{2,1,0:T(8,128)(2,1)}, bf16[4,336,128]{2,1,0:T(8,128)(2,1)S(1)}, u32[]{:S(2)}, u32[]{:S(2)}) collective-permute-start(bf16[4,336,128]{2,1,0:T(8,128)(2,1)} %get-tuple-element.30.refs_0_), channel_id=1, source_target_pairs={{0,1},{1,0},{2,3},{3,2},{4,5},{5,4},{6,7},{7,6},{8,24},{9,25},{10,... | collective-permute-start | bytes 1032200 | tf_op jit(solution)/shard_map/ppermute | solution.py:550
  15.9 14.8 %collective-permute-start.2 = (bf16[4,336,128]{2,1,0:T(8,128)(2,1)}, bf16[4,336,128]{2,1,0:T(8,128)(2,1)S(1)}, u32[]{:S(2)}, u32[]{:S(2)}) collective-permute-start(bf16[4,336,128]{2,1,0:T(8,128)(2,1)} %get-tuple-element.30.refs_0_), channel_id=1, source_target_pairs={{0,16},{1,17},{2,18},{3,19},{4,20},{5,21},{6,22},{7,23},{8,9},{9,8... | collective-permute-start | bytes 1032200 | tf_op jit(solution)/shard_map/ppermute | solution.py:550
  30.8 5.3 %copy-start.2 = (bf16[8,336,128]{2,1,0:T(8,128)(2,1)}, bf16[8,336,128]{2,1,0:T(8,128)(2,1)S(1)}, u32[]{:S(2)}) copy-start(bf16[8,336,128]{2,1,0:T(8,128)(2,1)S(1)} %constant_dynamic-update-slice_fusion.refs_2_) | copy-start | bytes 2064388
  30.8 5.3 %collective-permute-start.10 = (bf16[8,336,128]{2,1,0:T(8,128)(2,1)S(1)}, bf16[8,336,128]{2,1,0:T(8,128)(2,1)S(1)}, u32[]{:S(2)}, u32[]{:S(2)}) collective-permute-start(bf16[8,336,128]{2,1,0:T(8,128)(2,1)S(1)} %constant_dynamic-update-slice_fusion.refs_2_), channel_id=1, source_target_pairs={{0,8},{1,9},{2,10},{3,11},{4,12},{5,13},{6,14},{7,15},{8,0},{9,1},... | collective-permute-start | bytes 2064392 | tf_op jit(solution)/shard_map/ppermute | solution.py:550
  30.9 15.7 %collective-permute-start.9 = (bf16[4,336,128]{2,1,0:T(8,128)(2,1)S(1)}, bf16[4,336,128]{2,1,0:T(8,128)(2,1)S(1)}, u32[]{:S(2)}, u32[]{:S(2)}) collective-permute-start(bf16[4,336,128]{2,1,0:T(8,128)(2,1)S(1)} %collective-permute-done.2), channel_id=1, source_target_pairs={{0,1},{1,0},{2,3},{3,2},{4,5},{5,4},{6,7},{7,6},{8,24},{9,25},{10,... | collective-permute-start | bytes 1032200 | tf_op jit(solution)/shard_map/ppermute | solution.py:550
  32.5 14.6 %collective-permute-start.8 = (bf16[4,336,128]{2,1,0:T(8,128)(2,1)S(1)}, bf16[4,336,128]{2,1,0:T(8,128)(2,1)S(1)}, u32[]{:S(2)}, u32[]{:S(2)}) collective-permute-start(bf16[4,336,128]{2,1,0:T(8,128)(2,1)S(1)} %collective-permute-done.4), channel_id=1, source_target_pairs={{0,1},{1,0},{2,3},{3,2},{4,5},{5,4},{6,7},{7,6},{8,24},{9,25},{10,... | collective-permute-start | bytes 1032200 | tf_op jit(solution)/shard_map/ppermute | solution.py:550
  33.0 15.0 %collective-permute-start.7 = (bf16[4,336,128]{2,1,0:T(8,128)(2,1)S(1)}, bf16[4,336,128]{2,1,0:T(8,128)(2,1)S(1)}, u32[]{:S(2)}, u32[]{:S(2)}) collective-permute-start(bf16[4,336,128]{2,1,0:T(8,128)(2,1)S(1)} %collective-permute-done.4), channel_id=1, source_target_pairs={{0,16},{1,17},{2,18},{3,19},{4,20},{5,21},{6,22},{7,23},{8,9},{9,8... | collective-permute-start | bytes 1032200 | tf_op jit(solution)/shard_map/ppermute | solution.py:550
  34.5 13.5 %collective-permute-start.6 = (bf16[4,336,128]{2,1,0:T(8,128)(2,1)S(1)}, bf16[4,336,128]{2,1,0:T(8,128)(2,1)S(1)}, u32[]{:S(2)}, u32[]{:S(2)}) collective-permute-start(bf16[4,336,128]{2,1,0:T(8,128)(2,1)S(1)} %collective-permute-done.4), channel_id=1, source_target_pairs={{0,2},{1,3},{2,4},{3,5},{4,6},{5,7},{6,0},{7,1},{8,10},{9,11},{10,... | collective-permute-start | bytes 1032200 | tf_op jit(solution)/shard_map/ppermute | solution.py:550
  46.0 3.4 %collective-permute-start.13 = (f32[16,128]{1,0:T(8,128)}, f32[16,128]{1,0:T(8,128)S(1)}, u32[]{:S(2)}, u32[]{:S(2)}) collective-permute-start(f32[16,128]{1,0:T(8,128)} %get-tuple-element.38.refs_0_), channel_id=1, source_target_pairs={{0,24},{1,25},{2,26},{3,27},{4,28},{5,29},{6,30},{7,31},{8,16},{9,... | collective-permute-start | bytes 24584 | tf_op jit(solution)/shard_map/ppermute | solution.py:550
  46.5 3.9 %collective-permute-start.12 = (f32[16,128]{1,0:T(8,128)}, f32[16,128]{1,0:T(8,128)S(1)}, u32[]{:S(2)}, u32[]{:S(2)}) collective-permute-start(f32[16,128]{1,0:T(8,128)} %get-tuple-element.38.refs_0_), channel_id=1, source_target_pairs={{0,16},{1,17},{2,18},{3,19},{4,20},{5,21},{6,22},{7,23},{8,24},{9,... | collective-permute-start | bytes 24584 | tf_op jit(solution)/shard_map/ppermute | solution.py:550
  47.1 3.3 %collective-permute-start.11 = (f32[16,128]{1,0:T(8,128)}, f32[16,128]{1,0:T(8,128)S(1)}, u32[]{:S(2)}, u32[]{:S(2)}) collective-permute-start(f32[16,128]{1,0:T(8,128)} %get-tuple-element.38.refs_0_), channel_id=1, source_target_pairs={{0,8},{1,9},{2,10},{3,11},{4,12},{5,13},{6,14},{7,15},{8,0},{9,1},... | collective-permute-start | bytes 24584 | tf_op jit(solution)/shard_map/ppermute | solution.py:550
  49.4 2.9 %copy-start.5 = (f32[16,128]{1,0:T(8,128)}, f32[16,128]{1,0:T(8,128)S(1)}, u32[]{:S(2)}) copy-start(f32[16,128]{1,0:T(8,128)S(1)} %collective-permute-done.13.refs_3_) | copy-start | bytes 24580
  50.5 16.3 %collective-permute-start.14 = (bf16[8,336,128]{2,1,0:T(8,128)(2,1)S(1)}, bf16[8,336,128]{2,1,0:T(8,128)(2,1)S(1)}, u32[]{:S(2)}, u32[]{:S(2)}) collective-permute-start(bf16[8,336,128]{2,1,0:T(8,128)(2,1)S(1)} %constant_dynamic-update-slice_fusion.2), channel_id=1, source_target_pairs={{0,16},{1,17},{2,18},{3,19},{4,20},{5,21},{6,22},{7,23},{8,9},{9,8... | collective-permute-start | bytes 2064392 | tf_op jit(solution)/shard_map/ppermute | solution.py:550
  51.1 15.7 %collective-permute-start.15 = (bf16[4,336,128]{2,1,0:T(8,128)(2,1)S(1)}, bf16[4,336,128]{2,1,0:T(8,128)(2,1)S(1)}, u32[]{:S(2)}, u32[]{:S(2)}) collective-permute-start(bf16[4,336,128]{2,1,0:T(8,128)(2,1)S(1)} %collective-permute-done.7), channel_id=1, source_target_pairs={{0,1},{1,0},{2,3},{3,2},{4,5},{5,4},{6,7},{7,6},{8,24},{9,25},{10,... | collective-permute-start | bytes 1032200 | tf_op jit(solution)/shard_map/ppermute | solution.py:550
  53.8 3.9 %collective-permute-start.18 = (bf16[64,128]{1,0:T(8,128)(2,1)}, bf16[64,128]{1,0:T(8,128)(2,1)S(1)}, u32[]{:S(2)}, u32[]{:S(2)}) collective-permute-start(bf16[64,128]{1,0:T(8,128)(2,1)} %normalise.1), channel_id=1, source_target_pairs={{0,6},{1,7},{2,0},{3,1},{4,2},{5,3},{6,4},{7,5},{8,14},{9,15},{10,... | collective-permute-start | bytes 49160 | tf_op jit(solution)/shard_map/ppermute | solution.py:550
  56.0 4.8 %collective-permute-start.17 = (bf16[64,128]{1,0:T(8,128)(2,1)}, bf16[64,128]{1,0:T(8,128)(2,1)S(1)}, u32[]{:S(2)}, u32[]{:S(2)}) collective-permute-start(bf16[64,128]{1,0:T(8,128)(2,1)} %normalise.1), channel_id=1, source_target_pairs={{0,4},{1,5},{2,6},{3,7},{4,0},{5,1},{6,2},{7,3},{8,12},{9,13},{10,... | collective-permute-start | bytes 49160 | tf_op jit(solution)/shard_map/ppermute | solution.py:550
  56.0 5.7 %collective-permute-start.16 = (bf16[64,128]{1,0:T(8,128)(2,1)}, bf16[64,128]{1,0:T(8,128)(2,1)S(1)}, u32[]{:S(2)}, u32[]{:S(2)}) collective-permute-start(bf16[64,128]{1,0:T(8,128)(2,1)} %normalise.1), channel_id=1, source_target_pairs={{0,2},{1,3},{2,4},{3,5},{4,6},{5,7},{6,0},{7,1},{8,10},{9,11},{10,... | collective-permute-start | bytes 49160 | tf_op jit(solution)/shard_map/ppermute | solution.py:550
  62.5 9.5 %copy-start.4 = (bf16[256,128]{1,0:T(8,128)(2,1)}, bf16[256,128]{1,0:T(8,128)(2,1)S(1)}, u32[]{:S(2)}) copy-start(bf16[256,128]{1,0:T(8,128)(2,1)S(1)} %pad_maximum_fusion.refs_6_) | copy-start | bytes 196612
  62.5 4.3 %collective-permute-start.19 = (bf16[256,128]{1,0:T(8,128)(2,1)S(1)}, bf16[256,128]{1,0:T(8,128)(2,1)S(1)}, u32[]{:S(2)}, u32[]{:S(2)}) collective-permute-start(bf16[256,128]{1,0:T(8,128)(2,1)S(1)} %pad_maximum_fusion.refs_6_), channel_id=1, source_target_pairs={{0,1},{1,0},{2,3},{3,2},{4,5},{5,4},{6,7},{7,6},{8,9},{9,8},{10,11... | collective-permute-start | bytes 196616 | tf_op jit(solution)/shard_map/ppermute | solution.py:550
  66.8 5.3 %copy-start.14 = (bf16[256,128]{1,0:T(8,128)(2,1)}, bf16[256,128]{1,0:T(8,128)(2,1)S(1)}, u32[]{:S(2)}) copy-start(bf16[256,128]{1,0:T(8,128)(2,1)S(1)} %collective-permute-done.19.refs_7_) | copy-start | bytes 196612
  69.9 23.4 %collective-permute-start.20 = (bf16[24,336,128]{2,1,0:T(8,128)(2,1)}, bf16[24,336,128]{2,1,0:T(8,128)(2,1)}, u32[]{:S(2)}, u32[]{:S(2)}) collective-permute-start(bf16[24,336,128]{2,1,0:T(8,128)(2,1)} %constant_dynamic-update-slice_fusion.4.refs_4_), channel_id=1, source_target_pairs={{0,8},{1,9},{2,10},{3,11},{4,12},{5,13},{6,14},{7,15},{8,0},{9,1},... | collective-permute-start | bytes 6193160 | tf_op jit(solution)/shard_map/ppermute | solution.py:550
  69.9 19.8 %collective-permute-start.22 = (bf16[8,336,128]{2,1,0:T(8,128)(2,1)S(1)}, bf16[8,336,128]{2,1,0:T(8,128)(2,1)}, u32[]{:S(2)}, u32[]{:S(2)}) collective-permute-start(bf16[8,336,128]{2,1,0:T(8,128)(2,1)S(1)} %constant_dynamic-update-slice_fusion.2), channel_id=1, source_target_pairs={{0,1},{1,0},{2,3},{3,2},{4,5},{5,4},{6,7},{7,6},{8,24},{9,25},{10,... | collective-permute-start | bytes 2064392 | tf_op jit(solution)/shard_map/ppermute | solution.py:550
  70.8 19.0 %collective-permute-start.23 = (bf16[8,336,128]{2,1,0:T(8,128)(2,1)S(1)}, bf16[8,336,128]{2,1,0:T(8,128)(2,1)}, u32[]{:S(2)}, u32[]{:S(2)}) collective-permute-start(bf16[8,336,128]{2,1,0:T(8,128)(2,1)S(1)} %collective-permute-done.14), channel_id=1, source_target_pairs={{0,1},{1,0},{2,3},{3,2},{4,5},{5,4},{6,7},{7,6},{8,24},{9,25},{10,... | collective-permute-start | bytes 2064392 | tf_op jit(solution)/shard_map/ppermute | solution.py:550
  72.1 18.3 %collective-permute-start.21 = (bf16[12,336,128]{2,1,0:T(8,128)(2,1)S(1)}, bf16[12,336,128]{2,1,0:T(8,128)(2,1)S(1)}, u32[]{:S(2)}, u32[]{:S(2)}) collective-permute-start(bf16[12,336,128]{2,1,0:T(8,128)(2,1)S(1)} %constant_dynamic-update-slice_fusion.9.refs_5_), channel_id=1, source_target_pairs={{0,8},{1,9},{2,10},{3,11},{4,12},{5,13},{6,14},{7,15},{8,0},{9,1},... | collective-permute-start | bytes 3096584 | tf_op jit(solution)/shard_map/ppermute | solution.py:550
  89.8 2.6 %collective-permute-start.24 = (bf16[8,336,128]{2,1,0:T(8,128)(2,1)}, bf16[8,336,128]{2,1,0:T(8,128)(2,1)S(1)}, u32[]{:S(2)}, u32[]{:S(2)}) collective-permute-start(bf16[8,336,128]{2,1,0:T(8,128)(2,1)} %collective-permute-done.22.refs_2_), channel_id=1, source_target_pairs={{0,8},{1,9},{2,10},{3,11},{4,12},{5,13},{6,14},{7,15},{8,0},{9,1},... | collective-permute-start | bytes 2064392 | tf_op jit(solution)/shard_map/ppermute | solution.py:550
  90.4 3.0 %collective-permute-start.25 = (bf16[8,336,128]{2,1,0:T(8,128)(2,1)}, bf16[8,336,128]{2,1,0:T(8,128)(2,1)S(1)}, u32[]{:S(2)}, u32[]{:S(2)}) collective-permute-start(bf16[8,336,128]{2,1,0:T(8,128)(2,1)} %collective-permute-done.23.refs_3_), channel_id=1, source_target_pairs={{0,8},{1,9},{2,10},{3,11},{4,12},{5,13},{6,14},{7,15},{8,0},{9,1},... | collective-permute-start | bytes 2064392 | tf_op jit(solution)/shard_map/ppermute | solution.py:550
  90.4 2.9 %copy-start.10 = (bf16[12,336,128]{2,1,0:T(8,128)(2,1)}, bf16[12,336,128]{2,1,0:T(8,128)(2,1)S(1)}, u32[]{:S(2)}) copy-start(bf16[12,336,128]{2,1,0:T(8,128)(2,1)S(1)} %collective-permute-done.21.refs_1_) | copy-start | bytes 3096580
  (9 other events, 10.0 us)

commit v3 on v2

--- a/solution.py
+++ b/solution.py
@@ -446,15 +446,14 @@
             i = active[jnp.minimum(at, number - 1)]
             side = side_of(meta, i, my_cls)
             chosen = [meta[i, CLASS + side * classes + j] for j in range(classes)]
+            used = LANES + 2 * SPAN
+            added = jnp.dot(spread[:, :used], moved[:used, :], preferred_element_type=jnp.float32)
             for step in range(STEP_ANGLES):
-                columns = pl.ds(2 * step * LANES, 2 * LANES)
-                added = jnp.dot(spread[...], moved[:, columns], preferred_element_type=jnp.float32)
                 one_step(step)
-                for part in range(2):
-                    for j in range(classes):
-                        start = (2 * step + part) * local * SPAN
-                        to = pl.ds(pl.multiple_of(start + chosen[j] * SPAN, 8), SPAN)
-                        totals[to, :] += added[j * SPAN : (j + 1) * SPAN, part * LANES : (part + 1) * LANES]
+            for j in range(classes):
+                for tile in range(width // LANES):
+                    to = pl.ds(pl.multiple_of(tile * local * SPAN + chosen[j] * SPAN, 8), SPAN)
+                    totals[to, :] += added[j * SPAN : (j + 1) * SPAN, tile * LANES : (tile + 1) * LANES]
 
         def two(step, carry):
             at = 2 * step
@@ -562,11 +561,12 @@
     steps = jnp.asarray(tables[:, 1])
     tuned = x_size == 2 and y_size == 2 and z_size == 4
     if tuned:
-        e0, l0, z1, z3 = early(mine), late(mine), along_z(mine), back_z(mine)
-        e0, l0, z1, z3, refs = lax.optimization_barrier((e0, l0, z1, z3, refs))
+        e0, l0, z1 = early(mine), late(mine), along_z(mine)
+        e0, l0, z1, refs = lax.optimization_barrier((e0, l0, z1, refs))
         near = jnp.concatenate([e0, l0])
         row = [mine, rest, near, swap(near)]
         e1, l1, z2, f0 = early(z1), late(z1), along_z(z1), late(e0)
+        back = back_z(jnp.concatenate([mine, near]))
         weights, stats, partners = score(place, row, refs, steps, slots, classes)
         stats = [
             stats,
@@ -574,18 +574,17 @@
             send(stats, lambda x, c, z, y: (x + 1, c, z, y)),
             send(stats, lambda x, c, z, y: (x + 1, 1 - c, z, y)),
         ]
-        z2, z3, e1, l1, f0, *_ = lax.optimization_barrier((z2, z3, e1, l1, f0, *stats))
-        z23 = jnp.concatenate([z2, z3])
-        f1, e23 = late(e1), early(z23)
+        z2, e1, f0, *_ = lax.optimization_barrier((z2, e1, f0, *stats))
+        e2, f1 = early(z2), late(e1)
         weights = normalise(tuned, place, partners, weights, stats)
         weights = [weights] + [send(weights, lambda x, c, z, y, dz=dz: (x, c, z + dz, y)) for dz in range(1, z_size)]
         weights = jnp.concatenate(weights)
         weights = [weights, send(weights, lambda x, c, z, y: (x, c, z, y + 1))]
-        z23, e23, f1, *weights = lax.optimization_barrier((z23, e23, f1, *weights))
-        l23, f23 = late(z23), late(e23)
-        first = jnp.concatenate([z1, z23, e1, l1, f0])
-        second = jnp.concatenate([f1, e23])
-        parts = [[*row, first, second], [swap(first), swap(second), l23, f23]]
+        z2, e2, f0, *weights = lax.optimization_barrier((z2, e2, f0, *weights))
+        l2, f2, f3 = late(z2), late(e2), back_z(f0)
+        first = jnp.concatenate([z1, z2, e1, l1, f0])
+        second = jnp.concatenate([f1, e2])
+        parts = [[*row, first, second, back], [swap(first), swap(second), swap(back), l2, f2, f3]]
     else:
         row = lax.all_gather(mine, "cls", axis=0, tiled=True)
         parts = [[lax.all_gather(row, "dom", axis=0, tiled=True)]]
@@ -596,8 +595,9 @@
     held = None
     for k, part in enumerate(parts):
         if k:
-            *end, _ = lax.optimization_barrier((*part[2:], held[1]))
-            part = part[:2] + end + [swap(block) for block in end]
+            *end, _ = lax.optimization_barrier((*part[3:], held[1]))
+            end = jnp.concatenate(end)
+            part = part[:3] + [end, swap(end)]
         held = class_sum(
             place, part, weights, steps, held, k == len(parts) - 1, tuned, z_size, y_size, local, block_width, 2 * classes, slots * 2 * classes
         )

time: 118 us -> 117 us (level)
  waiting for transfers between devices: 19.9 us -> 25.7 us
  Pallas kernels: 54.1 us -> 48.4 us
  starting transfers between devices: 23.7 us -> 22 us
    ppermute x26 -> x27, waiting for transfers between devices: 19.9 us -> 25.7 us  [send(): return lax.ppermute(value, ('cls', 'dom'), moves(goal))]
    pallas_call x2, Pallas kernels: 39.5 us -> 33.8 us  [class_sum(): pl.pallas_call(functools.partial(sum_kernel, weight_rows, relative, z_siz...]
    ppermute x26 -> x27, starting transfers between devices: 23.7 us -> 22 us  [send(): return lax.ppermute(value, ('cls', 'dom'), moves(goal))]
    unnamed x39 -> x44, local copies, waits for them, and re-layouts: 8.97 us -> 9.11 us
  transfers between devices with their start and end apart: 26 -> 27, of which waited for: 10 -> 8; matrix products, arithmetic and copies ran while one was open for 9% -> 12% of each run, Pallas kernels for 23% -> 23%
where the time goes in v3:
time: 117 us; the launch traced here: 116 us
  Pallas kernels  48.4 us (41%)
  waiting for transfers between devices  25.7 us (22%)
  starting transfers between devices  22 us (19%)
  local copies, waits for them, and re-layouts  17.1 us (15%)
  other arithmetic  2.17 us (2%)
    pallas_call x2, Pallas kernels, class_sum(): pl.pallas_call(functools.partial(sum_kernel, weight_rows, relative, z_siz...  33.8 us
    ppermute x27, waiting for transfers between devices, send(): return lax.ppermute(value, ('cls', 'dom'), moves(goal))  25.7 us
    ppermute x27, starting transfers between devices, send(): return lax.ppermute(value, ('cls', 'dom'), moves(goal))  22 us
    unnamed x44, local copies, waits for them, and re-layouts  9.11 us
    pallas_call x1, Pallas kernels, score(): pl.pallas_call(functools.partial(score_kernel, count), out_shape=(jax.Sha...  9.03 us
    reshape x1, local copies, waits for them, and re-layouts, shards(): lax.optimization_barrier((references, mine))[0]  7.11 us
    pallas_call x1, Pallas kernels, prepare(): pl.pallas_call(functools.partial(prep_kernel, local), out_shape=(shape, s...  4.09 us
  transfers between devices with their start and end apart: 27, of which 8 were waited for; matrix products, arithmetic and copies ran while one was open for 12% of the time, Pallas kernels for 23%

profile of v3, /device:TPU:0, one launch (start us, length us, event | category | flops | bytes accessed | tf_op | source)
XLA Modules:
  0.0 115.6 jit_solution(35850811777074427)
XLA Ops:
  0.0 1.0 copy.10
  1.5 0.8 copy.7
  2.3 0.8 pad_add_fusion.near_ref
  5.5 4.1 %prepare.1 = (bf16[4,336,128]{2,1,0:T(8,128)(2,1)}, bf16[4,336,128]{2,1,0:T(8,128)(2,1)}) custom-call(s32[2]{0:T(128)} %pad_add_fusion.1.place_ref, s32[4,10]{1,0:T(4,128)} %copy-done.11, s32[4,10]{1,0:T(4,128)} %copy-done.12, bf16[4,288,128]{2,1,0:T(8,128)(2,1)} %bitcast.7, bf16[4,288,128]{2,1,0:T(8,128)(2,1)} %copy-done.2, ...), custom_call_target="tpu_custom_call" | custom-call | tf_op jit(solution)/shard_map/prepare/pallas_call | solution.py:133
  9.6 2.7 %collective-permute-start.2 = (bf16[4,336,128]{2,1,0:T(8,128)(2,1)}, bf16[4,336,128]{2,1,0:T(8,128)(2,1)S(1)}, u32[]{:S(2)}, u32[]{:S(2)}) collective-permute-start(bf16[4,336,128]{2,1,0:T(8,128)(2,1)} %get-tuple-element.28.refs_0_), channel_id=1, source_target_pairs={{0,16},{1,17},{2,18},{3,19},{4,20},{5,21},{6,22},{7,23},{8,9},{9,8... | collective-permute-start | bytes 1032200 | tf_op jit(solution)/shard_map/ppermute | solution.py:549
  12.2 1.5 %collective-permute-start.3 = (bf16[4,336,128]{2,1,0:T(8,128)(2,1)}, bf16[4,336,128]{2,1,0:T(8,128)(2,1)S(1)}, u32[]{:S(2)}, u32[]{:S(2)}) collective-permute-start(bf16[4,336,128]{2,1,0:T(8,128)(2,1)} %get-tuple-element.28.refs_0_), channel_id=1, source_target_pairs={{0,1},{1,0},{2,3},{3,2},{4,5},{5,4},{6,7},{7,6},{8,24},{9,25},{10,... | collective-permute-start | bytes 1032200 | tf_op jit(solution)/shard_map/ppermute | solution.py:549
  13.8 1.6 %collective-permute-start.4 = (bf16[4,336,128]{2,1,0:T(8,128)(2,1)}, bf16[4,336,128]{2,1,0:T(8,128)(2,1)S(1)}, u32[]{:S(2)}, u32[]{:S(2)}) collective-permute-start(bf16[4,336,128]{2,1,0:T(8,128)(2,1)} %get-tuple-element.28.refs_0_), channel_id=1, source_target_pairs={{0,2},{1,3},{2,4},{3,5},{4,6},{5,7},{6,0},{7,1},{8,10},{9,11},{10,... | collective-permute-start | bytes 1032200 | tf_op jit(solution)/shard_map/ppermute | solution.py:549
  15.3 7.1 %reshape.7.refs_4_ = bf16[50,36,1024]{2,1,0:T(8,128)(2,1)} reshape(bf16[50,36864]{1,0:T(8,128)(2,1)} %param.7) | data formatting | bytes 7372800 | tf_op jit(solution)/shard_map/reshape | solution.py:560
  22.5 3.2 %collective-permute-done.4 = bf16[4,336,128]{2,1,0:T(8,128)(2,1)S(1)} collective-permute-done((bf16[4,336,128]{2,1,0:T(8,128)(2,1)}, bf16[4,336,128]{2,1,0:T(8,128)(2,1)S(1)}, u32[]{:S(2)}, u32[]{:S(2)}) %collective-permute-start.4) | collective-permute-done | bytes 344096 | tf_op jit(solution)/shard_map/ppermute | solution.py:549
  27.1 3.8 %collective-permute-start.21 = (bf16[12,336,128]{2,1,0:T(8,128)(2,1)S(1)}, bf16[12,336,128]{2,1,0:T(8,128)(2,1)}, u32[]{:S(2)}, u32[]{:S(2)}) collective-permute-start(bf16[12,336,128]{2,1,0:T(8,128)(2,1)S(1)} %pad_maximum_fusion), channel_id=1, source_target_pairs={{0,6},{1,7},{2,0},{3,1},{4,2},{5,3},{6,4},{7,5},{8,14},{9,15},{10,... | collective-permute-start | bytes 3096584 | tf_op jit(solution)/shard_map/ppermute | solution.py:549
  30.9 0.8 copy-done.14
  31.7 9.0 %score.1 = (f32[8,8,128]{2,1,0:T(8,128)}, f32[16,128]{1,0:T(8,128)}, s32[8,3]{1,0:T(8,128)}) custom-call(s32[2]{0:T(128)} %pad_add_fusion.1.place_ref, bf16[4,336,128]{2,1,0:T(8,128)(2,1)} %get-tuple-element.28.refs_0_, bf16[4,336,128]{2,1,0:T(8,128)(2,1)} %get-tuple-element.32.refs_1_, bf16[8,336,128]{2,1,0:T(8,128)(2,1)} %copy-done.5, ...), custom_call_target="tpu_custom_call" | custom-call | flops 10000000000 | bytes 10000000 | tf_op jit(solution)/shard_map/score/pallas_call | solution.py:284
  40.8 1.5 %collective-permute-start.10 = (f32[16,128]{1,0:T(8,128)}, f32[16,128]{1,0:T(8,128)S(1)}, u32[]{:S(2)}, u32[]{:S(2)}) collective-permute-start(f32[16,128]{1,0:T(8,128)} %get-tuple-element.35.refs_0_), channel_id=1, source_target_pairs={{0,16},{1,17},{2,18},{3,19},{4,20},{5,21},{6,22},{7,23},{8,24},{9,... | collective-permute-start | bytes 24584 | tf_op jit(solution)/shard_map/ppermute | solution.py:549
  43.0 1.7 %collective-permute-done.10.refs_2_ = f32[16,128]{1,0:T(8,128)S(1)} collective-permute-done((f32[16,128]{1,0:T(8,128)}, f32[16,128]{1,0:T(8,128)S(1)}, u32[]{:S(2)}, u32[]{:S(2)}) %collective-permute-start.10) | collective-permute-done | bytes 8224 | tf_op jit(solution)/shard_map/ppermute | solution.py:549
  44.7 0.9 collective-permute-done.11.refs_3_
  46.3 1.5 %collective-permute-start.19 = (bf16[4,336,128]{2,1,0:T(8,128)(2,1)S(1)}, bf16[4,336,128]{2,1,0:T(8,128)(2,1)S(1)}, u32[]{:S(2)}, u32[]{:S(2)}) collective-permute-start(bf16[4,336,128]{2,1,0:T(8,128)(2,1)S(1)} %collective-permute-done.6), channel_id=1, source_target_pairs={{0,1},{1,0},{2,3},{3,2},{4,5},{5,4},{6,7},{7,6},{8,24},{9,25},{10,... | collective-permute-start | bytes 1032200 | tf_op jit(solution)/shard_map/ppermute | solution.py:549
  47.9 1.5 %normalise.1 = bf16[64,128]{1,0:T(8,128)(2,1)} custom-call(s32[2]{0:T(128)} %pad_add_fusion.1.place_ref, s32[8,3]{1,0:T(8,128)} %get-tuple-element.38.partner_ref, f32[8,8,128]{2,1,0:T(8,128)} %get-tuple-element.39.weight_ref, f32[16,128]{1,0:T(8,128)} %get-tuple-element.35.refs_0_, f32[16,128]{1,0:T(8,128)} %copy-done.10, f32[16,128]{1,0:T(8,128)} %copy-done.8, ...), custom_call_target="tpu_custom_call" | custom-call | tf_op jit(solution)/shard_map/normalise/pallas_call | solution.py:337
  50.0 10.7 %collective-permute-done.13 = bf16[64,128]{1,0:T(8,128)(2,1)S(1)} collective-permute-done((bf16[64,128]{1,0:T(8,128)(2,1)}, bf16[64,128]{1,0:T(8,128)(2,1)S(1)}, u32[]{:S(2)}, u32[]{:S(2)}) %collective-permute-start.13) | collective-permute-done | bytes 16416 | tf_op jit(solution)/shard_map/ppermute | solution.py:549
  60.8 0.9 collective-permute-start.17
  61.7 3.0 %collective-permute-done.15 = bf16[64,128]{1,0:T(8,128)(2,1)S(1)} collective-permute-done((bf16[64,128]{1,0:T(8,128)(2,1)}, bf16[64,128]{1,0:T(8,128)(2,1)S(1)}, u32[]{:S(2)}, u32[]{:S(2)}) %collective-permute-start.15) | collective-permute-done | bytes 16416 | tf_op jit(solution)/shard_map/ppermute | solution.py:549
  66.0 0.8 constant_dynamic-update-slice_fusion.6
  66.8 2.9 %collective-permute-done.16.refs_8_.refs_6_ = bf16[256,128]{1,0:T(8,128)(2,1)S(1)} collective-permute-done((bf16[256,128]{1,0:T(8,128)(2,1)S(1)}, bf16[256,128]{1,0:T(8,128)(2,1)S(1)}, u32[]{:S(2)}, u32[]{:S(2)}) %collective-permute-start.16) | collective-permute-done | bytes 65568 | tf_op jit(solution)/shard_map/ppermute | solution.py:549
  70.4 1.3 %collective-permute-start.24 = (bf16[4,336,128]{2,1,0:T(8,128)(2,1)S(1)}, bf16[4,336,128]{2,1,0:T(8,128)(2,1)S(1)}, u32[]{:S(2)}, u32[]{:S(2)}) collective-permute-start(bf16[4,336,128]{2,1,0:T(8,128)(2,1)S(1)} %collective-permute-done.12), channel_id=1, source_target_pairs={{0,1},{1,0},{2,3},{3,2},{4,5},{5,4},{6,7},{7,6},{8,24},{9,25},{10,... | collective-permute-start | bytes 1032200 | tf_op jit(solution)/shard_map/ppermute | solution.py:549
  71.7 1.9 %collective-permute-start.25 = (bf16[4,336,128]{2,1,0:T(8,128)(2,1)S(1)}, bf16[4,336,128]{2,1,0:T(8,128)(2,1)S(1)}, u32[]{:S(2)}, u32[]{:S(2)}) collective-permute-start(bf16[4,336,128]{2,1,0:T(8,128)(2,1)S(1)} %collective-permute-done.7), channel_id=1, source_target_pairs={{0,6},{1,7},{2,0},{3,1},{4,2},{5,3},{6,4},{7,5},{8,14},{9,15},{10,... | collective-permute-start | bytes 1032200 | tf_op jit(solution)/shard_map/ppermute | solution.py:549
  73.7 0.8 constant_dynamic-update-slice_fusion.5
  75.2 0.8 constant_dynamic-update-slice_fusion.3
  76.0 0.8 constant_dynamic-update-slice_fusion.2.refs_4_
  76.8 15.9 %class_sum.2 = (f32[16000,128]{1,0:T(8,128)}, f32[56,128]{1,0:T(8,128)}) custom-call(s32[2]{0:T(128)} %pad_add_fusion.1.place_ref, bf16[4,336,128]{2,1,0:T(8,128)(2,1)} %get-tuple-element.28.refs_0_, bf16[4,336,128]{2,1,0:T(8,128)(2,1)} %get-tuple-element.32.refs_1_, bf16[8,336,128]{2,1,0:T(8,128)(2,1)} %copy-done.5, bf16[8,336,128]{2,1,0:T(8,128)(2,1)} %copy-done.14, ...), custom_call_target="tpu_custom_call" | custom-call | flops 12800000000 | bytes 10000000 | tf_op jit(solution)/shard_map/class_sum/pallas_call | solution.py:511
  92.9 0.9 copy-done.4
  93.8 2.8 %collective-permute-done.20.refs_1_ = bf16[8,336,128]{2,1,0:T(8,128)(2,1)S(1)} collective-permute-done((bf16[8,336,128]{2,1,0:T(8,128)(2,1)S(1)}, bf16[8,336,128]{2,1,0:T(8,128)(2,1)S(1)}, u32[]{:S(2)}, u32[]{:S(2)}) %collective-permute-start.20) | collective-permute-done | bytes 688160 | tf_op jit(solution)/shard_map/ppermute | solution.py:549
  96.6 0.8 copy-done.15
  97.7 17.9 %class_sum.3 = bf16[50,36864]{1,0:T(8,128)(2,1)} custom-call(s32[2]{0:T(128)} %pad_add_fusion.1.place_ref, bf16[20,336,128]{2,1,0:T(8,128)(2,1)} %collective-permute-done.18.refs_0_, bf16[8,336,128]{2,1,0:T(8,128)(2,1)} %copy-done.15, bf16[12,336,128]{2,1,0:T(8,128)(2,1)} %collective-permute-done.22.refs_2_, bf16[12,336,128]{2,1,0:T(8,128)(2,1)} %copy-done.6, ...), custom_call_target="tpu_custom_call" | custom-call | flops 12800000000 | bytes 10000000 | tf_op jit(solution)/shard_map/class_sum/pallas_call | solution.py:511
  (80 shorter events, 9.8 us)
Async XLA Ops:
  1.0 3.2 %collective-permute-start.1 = (bf16[4,288,128]{2,1,0:T(8,128)(2,1)S(1)}, bf16[4,288,128]{2,1,0:T(8,128)(2,1)S(1)}, u32[]{:S(2)}, u32[]{:S(2)}) collective-permute-start(bf16[4,288,128]{2,1,0:T(8,128)(2,1)S(1)} %bitcast.6), channel_id=1, source_target_pairs={{0,8},{1,9},{2,10},{3,11},{4,12},{5,13},{6,14},{7,15},{8,0},{9,1},... | collective-permute-start | bytes 884744 | tf_op jit(solution)/shard_map/ppermute | solution.py:549
  3.1 1.2 %collective-permute-start = (s32[4,10]{1,0:T(4,128)S(1)}, s32[4,10]{1,0:T(4,128)S(1)}, u32[]{:S(2)}, u32[]{:S(2)}) collective-permute-start(s32[4,10]{1,0:T(4,128)S(1)} %pad_add_fusion.near_ref), channel_id=1, source_target_pairs={{0,8},{1,9},{2,10},{3,11},{4,12},{5,13},{6,14},{7,15},{8,0},{9,1},... | collective-permute-start | bytes 488 | tf_op jit(solution)/shard_map/ppermute | solution.py:549
  9.6 17.4 %copy-start.1 = (bf16[4,336,128]{2,1,0:T(8,128)(2,1)S(1)}, bf16[4,336,128]{2,1,0:T(8,128)(2,1)}, u32[]{:S(2)}) copy-start(bf16[4,336,128]{2,1,0:T(8,128)(2,1)} %get-tuple-element.28.refs_0_) | copy-start | bytes 1032196
  9.6 12.9 %collective-permute-start.2 = (bf16[4,336,128]{2,1,0:T(8,128)(2,1)}, bf16[4,336,128]{2,1,0:T(8,128)(2,1)S(1)}, u32[]{:S(2)}, u32[]{:S(2)}) collective-permute-start(bf16[4,336,128]{2,1,0:T(8,128)(2,1)} %get-tuple-element.28.refs_0_), channel_id=1, source_target_pairs={{0,16},{1,17},{2,18},{3,19},{4,20},{5,21},{6,22},{7,23},{8,9},{9,8... | collective-permute-start | bytes 1032200 | tf_op jit(solution)/shard_map/ppermute | solution.py:549
  12.2 10.2 %collective-permute-start.3 = (bf16[4,336,128]{2,1,0:T(8,128)(2,1)}, bf16[4,336,128]{2,1,0:T(8,128)(2,1)S(1)}, u32[]{:S(2)}, u32[]{:S(2)}) collective-permute-start(bf16[4,336,128]{2,1,0:T(8,128)(2,1)} %get-tuple-element.28.refs_0_), channel_id=1, source_target_pairs={{0,1},{1,0},{2,3},{3,2},{4,5},{5,4},{6,7},{7,6},{8,24},{9,25},{10,... | collective-permute-start | bytes 1032200 | tf_op jit(solution)/shard_map/ppermute | solution.py:549
  13.8 11.8 %collective-permute-start.4 = (bf16[4,336,128]{2,1,0:T(8,128)(2,1)}, bf16[4,336,128]{2,1,0:T(8,128)(2,1)S(1)}, u32[]{:S(2)}, u32[]{:S(2)}) collective-permute-start(bf16[4,336,128]{2,1,0:T(8,128)(2,1)} %get-tuple-element.28.refs_0_), channel_id=1, source_target_pairs={{0,2},{1,3},{2,4},{3,5},{4,6},{5,7},{6,0},{7,1},{8,10},{9,11},{10,... | collective-permute-start | bytes 1032200 | tf_op jit(solution)/shard_map/ppermute | solution.py:549
  25.7 5.2 %copy-start.5 = (bf16[8,336,128]{2,1,0:T(8,128)(2,1)}, bf16[8,336,128]{2,1,0:T(8,128)(2,1)S(1)}, u32[]{:S(2)}) copy-start(bf16[8,336,128]{2,1,0:T(8,128)(2,1)S(1)} %constant_dynamic-update-slice_fusion.refs_2_) | copy-start | bytes 2064388
  25.7 5.2 %collective-permute-start.8 = (bf16[8,336,128]{2,1,0:T(8,128)(2,1)S(1)}, bf16[8,336,128]{2,1,0:T(8,128)(2,1)S(1)}, u32[]{:S(2)}, u32[]{:S(2)}) collective-permute-start(bf16[8,336,128]{2,1,0:T(8,128)(2,1)S(1)} %constant_dynamic-update-slice_fusion.refs_2_), channel_id=1, source_target_pairs={{0,8},{1,9},{2,10},{3,11},{4,12},{5,13},{6,14},{7,15},{8,0},{9,1},... | collective-permute-start | bytes 2064392 | tf_op jit(solution)/shard_map/ppermute | solution.py:549
  25.8 16.5 %collective-permute-start.5 = (bf16[4,336,128]{2,1,0:T(8,128)(2,1)S(1)}, bf16[4,336,128]{2,1,0:T(8,128)(2,1)S(1)}, u32[]{:S(2)}, u32[]{:S(2)}) collective-permute-start(bf16[4,336,128]{2,1,0:T(8,128)(2,1)S(1)} %collective-permute-done.4), channel_id=1, source_target_pairs={{0,2},{1,3},{2,4},{3,5},{4,6},{5,7},{6,0},{7,1},{8,10},{9,11},{10,... | collective-permute-start | bytes 1032200 | tf_op jit(solution)/shard_map/ppermute | solution.py:549
  25.9 16.5 %collective-permute-start.6 = (bf16[4,336,128]{2,1,0:T(8,128)(2,1)S(1)}, bf16[4,336,128]{2,1,0:T(8,128)(2,1)S(1)}, u32[]{:S(2)}, u32[]{:S(2)}) collective-permute-start(bf16[4,336,128]{2,1,0:T(8,128)(2,1)S(1)} %collective-permute-done.4), channel_id=1, source_target_pairs={{0,16},{1,17},{2,18},{3,19},{4,20},{5,21},{6,22},{7,23},{8,9},{9,8... | collective-permute-start | bytes 1032200 | tf_op jit(solution)/shard_map/ppermute | solution.py:549
  26.5 16.5 %collective-permute-start.7 = (bf16[4,336,128]{2,1,0:T(8,128)(2,1)S(1)}, bf16[4,336,128]{2,1,0:T(8,128)(2,1)S(1)}, u32[]{:S(2)}, u32[]{:S(2)}) collective-permute-start(bf16[4,336,128]{2,1,0:T(8,128)(2,1)S(1)} %collective-permute-done.2), channel_id=1, source_target_pairs={{0,1},{1,0},{2,3},{3,2},{4,5},{5,4},{6,7},{7,6},{8,24},{9,25},{10,... | collective-permute-start | bytes 1032200 | tf_op jit(solution)/shard_map/ppermute | solution.py:549
  27.1 39.7 %collective-permute-start.21 = (bf16[12,336,128]{2,1,0:T(8,128)(2,1)S(1)}, bf16[12,336,128]{2,1,0:T(8,128)(2,1)}, u32[]{:S(2)}, u32[]{:S(2)}) collective-permute-start(bf16[12,336,128]{2,1,0:T(8,128)(2,1)S(1)} %pad_maximum_fusion), channel_id=1, source_target_pairs={{0,6},{1,7},{2,0},{3,1},{4,2},{5,3},{6,4},{7,5},{8,14},{9,15},{10,... | collective-permute-start | bytes 3096584 | tf_op jit(solution)/shard_map/ppermute | solution.py:549
  40.8 3.9 %collective-permute-start.10 = (f32[16,128]{1,0:T(8,128)}, f32[16,128]{1,0:T(8,128)S(1)}, u32[]{:S(2)}, u32[]{:S(2)}) collective-permute-start(f32[16,128]{1,0:T(8,128)} %get-tuple-element.35.refs_0_), channel_id=1, source_target_pairs={{0,16},{1,17},{2,18},{3,19},{4,20},{5,21},{6,22},{7,23},{8,24},{9,... | collective-permute-start | bytes 24584 | tf_op jit(solution)/shard_map/ppermute | solution.py:549
  42.3 3.3 %collective-permute-start.11 = (f32[16,128]{1,0:T(8,128)}, f32[16,128]{1,0:T(8,128)S(1)}, u32[]{:S(2)}, u32[]{:S(2)}) collective-permute-start(f32[16,128]{1,0:T(8,128)} %get-tuple-element.35.refs_0_), channel_id=1, source_target_pairs={{0,24},{1,25},{2,26},{3,27},{4,28},{5,29},{6,30},{7,31},{8,16},{9,... | collective-permute-start | bytes 24584 | tf_op jit(solution)/shard_map/ppermute | solution.py:549
  42.3 3.3 %collective-permute-start.9 = (f32[16,128]{1,0:T(8,128)}, f32[16,128]{1,0:T(8,128)S(1)}, u32[]{:S(2)}, u32[]{:S(2)}) collective-permute-start(f32[16,128]{1,0:T(8,128)} %get-tuple-element.35.refs_0_), channel_id=1, source_target_pairs={{0,8},{1,9},{2,10},{3,11},{4,12},{5,13},{6,14},{7,15},{8,0},{9,1},... | collective-permute-start | bytes 24584 | tf_op jit(solution)/shard_map/ppermute | solution.py:549
  45.6 24.1 %collective-permute-start.12 = (bf16[4,336,128]{2,1,0:T(8,128)(2,1)S(1)}, bf16[4,336,128]{2,1,0:T(8,128)(2,1)S(1)}, u32[]{:S(2)}, u32[]{:S(2)}) collective-permute-start(bf16[4,336,128]{2,1,0:T(8,128)(2,1)S(1)} %collective-permute-done.5), channel_id=1, source_target_pairs={{0,16},{1,17},{2,18},{3,19},{4,20},{5,21},{6,22},{7,23},{8,9},{9,8... | collective-permute-start | bytes 1032200 | tf_op jit(solution)/shard_map/ppermute | solution.py:549
  46.3 25.4 %collective-permute-start.19 = (bf16[4,336,128]{2,1,0:T(8,128)(2,1)S(1)}, bf16[4,336,128]{2,1,0:T(8,128)(2,1)S(1)}, u32[]{:S(2)}, u32[]{:S(2)}) collective-permute-start(bf16[4,336,128]{2,1,0:T(8,128)(2,1)S(1)} %collective-permute-done.6), channel_id=1, source_target_pairs={{0,1},{1,0},{2,3},{3,2},{4,5},{5,4},{6,7},{7,6},{8,24},{9,25},{10,... | collective-permute-start | bytes 1032200 | tf_op jit(solution)/shard_map/ppermute | solution.py:549
  49.4 11.3 %collective-permute-start.13 = (bf16[64,128]{1,0:T(8,128)(2,1)}, bf16[64,128]{1,0:T(8,128)(2,1)S(1)}, u32[]{:S(2)}, u32[]{:S(2)}) collective-permute-start(bf16[64,128]{1,0:T(8,128)(2,1)} %normalise.1), channel_id=1, source_target_pairs={{0,2},{1,3},{2,4},{3,5},{4,6},{5,7},{6,0},{7,1},{8,10},{9,11},{10,... | collective-permute-start | bytes 49160 | tf_op jit(solution)/shard_map/ppermute | solution.py:549
  49.4 11.4 %collective-permute-start.14 = (bf16[64,128]{1,0:T(8,128)(2,1)}, bf16[64,128]{1,0:T(8,128)(2,1)S(1)}, u32[]{:S(2)}, u32[]{:S(2)}) collective-permute-start(bf16[64,128]{1,0:T(8,128)(2,1)} %normalise.1), channel_id=1, source_target_pairs={{0,4},{1,5},{2,6},{3,7},{4,0},{5,1},{6,2},{7,3},{8,12},{9,13},{10,... | collective-permute-start | bytes 49160 | tf_op jit(solution)/shard_map/ppermute | solution.py:549
  60.7 3.9 %collective-permute-start.15 = (bf16[64,128]{1,0:T(8,128)(2,1)}, bf16[64,128]{1,0:T(8,128)(2,1)S(1)}, u32[]{:S(2)}, u32[]{:S(2)}) collective-permute-start(bf16[64,128]{1,0:T(8,128)(2,1)} %normalise.1), channel_id=1, source_target_pairs={{0,6},{1,7},{2,0},{3,1},{4,2},{5,3},{6,4},{7,5},{8,14},{9,15},{10,... | collective-permute-start | bytes 49160 | tf_op jit(solution)/shard_map/ppermute | solution.py:549
  60.8 14.4 %collective-permute-start.17 = (bf16[4,336,128]{2,1,0:T(8,128)(2,1)S(1)}, bf16[4,336,128]{2,1,0:T(8,128)(2,1)S(1)}, u32[]{:S(2)}, u32[]{:S(2)}) collective-permute-start(bf16[4,336,128]{2,1,0:T(8,128)(2,1)S(1)} %collective-permute-done.4), channel_id=1, source_target_pairs={{0,1},{1,0},{2,3},{3,2},{4,5},{5,4},{6,7},{7,6},{8,24},{9,25},{10,... | collective-permute-start | bytes 1032200 | tf_op jit(solution)/shard_map/ppermute | solution.py:549
  65.4 10.6 %copy-start.7 = (bf16[256,128]{1,0:T(8,128)(2,1)}, bf16[256,128]{1,0:T(8,128)(2,1)S(1)}, u32[]{:S(2)}) copy-start(bf16[256,128]{1,0:T(8,128)(2,1)S(1)} %pad_maximum_fusion.1.refs_7_.refs_5_) | copy-start | bytes 196612
  65.4 4.3 %collective-permute-start.16 = (bf16[256,128]{1,0:T(8,128)(2,1)S(1)}, bf16[256,128]{1,0:T(8,128)(2,1)S(1)}, u32[]{:S(2)}, u32[]{:S(2)}) collective-permute-start(bf16[256,128]{1,0:T(8,128)(2,1)S(1)} %pad_maximum_fusion.1.refs_7_.refs_5_), channel_id=1, source_target_pairs={{0,1},{1,0},{2,3},{3,2},{4,5},{5,4},{6,7},{7,6},{8,9},{9,8},{10,11... | collective-permute-start | bytes 196616 | tf_op jit(solution)/shard_map/ppermute | solution.py:549
  66.8 29.8 %collective-permute-start.22 = (bf16[12,336,128]{2,1,0:T(8,128)(2,1)}, bf16[12,336,128]{2,1,0:T(8,128)(2,1)}, u32[]{:S(2)}, u32[]{:S(2)}) collective-permute-start(bf16[12,336,128]{2,1,0:T(8,128)(2,1)} %collective-permute-done.21.refs_6_), channel_id=1, source_target_pairs={{0,8},{1,9},{2,10},{3,11},{4,12},{5,13},{6,14},{7,15},{8,0},{9,1},... | collective-permute-start | bytes 3096584 | tf_op jit(solution)/shard_map/ppermute | solution.py:549
  69.7 7.1 %copy-start.16 = (bf16[256,128]{1,0:T(8,128)(2,1)}, bf16[256,128]{1,0:T(8,128)(2,1)S(1)}, u32[]{:S(2)}) copy-start(bf16[256,128]{1,0:T(8,128)(2,1)S(1)} %collective-permute-done.16.refs_8_.refs_6_) | copy-start | bytes 196612
  69.7 23.0 %collective-permute-start.23 = (bf16[4,336,128]{2,1,0:T(8,128)(2,1)S(1)}, bf16[4,336,128]{2,1,0:T(8,128)(2,1)S(1)}, u32[]{:S(2)}, u32[]{:S(2)}) collective-permute-start(bf16[4,336,128]{2,1,0:T(8,128)(2,1)S(1)} %collective-permute-done.5), channel_id=1, source_target_pairs={{0,1},{1,0},{2,3},{3,2},{4,5},{5,4},{6,7},{7,6},{8,24},{9,25},{10,... | collective-permute-start | bytes 1032200 | tf_op jit(solution)/shard_map/ppermute | solution.py:549
  70.4 22.3 %collective-permute-start.24 = (bf16[4,336,128]{2,1,0:T(8,128)(2,1)S(1)}, bf16[4,336,128]{2,1,0:T(8,128)(2,1)S(1)}, u32[]{:S(2)}, u32[]{:S(2)}) collective-permute-start(bf16[4,336,128]{2,1,0:T(8,128)(2,1)S(1)} %collective-permute-done.12), channel_id=1, source_target_pairs={{0,1},{1,0},{2,3},{3,2},{4,5},{5,4},{6,7},{7,6},{8,24},{9,25},{10,... | collective-permute-start | bytes 1032200 | tf_op jit(solution)/shard_map/ppermute | solution.py:549
  71.7 21.0 %collective-permute-start.25 = (bf16[4,336,128]{2,1,0:T(8,128)(2,1)S(1)}, bf16[4,336,128]{2,1,0:T(8,128)(2,1)S(1)}, u32[]{:S(2)}, u32[]{:S(2)}) collective-permute-start(bf16[4,336,128]{2,1,0:T(8,128)(2,1)S(1)} %collective-permute-done.7), channel_id=1, source_target_pairs={{0,6},{1,7},{2,0},{3,1},{4,2},{5,3},{6,4},{7,5},{8,14},{9,15},{10,... | collective-permute-start | bytes 1032200 | tf_op jit(solution)/shard_map/ppermute | solution.py:549
  76.8 19.8 %collective-permute-start.18 = (bf16[20,336,128]{2,1,0:T(8,128)(2,1)}, bf16[20,336,128]{2,1,0:T(8,128)(2,1)}, u32[]{:S(2)}, u32[]{:S(2)}) collective-permute-start(bf16[20,336,128]{2,1,0:T(8,128)(2,1)} %constant_dynamic-update-slice_fusion.2.refs_4_), channel_id=1, source_target_pairs={{0,8},{1,9},{2,10},{3,11},{4,12},{5,13},{6,14},{7,15},{8,0},{9,1},... | collective-permute-start | bytes 5160968 | tf_op jit(solution)/shard_map/ppermute | solution.py:549
  92.8 3.7 %copy-start.6 = (bf16[12,336,128]{2,1,0:T(8,128)(2,1)}, bf16[12,336,128]{2,1,0:T(8,128)(2,1)S(1)}, u32[]{:S(2)}) copy-start(bf16[12,336,128]{2,1,0:T(8,128)(2,1)S(1)} %constant_dynamic-update-slice_fusion.9.refs_3_) | copy-start | bytes 3096580
  92.8 3.7 %collective-permute-start.26 = (bf16[12,336,128]{2,1,0:T(8,128)(2,1)S(1)}, bf16[12,336,128]{2,1,0:T(8,128)(2,1)S(1)}, u32[]{:S(2)}, u32[]{:S(2)}) collective-permute-start(bf16[12,336,128]{2,1,0:T(8,128)(2,1)S(1)} %constant_dynamic-update-slice_fusion.9.refs_3_), channel_id=1, source_target_pairs={{0,8},{1,9},{2,10},{3,11},{4,12},{5,13},{6,14},{7,15},{8,0},{9,1},... | collective-permute-start | bytes 3096584 | tf_op jit(solution)/shard_map/ppermute | solution.py:549
  93.8 2.8 %collective-permute-start.20 = (bf16[8,336,128]{2,1,0:T(8,128)(2,1)S(1)}, bf16[8,336,128]{2,1,0:T(8,128)(2,1)S(1)}, u32[]{:S(2)}, u32[]{:S(2)}) collective-permute-start(bf16[8,336,128]{2,1,0:T(8,128)(2,1)S(1)} %copy-done.4), channel_id=1, source_target_pairs={{0,8},{1,9},{2,10},{3,11},{4,12},{5,13},{6,14},{7,15},{8,0},{9,1},... | collective-permute-start | bytes 2064392 | tf_op jit(solution)/shard_map/ppermute | solution.py:549
  (12 other events, 20.5 us)

commit v4 on v3

--- a/solution.py
+++ b/solution.py
@@ -566,7 +566,7 @@
         near = jnp.concatenate([e0, l0])
         row = [mine, rest, near, swap(near)]
         e1, l1, z2, f0 = early(z1), late(z1), along_z(z1), late(e0)
-        back = back_z(jnp.concatenate([mine, near]))
+        z3 = back_z(lax.optimization_barrier((mine, z1))[0])
         weights, stats, partners = score(place, row, refs, steps, slots, classes)
         stats = [
             stats,
@@ -574,17 +574,19 @@
             send(stats, lambda x, c, z, y: (x + 1, c, z, y)),
             send(stats, lambda x, c, z, y: (x + 1, 1 - c, z, y)),
         ]
-        z2, e1, f0, *_ = lax.optimization_barrier((z2, e1, f0, *stats))
-        e2, f1 = early(z2), late(e1)
+        z2_late, e1_late, *_ = lax.optimization_barrier((z2, e1, *stats))
+        e2, f1 = early(z2_late), late(e1_late)
         weights = normalise(tuned, place, partners, weights, stats)
+        *held, weights = lax.optimization_barrier((z1, z2, z3, e1, l1, f0, weights))
         weights = [weights] + [send(weights, lambda x, c, z, y, dz=dz: (x, c, z + dz, y)) for dz in range(1, z_size)]
         weights = jnp.concatenate(weights)
+        first = jnp.concatenate(held)
+        first_back = swap(first)
+        z2_last, e2_last, near_last, f0_last, weights = lax.optimization_barrier((z2, e2, near, f0, weights))
+        l2, f2, back = late(z2_last), late(e2_last), back_z(jnp.concatenate([near_last, f0_last]))
         weights = [weights, send(weights, lambda x, c, z, y: (x, c, z, y + 1))]
-        z2, e2, f0, *weights = lax.optimization_barrier((z2, e2, f0, *weights))
-        l2, f2, f3 = late(z2), late(e2), back_z(f0)
-        first = jnp.concatenate([z1, z2, e1, l1, f0])
         second = jnp.concatenate([f1, e2])
-        parts = [[*row, first, second, back], [swap(first), swap(second), swap(back), l2, f2, f3]]
+        parts = [[*row, first, first_back, second], [swap(second), l2, f2, back]]
     else:
         row = lax.all_gather(mine, "cls", axis=0, tiled=True)
         parts = [[lax.all_gather(row, "dom", axis=0, tiled=True)]]
@@ -595,9 +597,8 @@
     held = None
     for k, part in enumerate(parts):
         if k:
-            *end, _ = lax.optimization_barrier((*part[3:], held[1]))
-            end = jnp.concatenate(end)
-            part = part[:3] + [end, swap(end)]
+            *end, _ = lax.optimization_barrier((*part[1:], held[1]))
+            part = part[:1] + end + [swap(block) for block in end]
         held = class_sum(
             place, part, weights, steps, held, k == len(parts) - 1, tuned, z_size, y_size, local, block_width, 2 * classes, slots * 2 * classes
         )

time: 117 us -> 117 us (level); the launches traced: 116 us -> 117 us
  waiting for transfers between devices: 25.7 us -> 29.7 us
  local copies, waits for them, and re-layouts: 17.1 us -> 13.8 us
    ppermute x27 -> x28, waiting for transfers between devices: 25.7 us -> 29.7 us  [send(): return lax.ppermute(value, ('cls', 'dom'), moves(goal))]
    unnamed x44 -> x51, local copies, waits for them, and re-layouts: 9.11 us -> 6.5 us
    ppermute x27 -> x28, starting transfers between devices: 22 us -> 22.8 us  [send(): return lax.ppermute(value, ('cls', 'dom'), moves(goal))]
  transfers between devices with their start and end apart: 27 -> 28, of which waited for: 8 -> 9; matrix products, arithmetic and copies ran while one was open for 12% -> 8% of each run, Pallas kernels for 23% -> 17%
where the time goes in v4:
time: 117 us
  Pallas kernels  48.7 us (42%)
  waiting for transfers between devices  29.7 us (25%)
  starting transfers between devices  22.8 us (19%)
  local copies, waits for them, and re-layouts  13.8 us (12%)
  other arithmetic  1.43 us (1%)
    pallas_call x2, Pallas kernels, class_sum(): pl.pallas_call(functools.partial(sum_kernel, weight_rows, relative, z_siz...  34.1 us
    ppermute x28, waiting for transfers between devices, send(): return lax.ppermute(value, ('cls', 'dom'), moves(goal))  29.7 us
    ppermute x28, starting transfers between devices, send(): return lax.ppermute(value, ('cls', 'dom'), moves(goal))  22.8 us
    pallas_call x1, Pallas kernels, score(): pl.pallas_call(functools.partial(score_kernel, count), out_shape=(jax.Sha...  9.03 us
    reshape x1, local copies, waits for them, and re-layouts, shards(): lax.optimization_barrier((references, mine))[0]  7.11 us
    unnamed x51, local copies, waits for them, and re-layouts  6.5 us
    pallas_call x1, Pallas kernels, prepare(): pl.pallas_call(functools.partial(prep_kernel, local), out_shape=(shape, s...  4.08 us
  transfers between devices with their start and end apart: 28, of which 9 were waited for; matrix products, arithmetic and copies ran while one was open for 8% of the time, Pallas kernels for 17%

profile of v4, /device:TPU:0, one launch (start us, length us, event | category | flops | bytes accessed | tf_op | source)
XLA Modules:
  0.0 116.8 jit_solution(3448961557442839984)
XLA Ops:
  0.0 1.0 copy.10
  1.5 0.8 copy.7
  2.3 0.8 pad_add_fusion.near_ref
  3.1 0.6 pad_add_fusion.1.place_ref
  4.8 0.7 copy-done.3
  5.5 4.1 %prepare.1 = (bf16[4,336,128]{2,1,0:T(8,128)(2,1)}, bf16[4,336,128]{2,1,0:T(8,128)(2,1)}) custom-call(s32[2]{0:T(128)} %pad_add_fusion.1.place_ref, s32[4,10]{1,0:T(4,128)} %copy-done.11, s32[4,10]{1,0:T(4,128)} %copy-done.12, bf16[4,288,128]{2,1,0:T(8,128)(2,1)} %bitcast.7, bf16[4,288,128]{2,1,0:T(8,128)(2,1)} %copy-done.3, ...), custom_call_target="tpu_custom_call" | custom-call | tf_op jit(solution)/shard_map/prepare/pallas_call | solution.py:133
  9.6 2.7 %collective-permute-start.2 = (bf16[4,336,128]{2,1,0:T(8,128)(2,1)}, bf16[4,336,128]{2,1,0:T(8,128)(2,1)S(1)}, u32[]{:S(2)}, u32[]{:S(2)}) collective-permute-start(bf16[4,336,128]{2,1,0:T(8,128)(2,1)} %get-tuple-element.45.refs_0_), channel_id=1, source_target_pairs={{0,16},{1,17},{2,18},{3,19},{4,20},{5,21},{6,22},{7,23},{8,9},{9,8... | collective-permute-start | bytes 1032200 | tf_op jit(solution)/shard_map/ppermute | solution.py:549
  12.2 1.5 %collective-permute-start.3 = (bf16[4,336,128]{2,1,0:T(8,128)(2,1)}, bf16[4,336,128]{2,1,0:T(8,128)(2,1)S(1)}, u32[]{:S(2)}, u32[]{:S(2)}) collective-permute-start(bf16[4,336,128]{2,1,0:T(8,128)(2,1)} %get-tuple-element.45.refs_0_), channel_id=1, source_target_pairs={{0,1},{1,0},{2,3},{3,2},{4,5},{5,4},{6,7},{7,6},{8,24},{9,25},{10,... | collective-permute-start | bytes 1032200 | tf_op jit(solution)/shard_map/ppermute | solution.py:549
  13.8 1.6 %collective-permute-start.4 = (bf16[4,336,128]{2,1,0:T(8,128)(2,1)}, bf16[4,336,128]{2,1,0:T(8,128)(2,1)S(1)}, u32[]{:S(2)}, u32[]{:S(2)}) collective-permute-start(bf16[4,336,128]{2,1,0:T(8,128)(2,1)} %get-tuple-element.45.refs_0_), channel_id=1, source_target_pairs={{0,2},{1,3},{2,4},{3,5},{4,6},{5,7},{6,0},{7,1},{8,10},{9,11},{10,... | collective-permute-start | bytes 1032200 | tf_op jit(solution)/shard_map/ppermute | solution.py:549
  15.3 7.1 %reshape.7.refs_4_ = bf16[50,36,1024]{2,1,0:T(8,128)(2,1)} reshape(bf16[50,36864]{1,0:T(8,128)(2,1)} %param.7) | data formatting | bytes 7372800 | tf_op jit(solution)/shard_map/reshape | solution.py:560
  22.5 3.2 %collective-permute-done.4 = bf16[4,336,128]{2,1,0:T(8,128)(2,1)S(1)} collective-permute-done((bf16[4,336,128]{2,1,0:T(8,128)(2,1)}, bf16[4,336,128]{2,1,0:T(8,128)(2,1)S(1)}, u32[]{:S(2)}, u32[]{:S(2)}) %collective-permute-start.4) | collective-permute-done | bytes 344096 | tf_op jit(solution)/shard_map/ppermute | solution.py:549
  25.8 2.1 %collective-permute-done.7.refs_3_ = bf16[8,336,128]{2,1,0:T(8,128)(2,1)S(1)} collective-permute-done((bf16[8,336,128]{2,1,0:T(8,128)(2,1)S(1)}, bf16[8,336,128]{2,1,0:T(8,128)(2,1)S(1)}, u32[]{:S(2)}, u32[]{:S(2)}) %collective-permute-start.7) | collective-permute-done | bytes 688160 | tf_op jit(solution)/shard_map/ppermute | solution.py:549
  27.9 0.9 copy-done.14
  28.8 9.0 %score.1 = (f32[8,8,128]{2,1,0:T(8,128)}, f32[16,128]{1,0:T(8,128)}, s32[8,3]{1,0:T(8,128)}) custom-call(s32[2]{0:T(128)} %pad_add_fusion.1.place_ref, bf16[4,336,128]{2,1,0:T(8,128)(2,1)} %get-tuple-element.45.refs_0_, bf16[4,336,128]{2,1,0:T(8,128)(2,1)} %get-tuple-element.38.refs_1_, bf16[8,336,128]{2,1,0:T(8,128)(2,1)} %copy-done, ...), custom_call_target="tpu_custom_call" | custom-call | flops 10000000000 | bytes 10000000 | tf_op jit(solution)/shard_map/score/pallas_call | solution.py:284
  38.6 1.5 %collective-permute-start.9 = (f32[16,128]{1,0:T(8,128)}, f32[16,128]{1,0:T(8,128)S(1)}, u32[]{:S(2)}, u32[]{:S(2)}) collective-permute-start(f32[16,128]{1,0:T(8,128)} %get-tuple-element.42.refs_0_), channel_id=1, source_target_pairs={{0,16},{1,17},{2,18},{3,19},{4,20},{5,21},{6,22},{7,23},{8,24},{9,... | collective-permute-start | bytes 24584 | tf_op jit(solution)/shard_map/ppermute | solution.py:549
  40.6 0.6 collective-permute-done.10.refs_3_
  41.2 3.2 %collective-permute-start.15 = (bf16[4,336,128]{2,1,0:T(8,128)(2,1)}, bf16[4,336,128]{2,1,0:T(8,128)(2,1)S(1)}, u32[]{:S(2)}, u32[]{:S(2)}) collective-permute-start(bf16[4,336,128]{2,1,0:T(8,128)(2,1)} %get-tuple-element.45.refs_0_), channel_id=1, source_target_pairs={{0,6},{1,7},{2,0},{3,1},{4,2},{5,3},{6,4},{7,5},{8,14},{9,15},{10,... | collective-permute-start | bytes 1032200 | tf_op jit(solution)/shard_map/ppermute | solution.py:549
  44.9 1.5 %collective-permute-start.14 = (bf16[4,336,128]{2,1,0:T(8,128)(2,1)S(1)}, bf16[4,336,128]{2,1,0:T(8,128)(2,1)S(1)}, u32[]{:S(2)}, u32[]{:S(2)}) collective-permute-start(bf16[4,336,128]{2,1,0:T(8,128)(2,1)S(1)} %collective-permute-done.2), channel_id=1, source_target_pairs={{0,1},{1,0},{2,3},{3,2},{4,5},{5,4},{6,7},{7,6},{8,24},{9,25},{10,... | collective-permute-start | bytes 1032200 | tf_op jit(solution)/shard_map/ppermute | solution.py:549
  46.5 1.5 %normalise.1 = bf16[64,128]{1,0:T(8,128)(2,1)} custom-call(s32[2]{0:T(128)} %pad_add_fusion.1.place_ref, s32[8,3]{1,0:T(8,128)} %get-tuple-element.46.partner_ref, f32[8,8,128]{2,1,0:T(8,128)} %get-tuple-element.47.weight_ref, f32[16,128]{1,0:T(8,128)} %get-tuple-element.42.refs_0_, f32[16,128]{1,0:T(8,128)} %copy-done.9, f32[16,128]{1,0:T(8,128)} %copy-done.10, ...), custom_call_target="tpu_custom_call" | custom-call | tf_op jit(solution)/shard_map/normalise/pallas_call | solution.py:337
  48.0 10.9 %collective-permute-done.15 = bf16[4,336,128]{2,1,0:T(8,128)(2,1)S(1)} collective-permute-done((bf16[4,336,128]{2,1,0:T(8,128)(2,1)}, bf16[4,336,128]{2,1,0:T(8,128)(2,1)S(1)}, u32[]{:S(2)}, u32[]{:S(2)}) %collective-permute-start.15) | collective-permute-done | bytes 344096 | tf_op jit(solution)/shard_map/ppermute | solution.py:549
  59.3 0.6 collective-permute-start.12
  60.4 0.7 collective-permute-start.17
  61.4 4.5 %collective-permute-done.17 = bf16[64,128]{1,0:T(8,128)(2,1)S(1)} collective-permute-done((bf16[64,128]{1,0:T(8,128)(2,1)S(1)}, bf16[64,128]{1,0:T(8,128)(2,1)S(1)}, u32[]{:S(2)}, u32[]{:S(2)}) %collective-permute-start.17) | collective-permute-done | bytes 16416 | tf_op jit(solution)/shard_map/ppermute | solution.py:549
  66.0 3.7 %collective-permute-done.19 = bf16[64,128]{1,0:T(8,128)(2,1)S(1)} collective-permute-done((bf16[64,128]{1,0:T(8,128)(2,1)S(1)}, bf16[64,128]{1,0:T(8,128)(2,1)S(1)}, u32[]{:S(2)}, u32[]{:S(2)}) %collective-permute-start.19) | collective-permute-done | bytes 16416 | tf_op jit(solution)/shard_map/ppermute | solution.py:549
  70.0 1.3 %collective-permute-start.24 = (bf16[256,128]{1,0:T(8,128)(2,1)S(1)}, bf16[256,128]{1,0:T(8,128)(2,1)S(1)}, u32[]{:S(2)}, u32[]{:S(2)}) collective-permute-start(bf16[256,128]{1,0:T(8,128)(2,1)S(1)} %pad_maximum_fusion.1.refs_7_), channel_id=1, source_target_pairs={{0,1},{1,0},{2,3},{3,2},{4,5},{5,4},{6,7},{7,6},{8,9},{9,8},{10,11... | collective-permute-start | bytes 196616 | tf_op jit(solution)/shard_map/ppermute | solution.py:549
  71.4 1.9 %collective-permute-start.22 = (bf16[12,336,128]{2,1,0:T(8,128)(2,1)S(1)}, bf16[12,336,128]{2,1,0:T(8,128)(2,1)}, u32[]{:S(2)}, u32[]{:S(2)}) collective-permute-start(bf16[12,336,128]{2,1,0:T(8,128)(2,1)S(1)} %pad_maximum_fusion), channel_id=1, source_target_pairs={{0,6},{1,7},{2,0},{3,1},{4,2},{5,3},{6,4},{7,5},{8,14},{9,15},{10,... | collective-permute-start | bytes 3096584 | tf_op jit(solution)/shard_map/ppermute | solution.py:549
  73.8 1.5 %collective-permute-start.21 = (bf16[4,336,128]{2,1,0:T(8,128)(2,1)S(1)}, bf16[4,336,128]{2,1,0:T(8,128)(2,1)S(1)}, u32[]{:S(2)}, u32[]{:S(2)}) collective-permute-start(bf16[4,336,128]{2,1,0:T(8,128)(2,1)S(1)} %collective-permute-done.12), channel_id=1, source_target_pairs={{0,1},{1,0},{2,3},{3,2},{4,5},{5,4},{6,7},{7,6},{8,24},{9,25},{10,... | collective-permute-start | bytes 1032200 | tf_op jit(solution)/shard_map/ppermute | solution.py:549
  75.4 0.8 copy-done.4
  76.2 17.7 %class_sum.2 = (f32[16000,128]{1,0:T(8,128)}, f32[56,128]{1,0:T(8,128)}) custom-call(s32[2]{0:T(128)} %pad_add_fusion.1.place_ref, bf16[4,336,128]{2,1,0:T(8,128)(2,1)} %get-tuple-element.45.refs_0_, bf16[4,336,128]{2,1,0:T(8,128)(2,1)} %get-tuple-element.38.refs_1_, bf16[8,336,128]{2,1,0:T(8,128)(2,1)} %copy-done, bf16[8,336,128]{2,1,0:T(8,128)(2,1)} %copy-done.14, ...), custom_call_target="tpu_custom_call" | custom-call | flops 16000000000 | bytes 10000000 | tf_op jit(solution)/shard_map/class_sum/pallas_call | solution.py:511
  95.1 3.8 %collective-permute-done.13.refs_0_ = bf16[8,336,128]{2,1,0:T(8,128)(2,1)S(1)} collective-permute-done((bf16[8,336,128]{2,1,0:T(8,128)(2,1)}, bf16[8,336,128]{2,1,0:T(8,128)(2,1)S(1)}, u32[]{:S(2)}, u32[]{:S(2)}) %collective-permute-start.13) | collective-permute-done | bytes 688160 | tf_op jit(solution)/shard_map/ppermute | solution.py:549
  99.0 0.8 copy-done.15
  100.4 16.3 %class_sum.3 = bf16[50,36864]{1,0:T(8,128)(2,1)} custom-call(s32[2]{0:T(128)} %pad_add_fusion.1.place_ref, bf16[8,336,128]{2,1,0:T(8,128)(2,1)} %copy-done.15, bf16[4,336,128]{2,1,0:T(8,128)(2,1)} %copy-done.16, bf16[4,336,128]{2,1,0:T(8,128)(2,1)} %copy-done.17, bf16[12,336,128]{2,1,0:T(8,128)(2,1)} %collective-permute-done.22.refs_3_, ...), custom_call_target="tpu_custom_call" | custom-call | flops 9600000000 | bytes 10000000 | tf_op jit(solution)/shard_map/class_sum/pallas_call | solution.py:511
  (88 shorter events, 7.5 us)
Async XLA Ops:
  1.0 3.2 %collective-permute-start.1 = (bf16[4,288,128]{2,1,0:T(8,128)(2,1)S(1)}, bf16[4,288,128]{2,1,0:T(8,128)(2,1)S(1)}, u32[]{:S(2)}, u32[]{:S(2)}) collective-permute-start(bf16[4,288,128]{2,1,0:T(8,128)(2,1)S(1)} %bitcast.6), channel_id=1, source_target_pairs={{0,8},{1,9},{2,10},{3,11},{4,12},{5,13},{6,14},{7,15},{8,0},{9,1},... | collective-permute-start | bytes 884744 | tf_op jit(solution)/shard_map/ppermute | solution.py:549
  3.1 1.2 collective-permute-start
  9.6 12.9 %collective-permute-start.2 = (bf16[4,336,128]{2,1,0:T(8,128)(2,1)}, bf16[4,336,128]{2,1,0:T(8,128)(2,1)S(1)}, u32[]{:S(2)}, u32[]{:S(2)}) collective-permute-start(bf16[4,336,128]{2,1,0:T(8,128)(2,1)} %get-tuple-element.45.refs_0_), channel_id=1, source_target_pairs={{0,16},{1,17},{2,18},{3,19},{4,20},{5,21},{6,22},{7,23},{8,9},{9,8... | collective-permute-start | bytes 1032200 | tf_op jit(solution)/shard_map/ppermute | solution.py:549
  12.2 10.2 %collective-permute-start.3 = (bf16[4,336,128]{2,1,0:T(8,128)(2,1)}, bf16[4,336,128]{2,1,0:T(8,128)(2,1)S(1)}, u32[]{:S(2)}, u32[]{:S(2)}) collective-permute-start(bf16[4,336,128]{2,1,0:T(8,128)(2,1)} %get-tuple-element.45.refs_0_), channel_id=1, source_target_pairs={{0,1},{1,0},{2,3},{3,2},{4,5},{5,4},{6,7},{7,6},{8,24},{9,25},{10,... | collective-permute-start | bytes 1032200 | tf_op jit(solution)/shard_map/ppermute | solution.py:549
  13.8 11.8 %collective-permute-start.4 = (bf16[4,336,128]{2,1,0:T(8,128)(2,1)}, bf16[4,336,128]{2,1,0:T(8,128)(2,1)S(1)}, u32[]{:S(2)}, u32[]{:S(2)}) collective-permute-start(bf16[4,336,128]{2,1,0:T(8,128)(2,1)} %get-tuple-element.45.refs_0_), channel_id=1, source_target_pairs={{0,2},{1,3},{2,4},{3,5},{4,6},{5,7},{6,0},{7,1},{8,10},{9,11},{10,... | collective-permute-start | bytes 1032200 | tf_op jit(solution)/shard_map/ppermute | solution.py:549
  25.7 2.2 %collective-permute-start.7 = (bf16[8,336,128]{2,1,0:T(8,128)(2,1)S(1)}, bf16[8,336,128]{2,1,0:T(8,128)(2,1)S(1)}, u32[]{:S(2)}, u32[]{:S(2)}) collective-permute-start(bf16[8,336,128]{2,1,0:T(8,128)(2,1)S(1)} %constant_dynamic-update-slice_fusion.refs_2_), channel_id=1, source_target_pairs={{0,8},{1,9},{2,10},{3,11},{4,12},{5,13},{6,14},{7,15},{8,0},{9,1},... | collective-permute-start | bytes 2064392 | tf_op jit(solution)/shard_map/ppermute | solution.py:549
  37.9 3.4 %collective-permute-start.10 = (f32[16,128]{1,0:T(8,128)}, f32[16,128]{1,0:T(8,128)S(1)}, u32[]{:S(2)}, u32[]{:S(2)}) collective-permute-start(f32[16,128]{1,0:T(8,128)} %get-tuple-element.42.refs_0_), channel_id=1, source_target_pairs={{0,24},{1,25},{2,26},{3,27},{4,28},{5,29},{6,30},{7,31},{8,16},{9,... | collective-permute-start | bytes 24584 | tf_op jit(solution)/shard_map/ppermute | solution.py:549
  38.2 6.2 %collective-permute-start.8 = (f32[16,128]{1,0:T(8,128)}, f32[16,128]{1,0:T(8,128)S(1)}, u32[]{:S(2)}, u32[]{:S(2)}) collective-permute-start(f32[16,128]{1,0:T(8,128)} %get-tuple-element.42.refs_0_), channel_id=1, source_target_pairs={{0,8},{1,9},{2,10},{3,11},{4,12},{5,13},{6,14},{7,15},{8,0},{9,1},... | collective-permute-start | bytes 24584 | tf_op jit(solution)/shard_map/ppermute | solution.py:549
  38.6 6.4 %collective-permute-start.9 = (f32[16,128]{1,0:T(8,128)}, f32[16,128]{1,0:T(8,128)S(1)}, u32[]{:S(2)}, u32[]{:S(2)}) collective-permute-start(f32[16,128]{1,0:T(8,128)} %get-tuple-element.42.refs_0_), channel_id=1, source_target_pairs={{0,16},{1,17},{2,18},{3,19},{4,20},{5,21},{6,22},{7,23},{8,24},{9,... | collective-permute-start | bytes 24584 | tf_op jit(solution)/shard_map/ppermute | solution.py:549
  40.1 18.9 %collective-permute-start.5 = (bf16[4,336,128]{2,1,0:T(8,128)(2,1)S(1)}, bf16[4,336,128]{2,1,0:T(8,128)(2,1)S(1)}, u32[]{:S(2)}, u32[]{:S(2)}) collective-permute-start(bf16[4,336,128]{2,1,0:T(8,128)(2,1)S(1)} %collective-permute-done.4), channel_id=1, source_target_pairs={{0,2},{1,3},{2,4},{3,5},{4,6},{5,7},{6,0},{7,1},{8,10},{9,11},{10,... | collective-permute-start | bytes 1032200 | tf_op jit(solution)/shard_map/ppermute | solution.py:549
  40.1 18.9 %collective-permute-start.6 = (bf16[4,336,128]{2,1,0:T(8,128)(2,1)S(1)}, bf16[4,336,128]{2,1,0:T(8,128)(2,1)S(1)}, u32[]{:S(2)}, u32[]{:S(2)}) collective-permute-start(bf16[4,336,128]{2,1,0:T(8,128)(2,1)S(1)} %collective-permute-done.4), channel_id=1, source_target_pairs={{0,16},{1,17},{2,18},{3,19},{4,20},{5,21},{6,22},{7,23},{8,9},{9,8... | collective-permute-start | bytes 1032200 | tf_op jit(solution)/shard_map/ppermute | solution.py:549
  41.2 17.7 %collective-permute-start.15 = (bf16[4,336,128]{2,1,0:T(8,128)(2,1)}, bf16[4,336,128]{2,1,0:T(8,128)(2,1)S(1)}, u32[]{:S(2)}, u32[]{:S(2)}) collective-permute-start(bf16[4,336,128]{2,1,0:T(8,128)(2,1)} %get-tuple-element.45.refs_0_), channel_id=1, source_target_pairs={{0,6},{1,7},{2,0},{3,1},{4,2},{5,3},{6,4},{7,5},{8,14},{9,15},{10,... | collective-permute-start | bytes 1032200 | tf_op jit(solution)/shard_map/ppermute | solution.py:549
  44.4 14.5 %collective-permute-start.16 = (bf16[4,336,128]{2,1,0:T(8,128)(2,1)S(1)}, bf16[4,336,128]{2,1,0:T(8,128)(2,1)S(1)}, u32[]{:S(2)}, u32[]{:S(2)}) collective-permute-start(bf16[4,336,128]{2,1,0:T(8,128)(2,1)S(1)} %collective-permute-done.4), channel_id=1, source_target_pairs={{0,1},{1,0},{2,3},{3,2},{4,5},{5,4},{6,7},{7,6},{8,24},{9,25},{10,... | collective-permute-start | bytes 1032200 | tf_op jit(solution)/shard_map/ppermute | solution.py:549
  44.9 14.0 %collective-permute-start.14 = (bf16[4,336,128]{2,1,0:T(8,128)(2,1)S(1)}, bf16[4,336,128]{2,1,0:T(8,128)(2,1)S(1)}, u32[]{:S(2)}, u32[]{:S(2)}) collective-permute-start(bf16[4,336,128]{2,1,0:T(8,128)(2,1)S(1)} %collective-permute-done.2), channel_id=1, source_target_pairs={{0,1},{1,0},{2,3},{3,2},{4,5},{5,4},{6,7},{7,6},{8,24},{9,25},{10,... | collective-permute-start | bytes 1032200 | tf_op jit(solution)/shard_map/ppermute | solution.py:549
  48.0 12.4 %copy-start.6 = (bf16[64,128]{1,0:T(8,128)(2,1)S(1)}, bf16[64,128]{1,0:T(8,128)(2,1)}, u32[]{:S(2)}) copy-start(bf16[64,128]{1,0:T(8,128)(2,1)} %normalise.1) | copy-start | bytes 49156
  48.0 23.3 %copy-start.1 = (bf16[8,336,128]{2,1,0:T(8,128)(2,1)S(1)}, bf16[8,336,128]{2,1,0:T(8,128)(2,1)}, u32[]{:S(2)}) copy-start(bf16[8,336,128]{2,1,0:T(8,128)(2,1)} %copy-done) | copy-start | bytes 2064388
  59.2 16.2 %copy-start.7 = (bf16[24,336,128]{2,1,0:T(8,128)(2,1)}, bf16[24,336,128]{2,1,0:T(8,128)(2,1)S(1)}, u32[]{:S(2)}) copy-start(bf16[24,336,128]{2,1,0:T(8,128)(2,1)S(1)} %constant_dynamic-update-slice_fusion.4.refs_4_) | copy-start | bytes 6193156
  59.3 16.2 %collective-permute-start.23 = (bf16[24,336,128]{2,1,0:T(8,128)(2,1)S(1)}, bf16[24,336,128]{2,1,0:T(8,128)(2,1)}, u32[]{:S(2)}, u32[]{:S(2)}) collective-permute-start(bf16[24,336,128]{2,1,0:T(8,128)(2,1)S(1)} %constant_dynamic-update-slice_fusion.4.refs_4_), channel_id=1, source_target_pairs={{0,8},{1,9},{2,10},{3,11},{4,12},{5,13},{6,14},{7,15},{8,0},{9,1},... | collective-permute-start | bytes 6193160 | tf_op jit(solution)/shard_map/ppermute | solution.py:549
  59.3 10.7 %collective-permute-start.12 = (bf16[4,336,128]{2,1,0:T(8,128)(2,1)S(1)}, bf16[4,336,128]{2,1,0:T(8,128)(2,1)S(1)}, u32[]{:S(2)}, u32[]{:S(2)}) collective-permute-start(bf16[4,336,128]{2,1,0:T(8,128)(2,1)S(1)} %collective-permute-done.5), channel_id=1, source_target_pairs={{0,16},{1,17},{2,18},{3,19},{4,20},{5,21},{6,22},{7,23},{8,9},{9,8... | collective-permute-start | bytes 1032200 | tf_op jit(solution)/shard_map/ppermute | solution.py:549
  59.9 13.9 %collective-permute-start.11 = (bf16[4,336,128]{2,1,0:T(8,128)(2,1)S(1)}, bf16[4,336,128]{2,1,0:T(8,128)(2,1)S(1)}, u32[]{:S(2)}, u32[]{:S(2)}) collective-permute-start(bf16[4,336,128]{2,1,0:T(8,128)(2,1)S(1)} %collective-permute-done.6), channel_id=1, source_target_pairs={{0,1},{1,0},{2,3},{3,2},{4,5},{5,4},{6,7},{7,6},{8,24},{9,25},{10,... | collective-permute-start | bytes 1032200 | tf_op jit(solution)/shard_map/ppermute | solution.py:549
  60.4 5.5 %collective-permute-start.17 = (bf16[64,128]{1,0:T(8,128)(2,1)S(1)}, bf16[64,128]{1,0:T(8,128)(2,1)S(1)}, u32[]{:S(2)}, u32[]{:S(2)}) collective-permute-start(bf16[64,128]{1,0:T(8,128)(2,1)S(1)} %copy-done.6), channel_id=1, source_target_pairs={{0,2},{1,3},{2,4},{3,5},{4,6},{5,7},{6,0},{7,1},{8,10},{9,11},{10,... | collective-permute-start | bytes 49160 | tf_op jit(solution)/shard_map/ppermute | solution.py:549
  61.2 4.8 %collective-permute-start.18 = (bf16[64,128]{1,0:T(8,128)(2,1)S(1)}, bf16[64,128]{1,0:T(8,128)(2,1)S(1)}, u32[]{:S(2)}, u32[]{:S(2)}) collective-permute-start(bf16[64,128]{1,0:T(8,128)(2,1)S(1)} %copy-done.6), channel_id=1, source_target_pairs={{0,4},{1,5},{2,6},{3,7},{4,0},{5,1},{6,2},{7,3},{8,12},{9,13},{10,... | collective-permute-start | bytes 49160 | tf_op jit(solution)/shard_map/ppermute | solution.py:549
  66.0 3.7 %collective-permute-start.19 = (bf16[64,128]{1,0:T(8,128)(2,1)S(1)}, bf16[64,128]{1,0:T(8,128)(2,1)S(1)}, u32[]{:S(2)}, u32[]{:S(2)}) collective-permute-start(bf16[64,128]{1,0:T(8,128)(2,1)S(1)} %copy-done.6), channel_id=1, source_target_pairs={{0,6},{1,7},{2,0},{3,1},{4,2},{5,3},{6,4},{7,5},{8,14},{9,15},{10,... | collective-permute-start | bytes 49160 | tf_op jit(solution)/shard_map/ppermute | solution.py:549
  69.7 5.7 %copy-start.5 = (bf16[256,128]{1,0:T(8,128)(2,1)}, bf16[256,128]{1,0:T(8,128)(2,1)S(1)}, u32[]{:S(2)}) copy-start(bf16[256,128]{1,0:T(8,128)(2,1)S(1)} %pad_maximum_fusion.1.refs_7_) | copy-start | bytes 196612
  70.0 5.4 %collective-permute-start.24 = (bf16[256,128]{1,0:T(8,128)(2,1)S(1)}, bf16[256,128]{1,0:T(8,128)(2,1)S(1)}, u32[]{:S(2)}, u32[]{:S(2)}) collective-permute-start(bf16[256,128]{1,0:T(8,128)(2,1)S(1)} %pad_maximum_fusion.1.refs_7_), channel_id=1, source_target_pairs={{0,1},{1,0},{2,3},{3,2},{4,5},{5,4},{6,7},{7,6},{8,9},{9,8},{10,11... | collective-permute-start | bytes 196616 | tf_op jit(solution)/shard_map/ppermute | solution.py:549
  71.4 22.6 %collective-permute-start.22 = (bf16[12,336,128]{2,1,0:T(8,128)(2,1)S(1)}, bf16[12,336,128]{2,1,0:T(8,128)(2,1)}, u32[]{:S(2)}, u32[]{:S(2)}) collective-permute-start(bf16[12,336,128]{2,1,0:T(8,128)(2,1)S(1)} %pad_maximum_fusion), channel_id=1, source_target_pairs={{0,6},{1,7},{2,0},{3,1},{4,2},{5,3},{6,4},{7,5},{8,14},{9,15},{10,... | collective-permute-start | bytes 3096584 | tf_op jit(solution)/shard_map/ppermute | solution.py:549
  73.3 20.7 %collective-permute-start.20 = (bf16[4,336,128]{2,1,0:T(8,128)(2,1)S(1)}, bf16[4,336,128]{2,1,0:T(8,128)(2,1)S(1)}, u32[]{:S(2)}, u32[]{:S(2)}) collective-permute-start(bf16[4,336,128]{2,1,0:T(8,128)(2,1)S(1)} %collective-permute-done.5), channel_id=1, source_target_pairs={{0,1},{1,0},{2,3},{3,2},{4,5},{5,4},{6,7},{7,6},{8,24},{9,25},{10,... | collective-permute-start | bytes 1032200 | tf_op jit(solution)/shard_map/ppermute | solution.py:549
  73.8 20.2 %collective-permute-start.21 = (bf16[4,336,128]{2,1,0:T(8,128)(2,1)S(1)}, bf16[4,336,128]{2,1,0:T(8,128)(2,1)S(1)}, u32[]{:S(2)}, u32[]{:S(2)}) collective-permute-start(bf16[4,336,128]{2,1,0:T(8,128)(2,1)S(1)} %collective-permute-done.12), channel_id=1, source_target_pairs={{0,1},{1,0},{2,3},{3,2},{4,5},{5,4},{6,7},{7,6},{8,24},{9,25},{10,... | collective-permute-start | bytes 1032200 | tf_op jit(solution)/shard_map/ppermute | solution.py:549
  94.0 4.9 %collective-permute-start.27 = (bf16[12,336,128]{2,1,0:T(8,128)(2,1)}, bf16[12,336,128]{2,1,0:T(8,128)(2,1)S(1)}, u32[]{:S(2)}, u32[]{:S(2)}) collective-permute-start(bf16[12,336,128]{2,1,0:T(8,128)(2,1)} %collective-permute-done.22.refs_3_), channel_id=1, source_target_pairs={{0,8},{1,9},{2,10},{3,11},{4,12},{5,13},{6,14},{7,15},{8,0},{9,1},... | collective-permute-start | bytes 3096584 | tf_op jit(solution)/shard_map/ppermute | solution.py:549
  94.1 4.8 %collective-permute-start.13 = (bf16[8,336,128]{2,1,0:T(8,128)(2,1)}, bf16[8,336,128]{2,1,0:T(8,128)(2,1)S(1)}, u32[]{:S(2)}, u32[]{:S(2)}) collective-permute-start(bf16[8,336,128]{2,1,0:T(8,128)(2,1)} %copy-done.4), channel_id=1, source_target_pairs={{0,8},{1,9},{2,10},{3,11},{4,12},{5,13},{6,14},{7,15},{8,0},{9,1},... | collective-permute-start | bytes 2064392 | tf_op jit(solution)/shard_map/ppermute | solution.py:549
  94.6 4.3 %collective-permute-start.25 = (bf16[4,336,128]{2,1,0:T(8,128)(2,1)S(1)}, bf16[4,336,128]{2,1,0:T(8,128)(2,1)S(1)}, u32[]{:S(2)}, u32[]{:S(2)}) collective-permute-start(bf16[4,336,128]{2,1,0:T(8,128)(2,1)S(1)} %collective-permute-done.20.refs_1_), channel_id=1, source_target_pairs={{0,8},{1,9},{2,10},{3,11},{4,12},{5,13},{6,14},{7,15},{8,0},{9,1},... | collective-permute-start | bytes 1032200 | tf_op jit(solution)/shard_map/ppermute | solution.py:549
  94.7 4.2 %collective-permute-start.26 = (bf16[4,336,128]{2,1,0:T(8,128)(2,1)S(1)}, bf16[4,336,128]{2,1,0:T(8,128)(2,1)S(1)}, u32[]{:S(2)}, u32[]{:S(2)}) collective-permute-start(bf16[4,336,128]{2,1,0:T(8,128)(2,1)S(1)} %collective-permute-done.21.refs_2_), channel_id=1, source_target_pairs={{0,8},{1,9},{2,10},{3,11},{4,12},{5,13},{6,14},{7,15},{8,0},{9,1},... | collective-permute-start | bytes 1032200 | tf_op jit(solution)/shard_map/ppermute | solution.py:549
  (17 other events, 33.7 us)

commit v5 on v4

--- a/solution.py
+++ b/solution.py
@@ -568,6 +568,7 @@
         e1, l1, z2, f0 = early(z1), late(z1), along_z(z1), late(e0)
         z3 = back_z(lax.optimization_barrier((mine, z1))[0])
         weights, stats, partners = score(place, row, refs, steps, slots, classes)
+        stats, z2, z3, e1, l1, f0 = lax.optimization_barrier((stats, z2, z3, e1, l1, f0))
         stats = [
             stats,
             swap(stats),

time: 117 us -> 111 us (0.949)
  waiting for transfers between devices: 29.7 us -> 21.3 us
  starting transfers between devices: 22.8 us -> 24.3 us
    ppermute x28, waiting for transfers between devices: 29.7 us -> 21.3 us  [send(): return lax.ppermute(value, ('cls', 'dom'), moves(goal))]
    ppermute x28, starting transfers between devices: 22.8 us -> 24.3 us  [send(): return lax.ppermute(value, ('cls', 'dom'), moves(goal))]
    unnamed x51 -> x53, local copies, waits for them, and re-layouts: 6.5 us -> 7.08 us
  transfers between devices with their start and end apart: 28 -> 28, of which waited for: 9 -> 7; matrix products, arithmetic and copies ran while one was open for 8% -> 9% of each run, Pallas kernels for 17% -> 25%
where the time goes in v5:
time: 111 us; the launch traced here: 110 us
  Pallas kernels  48.3 us (44%)
  starting transfers between devices  24.3 us (22%)
  waiting for transfers between devices  21.3 us (19%)
  local copies, waits for them, and re-layouts  14.3 us (13%)
  other arithmetic  1.45 us (1%)
    pallas_call x2, Pallas kernels, class_sum(): pl.pallas_call(functools.partial(sum_kernel, weight_rows, relative, z_siz...  33.7 us
    ppermute x28, starting transfers between devices, send(): return lax.ppermute(value, ('cls', 'dom'), moves(goal))  24.3 us
    ppermute x28, waiting for transfers between devices, send(): return lax.ppermute(value, ('cls', 'dom'), moves(goal))  21.3 us
    pallas_call x1, Pallas kernels, score(): pl.pallas_call(functools.partial(score_kernel, count), out_shape=(jax.Sha...  9.03 us
    reshape x1, local copies, waits for them, and re-layouts, shards(): lax.optimization_barrier((references, mine))[0]  7.11 us
    unnamed x53, local copies, waits for them, and re-layouts  7.08 us
    pallas_call x1, Pallas kernels, prepare(): pl.pallas_call(functools.partial(prep_kernel, local), out_shape=(shape, s...  4.09 us
  transfers between devices with their start and end apart: 28, of which 7 were waited for; matrix products, arithmetic and copies ran while one was open for 9% of the time, Pallas kernels for 25%

profile of v5, /device:TPU:0, one launch (start us, length us, event | category | flops | bytes accessed | tf_op | source)
XLA Modules:
  0.0 110.1 jit_solution(16576049583623295515)
XLA Ops:
  0.0 1.0 copy.10
  1.5 0.8 copy.7
  2.3 0.8 pad_add_fusion.near_ref
  3.1 0.6 pad_add_fusion.1.place_ref
  4.8 0.7 copy-done.3
  5.5 4.1 %prepare.1 = (bf16[4,336,128]{2,1,0:T(8,128)(2,1)}, bf16[4,336,128]{2,1,0:T(8,128)(2,1)}) custom-call(s32[2]{0:T(128)} %pad_add_fusion.1.place_ref, s32[4,10]{1,0:T(4,128)} %copy-done.11, s32[4,10]{1,0:T(4,128)} %copy-done.12, bf16[4,288,128]{2,1,0:T(8,128)(2,1)} %bitcast.7, bf16[4,288,128]{2,1,0:T(8,128)(2,1)} %copy-done.3, ...), custom_call_target="tpu_custom_call" | custom-call | tf_op jit(solution)/shard_map/prepare/pallas_call | solution.py:133
  9.6 2.7 %collective-permute-start.2 = (bf16[4,336,128]{2,1,0:T(8,128)(2,1)}, bf16[4,336,128]{2,1,0:T(8,128)(2,1)S(1)}, u32[]{:S(2)}, u32[]{:S(2)}) collective-permute-start(bf16[4,336,128]{2,1,0:T(8,128)(2,1)} %get-tuple-element.49.refs_0_), channel_id=1, source_target_pairs={{0,16},{1,17},{2,18},{3,19},{4,20},{5,21},{6,22},{7,23},{8,9},{9,8... | collective-permute-start | bytes 1032200 | tf_op jit(solution)/shard_map/ppermute | solution.py:549
  12.2 1.5 %collective-permute-start.3 = (bf16[4,336,128]{2,1,0:T(8,128)(2,1)}, bf16[4,336,128]{2,1,0:T(8,128)(2,1)S(1)}, u32[]{:S(2)}, u32[]{:S(2)}) collective-permute-start(bf16[4,336,128]{2,1,0:T(8,128)(2,1)} %get-tuple-element.49.refs_0_), channel_id=1, source_target_pairs={{0,1},{1,0},{2,3},{3,2},{4,5},{5,4},{6,7},{7,6},{8,24},{9,25},{10,... | collective-permute-start | bytes 1032200 | tf_op jit(solution)/shard_map/ppermute | solution.py:549
  13.8 1.6 %collective-permute-start.4 = (bf16[4,336,128]{2,1,0:T(8,128)(2,1)}, bf16[4,336,128]{2,1,0:T(8,128)(2,1)S(1)}, u32[]{:S(2)}, u32[]{:S(2)}) collective-permute-start(bf16[4,336,128]{2,1,0:T(8,128)(2,1)} %get-tuple-element.49.refs_0_), channel_id=1, source_target_pairs={{0,2},{1,3},{2,4},{3,5},{4,6},{5,7},{6,0},{7,1},{8,10},{9,11},{10,... | collective-permute-start | bytes 1032200 | tf_op jit(solution)/shard_map/ppermute | solution.py:549
  15.3 7.1 %reshape.7.refs_4_ = bf16[50,36,1024]{2,1,0:T(8,128)(2,1)} reshape(bf16[50,36864]{1,0:T(8,128)(2,1)} %param.7) | data formatting | bytes 7372800 | tf_op jit(solution)/shard_map/reshape | solution.py:560
  22.5 3.2 %collective-permute-done.4 = bf16[4,336,128]{2,1,0:T(8,128)(2,1)S(1)} collective-permute-done((bf16[4,336,128]{2,1,0:T(8,128)(2,1)}, bf16[4,336,128]{2,1,0:T(8,128)(2,1)S(1)}, u32[]{:S(2)}, u32[]{:S(2)}) %collective-permute-start.4) | collective-permute-done | bytes 344096 | tf_op jit(solution)/shard_map/ppermute | solution.py:549
  25.9 0.6 collective-permute-start.8
  27.0 1.5 %collective-permute-start.10 = (bf16[4,336,128]{2,1,0:T(8,128)(2,1)S(1)}, bf16[4,336,128]{2,1,0:T(8,128)(2,1)S(1)}, u32[]{:S(2)}, u32[]{:S(2)}) collective-permute-start(bf16[4,336,128]{2,1,0:T(8,128)(2,1)S(1)} %collective-permute-done.2), channel_id=1, source_target_pairs={{0,1},{1,0},{2,3},{3,2},{4,5},{5,4},{6,7},{7,6},{8,24},{9,25},{10,... | collective-permute-start | bytes 1032200 | tf_op jit(solution)/shard_map/ppermute | solution.py:549
  28.5 0.9 copy-done.14
  29.4 3.8 %collective-permute-start.7 = (bf16[4,336,128]{2,1,0:T(8,128)(2,1)S(1)}, bf16[4,336,128]{2,1,0:T(8,128)(2,1)S(1)}, u32[]{:S(2)}, u32[]{:S(2)}) collective-permute-start(bf16[4,336,128]{2,1,0:T(8,128)(2,1)S(1)} %copy-done.16), channel_id=1, source_target_pairs={{0,6},{1,7},{2,0},{3,1},{4,2},{5,3},{6,4},{7,5},{8,14},{9,15},{10,... | collective-permute-start | bytes 1032200 | tf_op jit(solution)/shard_map/ppermute | solution.py:549
  33.2 9.0 %score.1 = (f32[8,8,128]{2,1,0:T(8,128)}, f32[16,128]{1,0:T(8,128)}, s32[8,3]{1,0:T(8,128)}) custom-call(s32[2]{0:T(128)} %pad_add_fusion.1.place_ref, bf16[4,336,128]{2,1,0:T(8,128)(2,1)} %get-tuple-element.49.refs_0_, bf16[4,336,128]{2,1,0:T(8,128)(2,1)} %get-tuple-element.42.refs_1_, bf16[8,336,128]{2,1,0:T(8,128)(2,1)} %copy-done, ...), custom_call_target="tpu_custom_call" | custom-call | flops 10000000000 | bytes 10000000 | tf_op jit(solution)/shard_map/score/pallas_call | solution.py:284
  42.2 3.2 %collective-permute-done.7 = bf16[4,336,128]{2,1,0:T(8,128)(2,1)S(1)} collective-permute-done((bf16[4,336,128]{2,1,0:T(8,128)(2,1)S(1)}, bf16[4,336,128]{2,1,0:T(8,128)(2,1)S(1)}, u32[]{:S(2)}, u32[]{:S(2)}) %collective-permute-start.7) | collective-permute-done | bytes 344096 | tf_op jit(solution)/shard_map/ppermute | solution.py:549
  45.5 0.6 collective-permute-start.12
  46.1 1.3 %collective-permute-start.13 = (f32[16,128]{1,0:T(8,128)}, f32[16,128]{1,0:T(8,128)S(1)}, u32[]{:S(2)}, u32[]{:S(2)}) collective-permute-start(f32[16,128]{1,0:T(8,128)} %get-tuple-element.52.refs_0_), channel_id=1, source_target_pairs={{0,24},{1,25},{2,26},{3,27},{4,28},{5,29},{6,30},{7,31},{8,16},{9,... | collective-permute-start | bytes 24584 | tf_op jit(solution)/shard_map/ppermute | solution.py:549
  47.4 2.1 %collective-permute-done.12.refs_2_ = f32[16,128]{1,0:T(8,128)S(1)} collective-permute-done((f32[16,128]{1,0:T(8,128)}, f32[16,128]{1,0:T(8,128)S(1)}, u32[]{:S(2)}, u32[]{:S(2)}) %collective-permute-start.12) | collective-permute-done | bytes 8224 | tf_op jit(solution)/shard_map/ppermute | solution.py:549
  50.1 1.6 %normalise.1 = bf16[64,128]{1,0:T(8,128)(2,1)} custom-call(s32[2]{0:T(128)} %pad_add_fusion.1.place_ref, s32[8,3]{1,0:T(8,128)} %get-tuple-element.58.partner_ref, f32[8,8,128]{2,1,0:T(8,128)} %get-tuple-element.59.weight_ref, f32[16,128]{1,0:T(8,128)} %get-tuple-element.52.refs_0_, f32[16,128]{1,0:T(8,128)} %copy-done.8, f32[16,128]{1,0:T(8,128)} %copy-done.9, ...), custom_call_target="tpu_custom_call" | custom-call | tf_op jit(solution)/shard_map/normalise/pallas_call | solution.py:337
  52.2 1.5 %collective-permute-start.15 = (bf16[4,336,128]{2,1,0:T(8,128)(2,1)S(1)}, bf16[4,336,128]{2,1,0:T(8,128)(2,1)S(1)}, u32[]{:S(2)}, u32[]{:S(2)}) collective-permute-start(bf16[4,336,128]{2,1,0:T(8,128)(2,1)S(1)} %collective-permute-done.6), channel_id=1, source_target_pairs={{0,16},{1,17},{2,18},{3,19},{4,20},{5,21},{6,22},{7,23},{8,9},{9,8... | collective-permute-start | bytes 1032200 | tf_op jit(solution)/shard_map/ppermute | solution.py:549
  55.0 4.8 %collective-permute-done.17 = bf16[64,128]{1,0:T(8,128)(2,1)S(1)} collective-permute-done((bf16[64,128]{1,0:T(8,128)(2,1)S(1)}, bf16[64,128]{1,0:T(8,128)(2,1)S(1)}, u32[]{:S(2)}, u32[]{:S(2)}) %collective-permute-start.17) | collective-permute-done | bytes 16416 | tf_op jit(solution)/shard_map/ppermute | solution.py:549
  59.8 3.7 %collective-permute-done.19 = bf16[64,128]{1,0:T(8,128)(2,1)S(1)} collective-permute-done((bf16[64,128]{1,0:T(8,128)(2,1)S(1)}, bf16[64,128]{1,0:T(8,128)(2,1)S(1)}, u32[]{:S(2)}, u32[]{:S(2)}) %collective-permute-start.19) | collective-permute-done | bytes 16416 | tf_op jit(solution)/shard_map/ppermute | solution.py:549
  63.5 1.6 %collective-permute-start.24 = (bf16[256,128]{1,0:T(8,128)(2,1)S(1)}, bf16[256,128]{1,0:T(8,128)(2,1)S(1)}, u32[]{:S(2)}, u32[]{:S(2)}) collective-permute-start(bf16[256,128]{1,0:T(8,128)(2,1)S(1)} %pad_maximum_fusion.1.refs_7_), channel_id=1, source_target_pairs={{0,1},{1,0},{2,3},{3,2},{4,5},{5,4},{6,7},{7,6},{8,9},{9,8},{10,11... | collective-permute-start | bytes 196616 | tf_op jit(solution)/shard_map/ppermute | solution.py:549
  65.2 1.9 %collective-permute-start.22 = (bf16[12,336,128]{2,1,0:T(8,128)(2,1)S(1)}, bf16[12,336,128]{2,1,0:T(8,128)(2,1)}, u32[]{:S(2)}, u32[]{:S(2)}) collective-permute-start(bf16[12,336,128]{2,1,0:T(8,128)(2,1)S(1)} %pad_maximum_fusion), channel_id=1, source_target_pairs={{0,6},{1,7},{2,0},{3,1},{4,2},{5,3},{6,4},{7,5},{8,14},{9,15},{10,... | collective-permute-start | bytes 3096584 | tf_op jit(solution)/shard_map/ppermute | solution.py:549
  67.6 1.5 %collective-permute-start.21 = (bf16[4,336,128]{2,1,0:T(8,128)(2,1)S(1)}, bf16[4,336,128]{2,1,0:T(8,128)(2,1)S(1)}, u32[]{:S(2)}, u32[]{:S(2)}) collective-permute-start(bf16[4,336,128]{2,1,0:T(8,128)(2,1)S(1)} %collective-permute-done.15), channel_id=1, source_target_pairs={{0,1},{1,0},{2,3},{3,2},{4,5},{5,4},{6,7},{7,6},{8,24},{9,25},{10,... | collective-permute-start | bytes 1032200 | tf_op jit(solution)/shard_map/ppermute | solution.py:549
  69.2 0.8 copy-done.4
  70.0 18.2 %class_sum.2 = (f32[16000,128]{1,0:T(8,128)}, f32[56,128]{1,0:T(8,128)}) custom-call(s32[2]{0:T(128)} %pad_add_fusion.1.place_ref, bf16[4,336,128]{2,1,0:T(8,128)(2,1)} %get-tuple-element.49.refs_0_, bf16[4,336,128]{2,1,0:T(8,128)(2,1)} %get-tuple-element.42.refs_1_, bf16[8,336,128]{2,1,0:T(8,128)(2,1)} %copy-done, bf16[8,336,128]{2,1,0:T(8,128)(2,1)} %copy-done.14, ...), custom_call_target="tpu_custom_call" | custom-call | flops 16000000000 | bytes 10000000 | tf_op jit(solution)/shard_map/class_sum/pallas_call | solution.py:511
  89.4 3.8 %collective-permute-done.16.refs_0_ = bf16[8,336,128]{2,1,0:T(8,128)(2,1)S(1)} collective-permute-done((bf16[8,336,128]{2,1,0:T(8,128)(2,1)}, bf16[8,336,128]{2,1,0:T(8,128)(2,1)S(1)}, u32[]{:S(2)}, u32[]{:S(2)}) %collective-permute-start.16) | collective-permute-done | bytes 688160 | tf_op jit(solution)/shard_map/ppermute | solution.py:549
  93.2 0.8 copy-done.15
  94.6 15.5 %class_sum.3 = bf16[50,36864]{1,0:T(8,128)(2,1)} custom-call(s32[2]{0:T(128)} %pad_add_fusion.1.place_ref, bf16[8,336,128]{2,1,0:T(8,128)(2,1)} %copy-done.15, bf16[4,336,128]{2,1,0:T(8,128)(2,1)} %copy-done.17, bf16[4,336,128]{2,1,0:T(8,128)(2,1)} %copy-done.18, bf16[12,336,128]{2,1,0:T(8,128)(2,1)} %collective-permute-done.22.refs_3_, ...), custom_call_target="tpu_custom_call" | custom-call | flops 9600000000 | bytes 10000000 | tf_op jit(solution)/shard_map/class_sum/pallas_call | solution.py:511
  (90 shorter events, 7.3 us)
Async XLA Ops:
  1.0 3.2 %collective-permute-start.1 = (bf16[4,288,128]{2,1,0:T(8,128)(2,1)S(1)}, bf16[4,288,128]{2,1,0:T(8,128)(2,1)S(1)}, u32[]{:S(2)}, u32[]{:S(2)}) collective-permute-start(bf16[4,288,128]{2,1,0:T(8,128)(2,1)S(1)} %bitcast.6), channel_id=1, source_target_pairs={{0,8},{1,9},{2,10},{3,11},{4,12},{5,13},{6,14},{7,15},{8,0},{9,1},... | collective-permute-start | bytes 884744 | tf_op jit(solution)/shard_map/ppermute | solution.py:549
  3.1 1.2 %collective-permute-start = (s32[4,10]{1,0:T(4,128)S(1)}, s32[4,10]{1,0:T(4,128)S(1)}, u32[]{:S(2)}, u32[]{:S(2)}) collective-permute-start(s32[4,10]{1,0:T(4,128)S(1)} %pad_add_fusion.near_ref), channel_id=1, source_target_pairs={{0,8},{1,9},{2,10},{3,11},{4,12},{5,13},{6,14},{7,15},{8,0},{9,1},... | collective-permute-start | bytes 488 | tf_op jit(solution)/shard_map/ppermute | solution.py:549
  9.6 19.8 %copy-start.16 = (bf16[4,336,128]{2,1,0:T(8,128)(2,1)S(1)}, bf16[4,336,128]{2,1,0:T(8,128)(2,1)}, u32[]{:S(2)}) copy-start(bf16[4,336,128]{2,1,0:T(8,128)(2,1)} %get-tuple-element.49.refs_0_) | copy-start | bytes 1032196
  9.6 12.9 %collective-permute-start.2 = (bf16[4,336,128]{2,1,0:T(8,128)(2,1)}, bf16[4,336,128]{2,1,0:T(8,128)(2,1)S(1)}, u32[]{:S(2)}, u32[]{:S(2)}) collective-permute-start(bf16[4,336,128]{2,1,0:T(8,128)(2,1)} %get-tuple-element.49.refs_0_), channel_id=1, source_target_pairs={{0,16},{1,17},{2,18},{3,19},{4,20},{5,21},{6,22},{7,23},{8,9},{9,8... | collective-permute-start | bytes 1032200 | tf_op jit(solution)/shard_map/ppermute | solution.py:549
  12.2 10.2 %collective-permute-start.3 = (bf16[4,336,128]{2,1,0:T(8,128)(2,1)}, bf16[4,336,128]{2,1,0:T(8,128)(2,1)S(1)}, u32[]{:S(2)}, u32[]{:S(2)}) collective-permute-start(bf16[4,336,128]{2,1,0:T(8,128)(2,1)} %get-tuple-element.49.refs_0_), channel_id=1, source_target_pairs={{0,1},{1,0},{2,3},{3,2},{4,5},{5,4},{6,7},{7,6},{8,24},{9,25},{10,... | collective-permute-start | bytes 1032200 | tf_op jit(solution)/shard_map/ppermute | solution.py:549
  13.8 11.8 %collective-permute-start.4 = (bf16[4,336,128]{2,1,0:T(8,128)(2,1)}, bf16[4,336,128]{2,1,0:T(8,128)(2,1)S(1)}, u32[]{:S(2)}, u32[]{:S(2)}) collective-permute-start(bf16[4,336,128]{2,1,0:T(8,128)(2,1)} %get-tuple-element.49.refs_0_), channel_id=1, source_target_pairs={{0,2},{1,3},{2,4},{3,5},{4,6},{5,7},{6,0},{7,1},{8,10},{9,11},{10,... | collective-permute-start | bytes 1032200 | tf_op jit(solution)/shard_map/ppermute | solution.py:549
  25.7 7.5 %copy-start = (bf16[8,336,128]{2,1,0:T(8,128)(2,1)}, bf16[8,336,128]{2,1,0:T(8,128)(2,1)S(1)}, u32[]{:S(2)}) copy-start(bf16[8,336,128]{2,1,0:T(8,128)(2,1)S(1)} %constant_dynamic-update-slice_fusion.refs_2_) | copy-start | bytes 2064388
  25.7 2.8 %collective-permute-start.5 = (bf16[8,336,128]{2,1,0:T(8,128)(2,1)S(1)}, bf16[8,336,128]{2,1,0:T(8,128)(2,1)S(1)}, u32[]{:S(2)}, u32[]{:S(2)}) collective-permute-start(bf16[8,336,128]{2,1,0:T(8,128)(2,1)S(1)} %constant_dynamic-update-slice_fusion.refs_2_), channel_id=1, source_target_pairs={{0,8},{1,9},{2,10},{3,11},{4,12},{5,13},{6,14},{7,15},{8,0},{9,1},... | collective-permute-start | bytes 2064392 | tf_op jit(solution)/shard_map/ppermute | solution.py:549
  25.8 19.6 %collective-permute-start.6 = (bf16[4,336,128]{2,1,0:T(8,128)(2,1)S(1)}, bf16[4,336,128]{2,1,0:T(8,128)(2,1)S(1)}, u32[]{:S(2)}, u32[]{:S(2)}) collective-permute-start(bf16[4,336,128]{2,1,0:T(8,128)(2,1)S(1)} %collective-permute-done.4), channel_id=1, source_target_pairs={{0,2},{1,3},{2,4},{3,5},{4,6},{5,7},{6,0},{7,1},{8,10},{9,11},{10,... | collective-permute-start | bytes 1032200 | tf_op jit(solution)/shard_map/ppermute | solution.py:549
  25.9 19.6 %collective-permute-start.8 = (bf16[4,336,128]{2,1,0:T(8,128)(2,1)S(1)}, bf16[4,336,128]{2,1,0:T(8,128)(2,1)S(1)}, u32[]{:S(2)}, u32[]{:S(2)}) collective-permute-start(bf16[4,336,128]{2,1,0:T(8,128)(2,1)S(1)} %collective-permute-done.4), channel_id=1, source_target_pairs={{0,16},{1,17},{2,18},{3,19},{4,20},{5,21},{6,22},{7,23},{8,9},{9,8... | collective-permute-start | bytes 1032200 | tf_op jit(solution)/shard_map/ppermute | solution.py:549
  26.5 19.0 %collective-permute-start.9 = (bf16[4,336,128]{2,1,0:T(8,128)(2,1)S(1)}, bf16[4,336,128]{2,1,0:T(8,128)(2,1)S(1)}, u32[]{:S(2)}, u32[]{:S(2)}) collective-permute-start(bf16[4,336,128]{2,1,0:T(8,128)(2,1)S(1)} %collective-permute-done.4), channel_id=1, source_target_pairs={{0,1},{1,0},{2,3},{3,2},{4,5},{5,4},{6,7},{7,6},{8,24},{9,25},{10,... | collective-permute-start | bytes 1032200 | tf_op jit(solution)/shard_map/ppermute | solution.py:549
  27.0 18.5 %collective-permute-start.10 = (bf16[4,336,128]{2,1,0:T(8,128)(2,1)S(1)}, bf16[4,336,128]{2,1,0:T(8,128)(2,1)S(1)}, u32[]{:S(2)}, u32[]{:S(2)}) collective-permute-start(bf16[4,336,128]{2,1,0:T(8,128)(2,1)S(1)} %collective-permute-done.2), channel_id=1, source_target_pairs={{0,1},{1,0},{2,3},{3,2},{4,5},{5,4},{6,7},{7,6},{8,24},{9,25},{10,... | collective-permute-start | bytes 1032200 | tf_op jit(solution)/shard_map/ppermute | solution.py:549
  29.4 16.0 %collective-permute-start.7 = (bf16[4,336,128]{2,1,0:T(8,128)(2,1)S(1)}, bf16[4,336,128]{2,1,0:T(8,128)(2,1)S(1)}, u32[]{:S(2)}, u32[]{:S(2)}) collective-permute-start(bf16[4,336,128]{2,1,0:T(8,128)(2,1)S(1)} %copy-done.16), channel_id=1, source_target_pairs={{0,6},{1,7},{2,0},{3,1},{4,2},{5,3},{6,4},{7,5},{8,14},{9,15},{10,... | collective-permute-start | bytes 1032200 | tf_op jit(solution)/shard_map/ppermute | solution.py:549
  45.4 1.9 %collective-permute-start.11 = (f32[16,128]{1,0:T(8,128)}, f32[16,128]{1,0:T(8,128)S(1)}, u32[]{:S(2)}, u32[]{:S(2)}) collective-permute-start(f32[16,128]{1,0:T(8,128)} %get-tuple-element.52.refs_0_), channel_id=1, source_target_pairs={{0,8},{1,9},{2,10},{3,11},{4,12},{5,13},{6,14},{7,15},{8,0},{9,1},... | collective-permute-start | bytes 24584 | tf_op jit(solution)/shard_map/ppermute | solution.py:549
  45.5 4.0 %collective-permute-start.12 = (f32[16,128]{1,0:T(8,128)}, f32[16,128]{1,0:T(8,128)S(1)}, u32[]{:S(2)}, u32[]{:S(2)}) collective-permute-start(f32[16,128]{1,0:T(8,128)} %get-tuple-element.52.refs_0_), channel_id=1, source_target_pairs={{0,16},{1,17},{2,18},{3,19},{4,20},{5,21},{6,22},{7,23},{8,24},{9,... | collective-permute-start | bytes 24584 | tf_op jit(solution)/shard_map/ppermute | solution.py:549
  46.1 3.4 %collective-permute-start.13 = (f32[16,128]{1,0:T(8,128)}, f32[16,128]{1,0:T(8,128)S(1)}, u32[]{:S(2)}, u32[]{:S(2)}) collective-permute-start(f32[16,128]{1,0:T(8,128)} %get-tuple-element.52.refs_0_), channel_id=1, source_target_pairs={{0,24},{1,25},{2,26},{3,27},{4,28},{5,29},{6,30},{7,31},{8,16},{9,... | collective-permute-start | bytes 24584 | tf_op jit(solution)/shard_map/ppermute | solution.py:549
  51.7 13.5 %copy-start.1 = (bf16[8,336,128]{2,1,0:T(8,128)(2,1)S(1)}, bf16[8,336,128]{2,1,0:T(8,128)(2,1)}, u32[]{:S(2)}) copy-start(bf16[8,336,128]{2,1,0:T(8,128)(2,1)} %copy-done) | copy-start | bytes 2064388
  52.0 17.2 %copy-start.7 = (bf16[24,336,128]{2,1,0:T(8,128)(2,1)}, bf16[24,336,128]{2,1,0:T(8,128)(2,1)S(1)}, u32[]{:S(2)}) copy-start(bf16[24,336,128]{2,1,0:T(8,128)(2,1)S(1)} %constant_dynamic-update-slice_fusion.4.refs_4_) | copy-start | bytes 6193156
  52.0 17.2 %collective-permute-start.23 = (bf16[24,336,128]{2,1,0:T(8,128)(2,1)S(1)}, bf16[24,336,128]{2,1,0:T(8,128)(2,1)}, u32[]{:S(2)}, u32[]{:S(2)}) collective-permute-start(bf16[24,336,128]{2,1,0:T(8,128)(2,1)S(1)} %constant_dynamic-update-slice_fusion.4.refs_4_), channel_id=1, source_target_pairs={{0,8},{1,9},{2,10},{3,11},{4,12},{5,13},{6,14},{7,15},{8,0},{9,1},... | collective-permute-start | bytes 6193160 | tf_op jit(solution)/shard_map/ppermute | solution.py:549
  52.2 11.4 %collective-permute-start.15 = (bf16[4,336,128]{2,1,0:T(8,128)(2,1)S(1)}, bf16[4,336,128]{2,1,0:T(8,128)(2,1)S(1)}, u32[]{:S(2)}, u32[]{:S(2)}) collective-permute-start(bf16[4,336,128]{2,1,0:T(8,128)(2,1)S(1)} %collective-permute-done.6), channel_id=1, source_target_pairs={{0,16},{1,17},{2,18},{3,19},{4,20},{5,21},{6,22},{7,23},{8,9},{9,8... | collective-permute-start | bytes 1032200 | tf_op jit(solution)/shard_map/ppermute | solution.py:549
  53.6 14.0 %collective-permute-start.14 = (bf16[4,336,128]{2,1,0:T(8,128)(2,1)S(1)}, bf16[4,336,128]{2,1,0:T(8,128)(2,1)S(1)}, u32[]{:S(2)}, u32[]{:S(2)}) collective-permute-start(bf16[4,336,128]{2,1,0:T(8,128)(2,1)S(1)} %collective-permute-done.8), channel_id=1, source_target_pairs={{0,1},{1,0},{2,3},{3,2},{4,5},{5,4},{6,7},{7,6},{8,24},{9,25},{10,... | collective-permute-start | bytes 1032200 | tf_op jit(solution)/shard_map/ppermute | solution.py:549
  54.1 5.7 %collective-permute-start.17 = (bf16[64,128]{1,0:T(8,128)(2,1)S(1)}, bf16[64,128]{1,0:T(8,128)(2,1)S(1)}, u32[]{:S(2)}, u32[]{:S(2)}) collective-permute-start(bf16[64,128]{1,0:T(8,128)(2,1)S(1)} %copy-done.6), channel_id=1, source_target_pairs={{0,2},{1,3},{2,4},{3,5},{4,6},{5,7},{6,0},{7,1},{8,10},{9,11},{10,... | collective-permute-start | bytes 49160 | tf_op jit(solution)/shard_map/ppermute | solution.py:549
  54.7 5.1 %collective-permute-start.18 = (bf16[64,128]{1,0:T(8,128)(2,1)S(1)}, bf16[64,128]{1,0:T(8,128)(2,1)S(1)}, u32[]{:S(2)}, u32[]{:S(2)}) collective-permute-start(bf16[64,128]{1,0:T(8,128)(2,1)S(1)} %copy-done.6), channel_id=1, source_target_pairs={{0,4},{1,5},{2,6},{3,7},{4,0},{5,1},{6,2},{7,3},{8,12},{9,13},{10,... | collective-permute-start | bytes 49160 | tf_op jit(solution)/shard_map/ppermute | solution.py:549
  59.8 3.7 %collective-permute-start.19 = (bf16[64,128]{1,0:T(8,128)(2,1)S(1)}, bf16[64,128]{1,0:T(8,128)(2,1)S(1)}, u32[]{:S(2)}, u32[]{:S(2)}) collective-permute-start(bf16[64,128]{1,0:T(8,128)(2,1)S(1)} %copy-done.6), channel_id=1, source_target_pairs={{0,6},{1,7},{2,0},{3,1},{4,2},{5,3},{6,4},{7,5},{8,14},{9,15},{10,... | collective-permute-start | bytes 49160 | tf_op jit(solution)/shard_map/ppermute | solution.py:549
  63.5 5.7 %collective-permute-start.24 = (bf16[256,128]{1,0:T(8,128)(2,1)S(1)}, bf16[256,128]{1,0:T(8,128)(2,1)S(1)}, u32[]{:S(2)}, u32[]{:S(2)}) collective-permute-start(bf16[256,128]{1,0:T(8,128)(2,1)S(1)} %pad_maximum_fusion.1.refs_7_), channel_id=1, source_target_pairs={{0,1},{1,0},{2,3},{3,2},{4,5},{5,4},{6,7},{7,6},{8,9},{9,8},{10,11... | collective-permute-start | bytes 196616 | tf_op jit(solution)/shard_map/ppermute | solution.py:549
  65.2 23.0 %collective-permute-start.22 = (bf16[12,336,128]{2,1,0:T(8,128)(2,1)S(1)}, bf16[12,336,128]{2,1,0:T(8,128)(2,1)}, u32[]{:S(2)}, u32[]{:S(2)}) collective-permute-start(bf16[12,336,128]{2,1,0:T(8,128)(2,1)S(1)} %pad_maximum_fusion), channel_id=1, source_target_pairs={{0,6},{1,7},{2,0},{3,1},{4,2},{5,3},{6,4},{7,5},{8,14},{9,15},{10,... | collective-permute-start | bytes 3096584 | tf_op jit(solution)/shard_map/ppermute | solution.py:549
  67.1 21.2 %collective-permute-start.20 = (bf16[4,336,128]{2,1,0:T(8,128)(2,1)S(1)}, bf16[4,336,128]{2,1,0:T(8,128)(2,1)S(1)}, u32[]{:S(2)}, u32[]{:S(2)}) collective-permute-start(bf16[4,336,128]{2,1,0:T(8,128)(2,1)S(1)} %collective-permute-done.6), channel_id=1, source_target_pairs={{0,1},{1,0},{2,3},{3,2},{4,5},{5,4},{6,7},{7,6},{8,24},{9,25},{10,... | collective-permute-start | bytes 1032200 | tf_op jit(solution)/shard_map/ppermute | solution.py:549
  67.6 20.7 %collective-permute-start.21 = (bf16[4,336,128]{2,1,0:T(8,128)(2,1)S(1)}, bf16[4,336,128]{2,1,0:T(8,128)(2,1)S(1)}, u32[]{:S(2)}, u32[]{:S(2)}) collective-permute-start(bf16[4,336,128]{2,1,0:T(8,128)(2,1)S(1)} %collective-permute-done.15), channel_id=1, source_target_pairs={{0,1},{1,0},{2,3},{3,2},{4,5},{5,4},{6,7},{7,6},{8,24},{9,25},{10,... | collective-permute-start | bytes 1032200 | tf_op jit(solution)/shard_map/ppermute | solution.py:549
  88.3 4.9 %collective-permute-start.27 = (bf16[12,336,128]{2,1,0:T(8,128)(2,1)}, bf16[12,336,128]{2,1,0:T(8,128)(2,1)S(1)}, u32[]{:S(2)}, u32[]{:S(2)}) collective-permute-start(bf16[12,336,128]{2,1,0:T(8,128)(2,1)} %collective-permute-done.22.refs_3_), channel_id=1, source_target_pairs={{0,8},{1,9},{2,10},{3,11},{4,12},{5,13},{6,14},{7,15},{8,0},{9,1},... | collective-permute-start | bytes 3096584 | tf_op jit(solution)/shard_map/ppermute | solution.py:549
  88.4 4.8 %collective-permute-start.16 = (bf16[8,336,128]{2,1,0:T(8,128)(2,1)}, bf16[8,336,128]{2,1,0:T(8,128)(2,1)S(1)}, u32[]{:S(2)}, u32[]{:S(2)}) collective-permute-start(bf16[8,336,128]{2,1,0:T(8,128)(2,1)} %copy-done.4), channel_id=1, source_target_pairs={{0,8},{1,9},{2,10},{3,11},{4,12},{5,13},{6,14},{7,15},{8,0},{9,1},... | collective-permute-start | bytes 2064392 | tf_op jit(solution)/shard_map/ppermute | solution.py:549
  88.9 4.3 %collective-permute-start.25 = (bf16[4,336,128]{2,1,0:T(8,128)(2,1)S(1)}, bf16[4,336,128]{2,1,0:T(8,128)(2,1)S(1)}, u32[]{:S(2)}, u32[]{:S(2)}) collective-permute-start(bf16[4,336,128]{2,1,0:T(8,128)(2,1)S(1)} %collective-permute-done.20.refs_1_), channel_id=1, source_target_pairs={{0,8},{1,9},{2,10},{3,11},{4,12},{5,13},{6,14},{7,15},{8,0},{9,1},... | collective-permute-start | bytes 1032200 | tf_op jit(solution)/shard_map/ppermute | solution.py:549
  88.9 4.2 %collective-permute-start.26 = (bf16[4,336,128]{2,1,0:T(8,128)(2,1)S(1)}, bf16[4,336,128]{2,1,0:T(8,128)(2,1)S(1)}, u32[]{:S(2)}, u32[]{:S(2)}) collective-permute-start(bf16[4,336,128]{2,1,0:T(8,128)(2,1)S(1)} %collective-permute-done.21.refs_2_), channel_id=1, source_target_pairs={{0,8},{1,9},{2,10},{3,11},{4,12},{5,13},{6,14},{7,15},{8,0},{9,1},... | collective-permute-start | bytes 1032200 | tf_op jit(solution)/shard_map/ppermute | solution.py:549
  (18 other events, 34.1 us)

commit v6 on v5

--- a/solution.py
+++ b/solution.py
@@ -50,18 +50,19 @@
     return table_ref[2 * axis, size, at, :], table_ref[2 * axis + 1, size, at, :] * sign
 
 
-def prep_kernel(local, place_ref, near_ref, far_ref, image_near, image_far, table_ref, mine_ref, rest_ref, raw):
-    count = near_ref.shape[0]
-    listed = near_ref.shape[1] - 2
+def prep_kernel(
+    local, near_ref, near_off, far_ref, far_off, image_near, image_far, table_ref, mine_ref, rest_ref, raw
+):
+    count, listed = near_ref.shape
     rows = image_near.shape[1]
     half = listed // 2
     share = count // 2
-    my_cls, my_dom = place_ref[0], place_ref[1]
+    my_cls, my_dom = lax.axis_index("cls"), lax.axis_index("dom")
     core = lax.rem(my_cls, 2)
     raw[...] = jnp.zeros_like(raw)
     lane = lax.broadcasted_iota(jnp.int32, (META_ROWS, LANES), 1)
     for far in range(2):
-        record, image_ref = (far_ref, image_far) if far else (near_ref, image_near)
+        record, prior, image_ref = (far_ref, far_off, image_far) if far else (near_ref, near_off, image_near)
         source_core = 1 - core if far else core
         source = my_cls - core + source_core
         cand = [[record[u, k] for k in range(listed)] for u in range(count)]
@@ -101,8 +102,8 @@
             for step in range(STEP_ANGLES):
                 re = raw[pl.ds(2 * step, SPAN, stride=PIECES), :]
                 im = raw[pl.ds(2 * step + 1, SPAN, stride=PIECES), :]
-                cx, sx = axis_phase(table_ref, 0, step, record[u, listed])
-                cy, sy = axis_phase(table_ref, 1, step, record[u, listed + 1])
+                cx, sx = axis_phase(table_ref, 0, step, prior[u, 0])
+                cy, sy = axis_phase(table_ref, 1, step, prior[u, 1])
                 cosine = cx * cy - sx * sy
                 sine = sx * cy + cx * sy
                 moved += [re * cosine + im * sine, im * cosine - re * sine]
@@ -127,18 +128,18 @@
 HBM_SPEC = pl.BlockSpec(memory_space=pl.ANY)
 
 
-def prepare(place, near, far, image_near, image_far, tables, local):
-    count = near.shape[0]
+def prepare(near, far, image_near, image_far, tables, local):
+    count = image_near.shape[0]
     shape = jax.ShapeDtypeStruct((count, IMAGE_ROWS + META_ROWS, LANES), image_near.dtype)
     return pl.pallas_call(
         functools.partial(prep_kernel, local),
         out_shape=(shape, shape),
-        in_specs=[SMEM_SPEC] * 3 + [VMEM_SPEC] * 3,
+        in_specs=[SMEM_SPEC] * 4 + [VMEM_SPEC] * 3,
         out_specs=(VMEM_SPEC, VMEM_SPEC),
         scratch_shapes=[pltpu.VMEM((IMAGE_ROWS, LANES), jnp.float32)],
         compiler_params=pltpu.CompilerParams(vmem_limit_bytes=VMEM_LIMIT),
         name="prepare",
-    )(place, near, far, image_near, image_far, tables)
+    )(*near, *far, image_near, image_far, tables)
 
 
 def read_meta(source, meta_vmem, row):
@@ -195,7 +196,7 @@
     moved[LANES : LANES + 2 * SPAN, at] = jnp.concatenate(blocks[3:], axis=0).astype(jnp.bfloat16)
 
 
-def score_kernel(count, place_ref, *refs):
+def score_kernel(count, *refs):
     image_refs = refs[:count]
     (
         refs_ref, table_ref, weight_ref, stat_ref, partner_ref,
@@ -204,7 +205,7 @@
     total = images.shape[0]
     slots = weight_ref.shape[0]
     classes = picked_a.shape[0] // 48
-    my_cls, my_dom = place_ref[0], place_ref[1]
+    my_cls, my_dom = lax.axis_index("cls"), lax.axis_index("dom")
     copies, at = [], 0
     for b, ref in enumerate(image_refs):
         copies.append(pltpu.make_async_copy(ref, images.at[pl.ds(at, ref.shape[0])], image_sem.at[b]))
@@ -278,7 +279,7 @@
     lax.fori_loop(0, lax.div(number + 1, 2), two, 0)
 
 
-def score(place, buffers, refs, tables, slots, classes):
+def score(buffers, refs, tables, slots, classes):
     count, total = len(buffers), sum(buffer.shape[0] for buffer in buffers)
     width = refs.shape[2]
     return pl.pallas_call(
@@ -288,7 +289,7 @@
             jax.ShapeDtypeStruct((2 * slots, LANES), jnp.float32),
             jax.ShapeDtypeStruct((slots, 3), jnp.int32),
         ),
-        in_specs=[SMEM_SPEC] + [HBM_SPEC] * count + [VMEM_SPEC] * 2,
+        in_specs=[HBM_SPEC] * count + [VMEM_SPEC] * 2,
         out_specs=(VMEM_SPEC, VMEM_SPEC, SMEM_SPEC),
         scratch_shapes=[
             pltpu.VMEM((total, IMAGE_ROWS + META_ROWS, LANES), jnp.bfloat16),
@@ -305,13 +306,13 @@
         compiler_params=pltpu.CompilerParams(vmem_limit_bytes=VMEM_LIMIT),
         cost_estimate=pl.CostEstimate(flops=10**10, bytes_accessed=10**7, transcendentals=0),
         name="score",
-    )(place, *buffers, refs, tables)
-
-
-def weight_kernel(flip, place_ref, partner_ref, weight_ref, *refs):
+    )(*buffers, refs, tables)
+
+
+def weight_kernel(flip, partner_ref, weight_ref, *refs):
     stat_refs, out_ref = refs[:-1], refs[-1]
     slots, lines, _ = weight_ref.shape
-    my_cls = place_ref[0]
+    my_cls = lax.axis_index("cls")
     done = []
     for slot in range(slots):
         other, other_slot = partner_ref[slot, OTHER], partner_ref[slot, OTHER_SLOT]
@@ -332,18 +333,18 @@
     out_ref[...] = jnp.concatenate(done, axis=0).astype(out_ref.dtype)
 
 
-def normalise(flip, place, partners, weights, stats):
+def normalise(flip, partners, weights, stats):
     slots, lines, _ = weights.shape
     return pl.pallas_call(
         functools.partial(weight_kernel, flip),
         out_shape=jax.ShapeDtypeStruct((slots * lines, LANES), jnp.bfloat16),
-        in_specs=[SMEM_SPEC] * 2 + [VMEM_SPEC] * (1 + len(stats)),
+        in_specs=[SMEM_SPEC] + [VMEM_SPEC] * (1 + len(stats)),
         out_specs=VMEM_SPEC,
         name="normalise",
-    )(place, partners, weights, *stats)
-
-
-def sum_kernel(weight_rows, relative, z_size, y_size, lines, local, width, count, n_weights, first, last, place_ref, *refs):
+    )(partners, weights, *stats)
+
+
+def sum_kernel(weight_rows, relative, z_size, y_size, lines, local, width, count, n_weights, first, last, *refs):
     refs = list(refs)
     image_refs = [refs.pop(0) for _ in range(count)]
     weight_refs = [refs.pop(0) for _ in range(n_weights)]
@@ -389,7 +390,7 @@
     moved_b[...] = jnp.zeros_like(moved_b)
     for b in range(n_weights):
         weights[b * chunk : (b + 1) * chunk, :] = weight_refs[b][...].astype(jnp.float32)
-    my_cls, my_dom = place_ref[0], place_ref[1]
+    my_cls, my_dom = lax.axis_index("cls"), lax.axis_index("dom")
     my_z, my_y = lax.div(my_dom, y_size), lax.rem(my_dom, y_size)
     lane = lax.broadcasted_iota(jnp.int32, (lines, LANES), 1)
     index_ref[...] = turned_lanes(-1)
@@ -481,7 +482,7 @@
             out_ref[:, pl.ds(turn * width + tile * LANES, LANES)] = (line * scale).astype(out_ref.dtype)
 
 
-def class_sum(place, buffers, weights, tables, given, last, relative, z_size, y_size, local, width, lines, weight_rows):
+def class_sum(buffers, weights, tables, given, last, relative, z_size, y_size, local, width, lines, weight_rows):
     count = len(buffers)
     total = sum(buffer.shape[0] for buffer in buffers)
     wave = total if total <= 128 else math.gcd(total, 128)
@@ -513,8 +514,7 @@
             sum_kernel, weight_rows, relative, z_size, y_size, lines, local, width, count, len(weights), first, last
         ),
         out_shape=out if last else held,
-        in_specs=[SMEM_SPEC]
-        + [HBM_SPEC] * count
+        in_specs=[HBM_SPEC] * count
         + [VMEM_SPEC] * (len(weights) + 1)
         + ([] if first else [HBM_SPEC] * 2),
         out_specs=VMEM_SPEC if last else (VMEM_SPEC, VMEM_SPEC),
@@ -522,7 +522,7 @@
         compiler_params=pltpu.CompilerParams(vmem_limit_bytes=VMEM_LIMIT),
         cost_estimate=pl.CostEstimate(flops=total * 2 * 10**8, bytes_accessed=10**7, transcendentals=0),
         name="class_sum",
-    )(place, *buffers, *weights, tables, *([] if first else given))
+    )(*buffers, *weights, tables, *([] if first else given))
 
 
 def shards(x_size, y_size, z_size, particles, references, candidates, offsets):
@@ -534,7 +534,6 @@
     block_width = width // ROT
     slots = groups * (count // 2)
     tables = trig_tables()
-    place = jnp.stack([lax.axis_index("cls"), lax.axis_index("dom")]).astype(jnp.int32)
 
     def moves(goal):
         out = []
@@ -555,19 +554,19 @@
     late = functools.partial(send, goal=lambda x, c, z, y: (x + c, c, z, y + 1 - c))
 
     images = particles.reshape(count, width // LANES, LANES)
-    record = jnp.concatenate([candidates, offsets], axis=1)
-    mine, rest = prepare(place, record, swap(record), images, swap(images), jnp.asarray(tables), local)
+    near, far = (candidates, offsets), (swap(candidates), swap(offsets))
+    mine, rest = prepare(near, far, images, swap(images), jnp.asarray(tables), local)
     refs = lax.optimization_barrier((references, mine))[0].reshape(local, ROT, block_width)
     steps = jnp.asarray(tables[:, 1])
     tuned = x_size == 2 and y_size == 2 and z_size == 4
     if tuned:
-        e0, l0, z1 = early(mine), late(mine), along_z(mine)
+        z1, e0, l0 = along_z(mine), early(mine), late(mine)
         e0, l0, z1, refs = lax.optimization_barrier((e0, l0, z1, refs))
         near = jnp.concatenate([e0, l0])
         row = [mine, rest, near, swap(near)]
         e1, l1, z2, f0 = early(z1), late(z1), along_z(z1), late(e0)
         z3 = back_z(lax.optimization_barrier((mine, z1))[0])
-        weights, stats, partners = score(place, row, refs, steps, slots, classes)
+        weights, stats, partners = score(row, refs, steps, slots, classes)
         stats, z2, z3, e1, l1, f0 = lax.optimization_barrier((stats, z2, z3, e1, l1, f0))
         stats = [
             stats,
@@ -577,7 +576,7 @@
         ]
         z2_late, e1_late, *_ = lax.optimization_barrier((z2, e1, *stats))
         e2, f1 = early(z2_late), late(e1_late)
-        weights = normalise(tuned, place, partners, weights, stats)
+        weights = normalise(tuned, partners, weights, stats)
         *held, weights = lax.optimization_barrier((z1, z2, z3, e1, l1, f0, weights))
         weights = [weights] + [send(weights, lambda x, c, z, y, dz=dz: (x, c, z + dz, y)) for dz in range(1, z_size)]
         weights = jnp.concatenate(weights)
@@ -591,9 +590,9 @@
     else:
         row = lax.all_gather(mine, "cls", axis=0, tiled=True)
         parts = [[lax.all_gather(row, "dom", axis=0, tiled=True)]]
-        weights, stats, partners = score(place, [row], refs, steps, slots, classes)
+        weights, stats, partners = score([row], refs, steps, slots, classes)
         stats = [lax.all_gather(stats, "cls", axis=0, tiled=False)]
-        weights = normalise(tuned, place, partners, weights, stats)
+        weights = normalise(tuned, partners, weights, stats)
         weights = [lax.all_gather(weights, "dom", axis=0, tiled=True)]
     held = None
     for k, part in enumerate(parts):
@@ -601,7 +600,7 @@
             *end, _ = lax.optimization_barrier((*part[1:], held[1]))
             part = part[:1] + end + [swap(block) for block in end]
         held = class_sum(
-            place, part, weights, steps, held, k == len(parts) - 1, tuned, z_size, y_size, local, block_width, 2 * classes, slots * 2 * classes
+            part, weights, steps, held, k == len(parts) - 1, tuned, z_size, y_size, local, block_width, 2 * classes, slots * 2 * classes
         )
     return held
 

time: 111 us -> 111 us (level)
  other arithmetic: 1.45 us -> 0.1 us
    ppermute x28 -> x29, waiting for transfers between devices: 21.3 us -> 22.4 us  [send(): return lax.ppermute(value, ('cls', 'dom'), moves(goal))]
    ppermute x28 -> x29, starting transfers between devices: 24.3 us -> 24.3 us  [send(): return lax.ppermute(value, ('cls', 'dom'), moves(goal))]
    unnamed x53 -> x55, local copies, waits for them, and re-layouts: 7.08 us -> 7.06 us
  transfers between devices with their start and end apart: 28 -> 29, of which waited for: 7 -> 8; matrix products, arithmetic and copies ran while one was open for 9% -> 7% of each run, Pallas kernels for 25% -> 24%
where the time goes in v6:
time: 111 us; the launch traced here: 110 us
  Pallas kernels  48.8 us (44%)
  starting transfers between devices  24.3 us (22%)
  waiting for transfers between devices  22.4 us (20%)
  local copies, waits for them, and re-layouts  14.3 us (13%)
    pallas_call x2, Pallas kernels, class_sum(): pl.pallas_call(functools.partial(sum_kernel, weight_rows, relative, z_siz...  34.1 us
    ppermute x29, starting transfers between devices, send(): return lax.ppermute(value, ('cls', 'dom'), moves(goal))  24.3 us
    ppermute x29, waiting for transfers between devices, send(): return lax.ppermute(value, ('cls', 'dom'), moves(goal))  22.4 us
    pallas_call x1, Pallas kernels, score(): pl.pallas_call(functools.partial(score_kernel, count), out_shape=(jax.Sha...  9.04 us
    reshape x1, local copies, waits for them, and re-layouts, shards(): lax.optimization_barrier((references, mine))[0]  7.11 us
    unnamed x55, local copies, waits for them, and re-layouts  7.06 us
    pallas_call x1, Pallas kernels, prepare(): pl.pallas_call(functools.partial(prep_kernel, local), out_shape=(shape, s...  4.09 us
  transfers between devices with their start and end apart: 29, of which 8 were waited for; matrix products, arithmetic and copies ran while one was open for 7% of the time, Pallas kernels for 24%

profile of v6, /device:TPU:0, one launch (start us, length us, event | category | flops | bytes accessed | tf_op | source)
XLA Modules:
  0.0 110.2 jit_solution(8192013150387867945)
XLA Ops:
  0.0 1.0 copy.11
  1.6 0.8 copy.8.near_off
  2.8 0.8 collective-permute-done.1.far_off
  4.2 0.7 copy-done.3
  4.9 4.1 %prepare.1 = (bf16[4,336,128]{2,1,0:T(8,128)(2,1)}, bf16[4,336,128]{2,1,0:T(8,128)(2,1)}) custom-call(s32[4,8]{1,0:T(4,128)} %near_ref.1, s32[4,2]{1,0:T(4,128)} %copy-done.8, s32[4,8]{1,0:T(4,128)} %copy-done.12, s32[4,2]{1,0:T(4,128)} %copy-done.13, bf16[4,288,128]{2,1,0:T(8,128)(2,1)} %bitcast.5, bf16[4,288,128]{2,1,0:T(8,128)(2,1)} %copy-done.3, ...), custom_call_target="tpu_custom_call" | custom-call | tf_op jit(solution)/shard_map/prepare/pallas_call | solution.py:134
  9.0 2.8 %collective-permute-start.3 = (bf16[4,336,128]{2,1,0:T(8,128)(2,1)}, bf16[4,336,128]{2,1,0:T(8,128)(2,1)S(1)}, u32[]{:S(2)}, u32[]{:S(2)}) collective-permute-start(bf16[4,336,128]{2,1,0:T(8,128)(2,1)} %get-tuple-element.49.refs_0_), channel_id=1, source_target_pairs={{0,16},{1,17},{2,18},{3,19},{4,20},{5,21},{6,22},{7,23},{8,9},{9,8... | collective-permute-start | bytes 1032200 | tf_op jit(solution)/shard_map/ppermute | solution.py:548
  11.8 1.5 %collective-permute-start.4 = (bf16[4,336,128]{2,1,0:T(8,128)(2,1)}, bf16[4,336,128]{2,1,0:T(8,128)(2,1)S(1)}, u32[]{:S(2)}, u32[]{:S(2)}) collective-permute-start(bf16[4,336,128]{2,1,0:T(8,128)(2,1)} %get-tuple-element.49.refs_0_), channel_id=1, source_target_pairs={{0,1},{1,0},{2,3},{3,2},{4,5},{5,4},{6,7},{7,6},{8,24},{9,25},{10,... | collective-permute-start | bytes 1032200 | tf_op jit(solution)/shard_map/ppermute | solution.py:548
  13.4 1.6 %collective-permute-start.5 = (bf16[4,336,128]{2,1,0:T(8,128)(2,1)}, bf16[4,336,128]{2,1,0:T(8,128)(2,1)S(1)}, u32[]{:S(2)}, u32[]{:S(2)}) collective-permute-start(bf16[4,336,128]{2,1,0:T(8,128)(2,1)} %get-tuple-element.49.refs_0_), channel_id=1, source_target_pairs={{0,2},{1,3},{2,4},{3,5},{4,6},{5,7},{6,0},{7,1},{8,10},{9,11},{10,... | collective-permute-start | bytes 1032200 | tf_op jit(solution)/shard_map/ppermute | solution.py:548
  14.9 7.1 %reshape.7.refs_4_ = bf16[50,36,1024]{2,1,0:T(8,128)(2,1)} reshape(bf16[50,36864]{1,0:T(8,128)(2,1)} %param.7) | data formatting | bytes 7372800 | tf_op jit(solution)/shard_map/reshape | solution.py:559
  22.1 3.0 %collective-permute-done.5 = bf16[4,336,128]{2,1,0:T(8,128)(2,1)S(1)} collective-permute-done((bf16[4,336,128]{2,1,0:T(8,128)(2,1)}, bf16[4,336,128]{2,1,0:T(8,128)(2,1)S(1)}, u32[]{:S(2)}, u32[]{:S(2)}) %collective-permute-start.5) | collective-permute-done | bytes 344096 | tf_op jit(solution)/shard_map/ppermute | solution.py:548
  25.2 0.6 collective-permute-start.10
  26.4 1.5 %collective-permute-start.11 = (bf16[4,336,128]{2,1,0:T(8,128)(2,1)S(1)}, bf16[4,336,128]{2,1,0:T(8,128)(2,1)S(1)}, u32[]{:S(2)}, u32[]{:S(2)}) collective-permute-start(bf16[4,336,128]{2,1,0:T(8,128)(2,1)S(1)} %collective-permute-done.3), channel_id=1, source_target_pairs={{0,1},{1,0},{2,3},{3,2},{4,5},{5,4},{6,7},{7,6},{8,24},{9,25},{10,... | collective-permute-start | bytes 1032200 | tf_op jit(solution)/shard_map/ppermute | solution.py:548
  27.9 0.9 copy-done.15
  28.8 3.8 %collective-permute-start.8 = (bf16[4,336,128]{2,1,0:T(8,128)(2,1)S(1)}, bf16[4,336,128]{2,1,0:T(8,128)(2,1)S(1)}, u32[]{:S(2)}, u32[]{:S(2)}) collective-permute-start(bf16[4,336,128]{2,1,0:T(8,128)(2,1)S(1)} %copy-done.17), channel_id=1, source_target_pairs={{0,6},{1,7},{2,0},{3,1},{4,2},{5,3},{6,4},{7,5},{8,14},{9,15},{10,... | collective-permute-start | bytes 1032200 | tf_op jit(solution)/shard_map/ppermute | solution.py:548
  32.6 9.0 %score.1 = (f32[8,8,128]{2,1,0:T(8,128)}, f32[16,128]{1,0:T(8,128)}, s32[8,3]{1,0:T(8,128)}) custom-call(bf16[4,336,128]{2,1,0:T(8,128)(2,1)} %get-tuple-element.49.refs_0_, bf16[4,336,128]{2,1,0:T(8,128)(2,1)} %get-tuple-element.42.refs_1_, bf16[8,336,128]{2,1,0:T(8,128)(2,1)} %copy-done, bf16[8,336,128]{2,1,0:T(8,128)(2,1)} %copy-done.15, ...), custom_call_target="tpu_custom_call" | custom-call | flops 10000000000 | bytes 10000000 | tf_op jit(solution)/shard_map/score/pallas_call | solution.py:285
  41.6 3.5 %collective-permute-done.8 = bf16[4,336,128]{2,1,0:T(8,128)(2,1)S(1)} collective-permute-done((bf16[4,336,128]{2,1,0:T(8,128)(2,1)S(1)}, bf16[4,336,128]{2,1,0:T(8,128)(2,1)S(1)}, u32[]{:S(2)}, u32[]{:S(2)}) %collective-permute-start.8) | collective-permute-done | bytes 344096 | tf_op jit(solution)/shard_map/ppermute | solution.py:548
  45.2 1.2 %collective-permute-start.13 = (f32[16,128]{1,0:T(8,128)}, f32[16,128]{1,0:T(8,128)S(1)}, u32[]{:S(2)}, u32[]{:S(2)}) collective-permute-start(f32[16,128]{1,0:T(8,128)} %get-tuple-element.52.refs_0_), channel_id=1, source_target_pairs={{0,16},{1,17},{2,18},{3,19},{4,20},{5,21},{6,22},{7,23},{8,24},{9,... | collective-permute-start | bytes 24584 | tf_op jit(solution)/shard_map/ppermute | solution.py:548
  46.4 0.6 collective-permute-start.14
  47.1 2.1 %collective-permute-done.13.refs_2_ = f32[16,128]{1,0:T(8,128)S(1)} collective-permute-done((f32[16,128]{1,0:T(8,128)}, f32[16,128]{1,0:T(8,128)S(1)}, u32[]{:S(2)}, u32[]{:S(2)}) %collective-permute-start.13) | collective-permute-done | bytes 8224 | tf_op jit(solution)/shard_map/ppermute | solution.py:548
  50.3 1.5 %normalise.1 = bf16[64,128]{1,0:T(8,128)(2,1)} custom-call(s32[8,3]{1,0:T(8,128)} %get-tuple-element.58.partner_ref, f32[8,8,128]{2,1,0:T(8,128)} %get-tuple-element.59.weight_ref, f32[16,128]{1,0:T(8,128)} %get-tuple-element.52.refs_0_, f32[16,128]{1,0:T(8,128)} %copy-done.9, f32[16,128]{1,0:T(8,128)} %copy-done.10, f32[16,128]{1,0:T(8,128)} %copy-done.11), custom_call_target="tpu_custom_call" | custom-call | tf_op jit(solution)/shard_map/normalise/pallas_call | solution.py:338
  52.4 0.9 collective-permute-start.16
  54.7 4.9 %collective-permute-done.18 = bf16[64,128]{1,0:T(8,128)(2,1)S(1)} collective-permute-done((bf16[64,128]{1,0:T(8,128)(2,1)S(1)}, bf16[64,128]{1,0:T(8,128)(2,1)S(1)}, u32[]{:S(2)}, u32[]{:S(2)}) %collective-permute-start.18) | collective-permute-done | bytes 16416 | tf_op jit(solution)/shard_map/ppermute | solution.py:548
  59.6 3.7 %collective-permute-done.20 = bf16[64,128]{1,0:T(8,128)(2,1)S(1)} collective-permute-done((bf16[64,128]{1,0:T(8,128)(2,1)S(1)}, bf16[64,128]{1,0:T(8,128)(2,1)S(1)}, u32[]{:S(2)}, u32[]{:S(2)}) %collective-permute-start.20) | collective-permute-done | bytes 16416 | tf_op jit(solution)/shard_map/ppermute | solution.py:548
  63.3 1.5 %collective-permute-start.25 = (bf16[256,128]{1,0:T(8,128)(2,1)S(1)}, bf16[256,128]{1,0:T(8,128)(2,1)S(1)}, u32[]{:S(2)}, u32[]{:S(2)}) collective-permute-start(bf16[256,128]{1,0:T(8,128)(2,1)S(1)} %pad_maximum_fusion.1.refs_7_), channel_id=1, source_target_pairs={{0,1},{1,0},{2,3},{3,2},{4,5},{5,4},{6,7},{7,6},{8,9},{9,8},{10,11... | collective-permute-start | bytes 196616 | tf_op jit(solution)/shard_map/ppermute | solution.py:548
  64.9 1.9 %collective-permute-start.23 = (bf16[12,336,128]{2,1,0:T(8,128)(2,1)S(1)}, bf16[12,336,128]{2,1,0:T(8,128)(2,1)}, u32[]{:S(2)}, u32[]{:S(2)}) collective-permute-start(bf16[12,336,128]{2,1,0:T(8,128)(2,1)S(1)} %pad_maximum_fusion), channel_id=1, source_target_pairs={{0,6},{1,7},{2,0},{3,1},{4,2},{5,3},{6,4},{7,5},{8,14},{9,15},{10,... | collective-permute-start | bytes 3096584 | tf_op jit(solution)/shard_map/ppermute | solution.py:548
  66.7 0.6 collective-permute-start.21
  67.4 1.4 %collective-permute-start.22 = (bf16[4,336,128]{2,1,0:T(8,128)(2,1)S(1)}, bf16[4,336,128]{2,1,0:T(8,128)(2,1)S(1)}, u32[]{:S(2)}, u32[]{:S(2)}) collective-permute-start(bf16[4,336,128]{2,1,0:T(8,128)(2,1)S(1)} %collective-permute-done.16), channel_id=1, source_target_pairs={{0,1},{1,0},{2,3},{3,2},{4,5},{5,4},{6,7},{7,6},{8,24},{9,25},{10,... | collective-permute-start | bytes 1032200 | tf_op jit(solution)/shard_map/ppermute | solution.py:548
  68.9 0.8 copy-done.4
  69.7 17.8 %class_sum.2 = (f32[16000,128]{1,0:T(8,128)}, f32[56,128]{1,0:T(8,128)}) custom-call(bf16[4,336,128]{2,1,0:T(8,128)(2,1)} %get-tuple-element.49.refs_0_, bf16[4,336,128]{2,1,0:T(8,128)(2,1)} %get-tuple-element.42.refs_1_, bf16[8,336,128]{2,1,0:T(8,128)(2,1)} %copy-done, bf16[8,336,128]{2,1,0:T(8,128)(2,1)} %copy-done.15, bf16[24,336,128]{2,1,0:T(8,128)(2,1)} %copy-done.7, ...), custom_call_target="tpu_custom_call" | custom-call | flops 16000000000 | bytes 10000000 | tf_op jit(solution)/shard_map/class_sum/pallas_call | solution.py:512
  88.6 3.8 %collective-permute-done.17.refs_0_ = bf16[8,336,128]{2,1,0:T(8,128)(2,1)S(1)} collective-permute-done((bf16[8,336,128]{2,1,0:T(8,128)(2,1)}, bf16[8,336,128]{2,1,0:T(8,128)(2,1)S(1)}, u32[]{:S(2)}, u32[]{:S(2)}) %collective-permute-start.17) | collective-permute-done | bytes 688160 | tf_op jit(solution)/shard_map/ppermute | solution.py:548
  92.5 0.8 copy-done.16
  93.9 16.3 %class_sum.3 = bf16[50,36864]{1,0:T(8,128)(2,1)} custom-call(bf16[8,336,128]{2,1,0:T(8,128)(2,1)} %copy-done.16, bf16[4,336,128]{2,1,0:T(8,128)(2,1)} %copy-done.18, bf16[4,336,128]{2,1,0:T(8,128)(2,1)} %copy-done.19, bf16[12,336,128]{2,1,0:T(8,128)(2,1)} %collective-permute-done.23.refs_3_, bf16[4,336,128]{2,1,0:T(8,128)(2,1)} %copy-done.20, ...), custom_call_target="tpu_custom_call" | custom-call | flops 9600000000 | bytes 10000000 | tf_op jit(solution)/shard_map/class_sum/pallas_call | solution.py:512
  (92 shorter events, 7.4 us)
Async XLA Ops:
  1.0 2.6 %collective-permute-start.2 = (bf16[4,288,128]{2,1,0:T(8,128)(2,1)S(1)}, bf16[4,288,128]{2,1,0:T(8,128)(2,1)S(1)}, u32[]{:S(2)}, u32[]{:S(2)}) collective-permute-start(bf16[4,288,128]{2,1,0:T(8,128)(2,1)S(1)} %bitcast.4), channel_id=1, source_target_pairs={{0,8},{1,9},{2,10},{3,11},{4,12},{5,13},{6,14},{7,15},{8,0},{9,1},... | collective-permute-start | bytes 884744 | tf_op jit(solution)/shard_map/ppermute | solution.py:548
  1.5 2.1 %collective-permute-start = (s32[4,8]{1,0:T(4,128)}, s32[4,8]{1,0:T(4,128)S(1)}, u32[]{:S(2)}, u32[]{:S(2)}) collective-permute-start(s32[4,8]{1,0:T(4,128)} %near_ref.1), channel_id=1, source_target_pairs={{0,8},{1,9},{2,10},{3,11},{4,12},{5,13},{6,14},{7,15},{8,0},{9,1},... | collective-permute-start | bytes 392 | tf_op jit(solution)/shard_map/ppermute | solution.py:548
  2.4 1.3 %collective-permute-start.1 = (s32[4,2]{1,0:T(4,128)S(1)}, s32[4,2]{1,0:T(4,128)S(1)}, u32[]{:S(2)}, u32[]{:S(2)}) collective-permute-start(s32[4,2]{1,0:T(4,128)S(1)} %copy.8.near_off), channel_id=1, source_target_pairs={{0,8},{1,9},{2,10},{3,11},{4,12},{5,13},{6,14},{7,15},{8,0},{9,1},... | collective-permute-start | bytes 104 | tf_op jit(solution)/shard_map/ppermute | solution.py:548
  9.0 19.7 %copy-start.17 = (bf16[4,336,128]{2,1,0:T(8,128)(2,1)S(1)}, bf16[4,336,128]{2,1,0:T(8,128)(2,1)}, u32[]{:S(2)}) copy-start(bf16[4,336,128]{2,1,0:T(8,128)(2,1)} %get-tuple-element.49.refs_0_) | copy-start | bytes 1032196
  9.0 13.0 %collective-permute-start.3 = (bf16[4,336,128]{2,1,0:T(8,128)(2,1)}, bf16[4,336,128]{2,1,0:T(8,128)(2,1)S(1)}, u32[]{:S(2)}, u32[]{:S(2)}) collective-permute-start(bf16[4,336,128]{2,1,0:T(8,128)(2,1)} %get-tuple-element.49.refs_0_), channel_id=1, source_target_pairs={{0,16},{1,17},{2,18},{3,19},{4,20},{5,21},{6,22},{7,23},{8,9},{9,8... | collective-permute-start | bytes 1032200 | tf_op jit(solution)/shard_map/ppermute | solution.py:548
  11.8 10.2 %collective-permute-start.4 = (bf16[4,336,128]{2,1,0:T(8,128)(2,1)}, bf16[4,336,128]{2,1,0:T(8,128)(2,1)S(1)}, u32[]{:S(2)}, u32[]{:S(2)}) collective-permute-start(bf16[4,336,128]{2,1,0:T(8,128)(2,1)} %get-tuple-element.49.refs_0_), channel_id=1, source_target_pairs={{0,1},{1,0},{2,3},{3,2},{4,5},{5,4},{6,7},{7,6},{8,24},{9,25},{10,... | collective-permute-start | bytes 1032200 | tf_op jit(solution)/shard_map/ppermute | solution.py:548
  13.4 11.7 %collective-permute-start.5 = (bf16[4,336,128]{2,1,0:T(8,128)(2,1)}, bf16[4,336,128]{2,1,0:T(8,128)(2,1)S(1)}, u32[]{:S(2)}, u32[]{:S(2)}) collective-permute-start(bf16[4,336,128]{2,1,0:T(8,128)(2,1)} %get-tuple-element.49.refs_0_), channel_id=1, source_target_pairs={{0,2},{1,3},{2,4},{3,5},{4,6},{5,7},{6,0},{7,1},{8,10},{9,11},{10,... | collective-permute-start | bytes 1032200 | tf_op jit(solution)/shard_map/ppermute | solution.py:548
  25.1 2.7 %collective-permute-start.6 = (bf16[8,336,128]{2,1,0:T(8,128)(2,1)S(1)}, bf16[8,336,128]{2,1,0:T(8,128)(2,1)S(1)}, u32[]{:S(2)}, u32[]{:S(2)}) collective-permute-start(bf16[8,336,128]{2,1,0:T(8,128)(2,1)S(1)} %constant_dynamic-update-slice_fusion.refs_2_), channel_id=1, source_target_pairs={{0,8},{1,9},{2,10},{3,11},{4,12},{5,13},{6,14},{7,15},{8,0},{9,1},... | collective-permute-start | bytes 2064392 | tf_op jit(solution)/shard_map/ppermute | solution.py:548
  25.2 19.9 %collective-permute-start.10 = (bf16[4,336,128]{2,1,0:T(8,128)(2,1)S(1)}, bf16[4,336,128]{2,1,0:T(8,128)(2,1)S(1)}, u32[]{:S(2)}, u32[]{:S(2)}) collective-permute-start(bf16[4,336,128]{2,1,0:T(8,128)(2,1)S(1)} %collective-permute-done.5), channel_id=1, source_target_pairs={{0,1},{1,0},{2,3},{3,2},{4,5},{5,4},{6,7},{7,6},{8,24},{9,25},{10,... | collective-permute-start | bytes 1032200 | tf_op jit(solution)/shard_map/ppermute | solution.py:548
  25.8 19.3 %collective-permute-start.7 = (bf16[4,336,128]{2,1,0:T(8,128)(2,1)S(1)}, bf16[4,336,128]{2,1,0:T(8,128)(2,1)S(1)}, u32[]{:S(2)}, u32[]{:S(2)}) collective-permute-start(bf16[4,336,128]{2,1,0:T(8,128)(2,1)S(1)} %collective-permute-done.5), channel_id=1, source_target_pairs={{0,2},{1,3},{2,4},{3,5},{4,6},{5,7},{6,0},{7,1},{8,10},{9,11},{10,... | collective-permute-start | bytes 1032200 | tf_op jit(solution)/shard_map/ppermute | solution.py:548
  25.8 19.3 %collective-permute-start.9 = (bf16[4,336,128]{2,1,0:T(8,128)(2,1)S(1)}, bf16[4,336,128]{2,1,0:T(8,128)(2,1)S(1)}, u32[]{:S(2)}, u32[]{:S(2)}) collective-permute-start(bf16[4,336,128]{2,1,0:T(8,128)(2,1)S(1)} %collective-permute-done.5), channel_id=1, source_target_pairs={{0,16},{1,17},{2,18},{3,19},{4,20},{5,21},{6,22},{7,23},{8,9},{9,8... | collective-permute-start | bytes 1032200 | tf_op jit(solution)/shard_map/ppermute | solution.py:548
  26.4 18.8 %collective-permute-start.11 = (bf16[4,336,128]{2,1,0:T(8,128)(2,1)S(1)}, bf16[4,336,128]{2,1,0:T(8,128)(2,1)S(1)}, u32[]{:S(2)}, u32[]{:S(2)}) collective-permute-start(bf16[4,336,128]{2,1,0:T(8,128)(2,1)S(1)} %collective-permute-done.3), channel_id=1, source_target_pairs={{0,1},{1,0},{2,3},{3,2},{4,5},{5,4},{6,7},{7,6},{8,24},{9,25},{10,... | collective-permute-start | bytes 1032200 | tf_op jit(solution)/shard_map/ppermute | solution.py:548
  28.8 16.3 %collective-permute-start.8 = (bf16[4,336,128]{2,1,0:T(8,128)(2,1)S(1)}, bf16[4,336,128]{2,1,0:T(8,128)(2,1)S(1)}, u32[]{:S(2)}, u32[]{:S(2)}) collective-permute-start(bf16[4,336,128]{2,1,0:T(8,128)(2,1)S(1)} %copy-done.17), channel_id=1, source_target_pairs={{0,6},{1,7},{2,0},{3,1},{4,2},{5,3},{6,4},{7,5},{8,14},{9,15},{10,... | collective-permute-start | bytes 1032200 | tf_op jit(solution)/shard_map/ppermute | solution.py:548
  45.1 1.9 %collective-permute-start.12 = (f32[16,128]{1,0:T(8,128)}, f32[16,128]{1,0:T(8,128)S(1)}, u32[]{:S(2)}, u32[]{:S(2)}) collective-permute-start(f32[16,128]{1,0:T(8,128)} %get-tuple-element.52.refs_0_), channel_id=1, source_target_pairs={{0,8},{1,9},{2,10},{3,11},{4,12},{5,13},{6,14},{7,15},{8,0},{9,1},... | collective-permute-start | bytes 24584 | tf_op jit(solution)/shard_map/ppermute | solution.py:548
  45.2 3.9 %collective-permute-start.13 = (f32[16,128]{1,0:T(8,128)}, f32[16,128]{1,0:T(8,128)S(1)}, u32[]{:S(2)}, u32[]{:S(2)}) collective-permute-start(f32[16,128]{1,0:T(8,128)} %get-tuple-element.52.refs_0_), channel_id=1, source_target_pairs={{0,16},{1,17},{2,18},{3,19},{4,20},{5,21},{6,22},{7,23},{8,24},{9,... | collective-permute-start | bytes 24584 | tf_op jit(solution)/shard_map/ppermute | solution.py:548
  46.4 3.3 %collective-permute-start.14 = (f32[16,128]{1,0:T(8,128)}, f32[16,128]{1,0:T(8,128)S(1)}, u32[]{:S(2)}, u32[]{:S(2)}) collective-permute-start(f32[16,128]{1,0:T(8,128)} %get-tuple-element.52.refs_0_), channel_id=1, source_target_pairs={{0,24},{1,25},{2,26},{3,27},{4,28},{5,29},{6,30},{7,31},{8,16},{9,... | collective-permute-start | bytes 24584 | tf_op jit(solution)/shard_map/ppermute | solution.py:548
  51.9 12.9 %copy-start.1 = (bf16[8,336,128]{2,1,0:T(8,128)(2,1)S(1)}, bf16[8,336,128]{2,1,0:T(8,128)(2,1)}, u32[]{:S(2)}) copy-start(bf16[8,336,128]{2,1,0:T(8,128)(2,1)} %copy-done) | copy-start | bytes 2064388
  52.2 16.7 %copy-start.7 = (bf16[24,336,128]{2,1,0:T(8,128)(2,1)}, bf16[24,336,128]{2,1,0:T(8,128)(2,1)S(1)}, u32[]{:S(2)}) copy-start(bf16[24,336,128]{2,1,0:T(8,128)(2,1)S(1)} %constant_dynamic-update-slice_fusion.4.refs_4_) | copy-start | bytes 6193156
  52.2 16.7 %collective-permute-start.24 = (bf16[24,336,128]{2,1,0:T(8,128)(2,1)S(1)}, bf16[24,336,128]{2,1,0:T(8,128)(2,1)}, u32[]{:S(2)}, u32[]{:S(2)}) collective-permute-start(bf16[24,336,128]{2,1,0:T(8,128)(2,1)S(1)} %constant_dynamic-update-slice_fusion.4.refs_4_), channel_id=1, source_target_pairs={{0,8},{1,9},{2,10},{3,11},{4,12},{5,13},{6,14},{7,15},{8,0},{9,1},... | collective-permute-start | bytes 6193160 | tf_op jit(solution)/shard_map/ppermute | solution.py:548
  52.4 10.9 %collective-permute-start.16 = (bf16[4,336,128]{2,1,0:T(8,128)(2,1)S(1)}, bf16[4,336,128]{2,1,0:T(8,128)(2,1)S(1)}, u32[]{:S(2)}, u32[]{:S(2)}) collective-permute-start(bf16[4,336,128]{2,1,0:T(8,128)(2,1)S(1)} %collective-permute-done.7), channel_id=1, source_target_pairs={{0,16},{1,17},{2,18},{3,19},{4,20},{5,21},{6,22},{7,23},{8,9},{9,8... | collective-permute-start | bytes 1032200 | tf_op jit(solution)/shard_map/ppermute | solution.py:548
  53.3 14.1 %collective-permute-start.15 = (bf16[4,336,128]{2,1,0:T(8,128)(2,1)S(1)}, bf16[4,336,128]{2,1,0:T(8,128)(2,1)S(1)}, u32[]{:S(2)}, u32[]{:S(2)}) collective-permute-start(bf16[4,336,128]{2,1,0:T(8,128)(2,1)S(1)} %collective-permute-done.9), channel_id=1, source_target_pairs={{0,1},{1,0},{2,3},{3,2},{4,5},{5,4},{6,7},{7,6},{8,24},{9,25},{10,... | collective-permute-start | bytes 1032200 | tf_op jit(solution)/shard_map/ppermute | solution.py:548
  53.8 5.7 %collective-permute-start.18 = (bf16[64,128]{1,0:T(8,128)(2,1)S(1)}, bf16[64,128]{1,0:T(8,128)(2,1)S(1)}, u32[]{:S(2)}, u32[]{:S(2)}) collective-permute-start(bf16[64,128]{1,0:T(8,128)(2,1)S(1)} %copy-done.6), channel_id=1, source_target_pairs={{0,2},{1,3},{2,4},{3,5},{4,6},{5,7},{6,0},{7,1},{8,10},{9,11},{10,... | collective-permute-start | bytes 49160 | tf_op jit(solution)/shard_map/ppermute | solution.py:548
  54.4 5.1 %collective-permute-start.19 = (bf16[64,128]{1,0:T(8,128)(2,1)S(1)}, bf16[64,128]{1,0:T(8,128)(2,1)S(1)}, u32[]{:S(2)}, u32[]{:S(2)}) collective-permute-start(bf16[64,128]{1,0:T(8,128)(2,1)S(1)} %copy-done.6), channel_id=1, source_target_pairs={{0,4},{1,5},{2,6},{3,7},{4,0},{5,1},{6,2},{7,3},{8,12},{9,13},{10,... | collective-permute-start | bytes 49160 | tf_op jit(solution)/shard_map/ppermute | solution.py:548
  59.5 3.7 %collective-permute-start.20 = (bf16[64,128]{1,0:T(8,128)(2,1)S(1)}, bf16[64,128]{1,0:T(8,128)(2,1)S(1)}, u32[]{:S(2)}, u32[]{:S(2)}) collective-permute-start(bf16[64,128]{1,0:T(8,128)(2,1)S(1)} %copy-done.6), channel_id=1, source_target_pairs={{0,6},{1,7},{2,0},{3,1},{4,2},{5,3},{6,4},{7,5},{8,14},{9,15},{10,... | collective-permute-start | bytes 49160 | tf_op jit(solution)/shard_map/ppermute | solution.py:548
  63.3 5.5 %collective-permute-start.25 = (bf16[256,128]{1,0:T(8,128)(2,1)S(1)}, bf16[256,128]{1,0:T(8,128)(2,1)S(1)}, u32[]{:S(2)}, u32[]{:S(2)}) collective-permute-start(bf16[256,128]{1,0:T(8,128)(2,1)S(1)} %pad_maximum_fusion.1.refs_7_), channel_id=1, source_target_pairs={{0,1},{1,0},{2,3},{3,2},{4,5},{5,4},{6,7},{7,6},{8,9},{9,8},{10,11... | collective-permute-start | bytes 196616 | tf_op jit(solution)/shard_map/ppermute | solution.py:548
  64.9 22.7 %collective-permute-start.23 = (bf16[12,336,128]{2,1,0:T(8,128)(2,1)S(1)}, bf16[12,336,128]{2,1,0:T(8,128)(2,1)}, u32[]{:S(2)}, u32[]{:S(2)}) collective-permute-start(bf16[12,336,128]{2,1,0:T(8,128)(2,1)S(1)} %pad_maximum_fusion), channel_id=1, source_target_pairs={{0,6},{1,7},{2,0},{3,1},{4,2},{5,3},{6,4},{7,5},{8,14},{9,15},{10,... | collective-permute-start | bytes 3096584 | tf_op jit(solution)/shard_map/ppermute | solution.py:548
  66.7 20.8 %collective-permute-start.21 = (bf16[4,336,128]{2,1,0:T(8,128)(2,1)S(1)}, bf16[4,336,128]{2,1,0:T(8,128)(2,1)S(1)}, u32[]{:S(2)}, u32[]{:S(2)}) collective-permute-start(bf16[4,336,128]{2,1,0:T(8,128)(2,1)S(1)} %collective-permute-done.7), channel_id=1, source_target_pairs={{0,1},{1,0},{2,3},{3,2},{4,5},{5,4},{6,7},{7,6},{8,24},{9,25},{10,... | collective-permute-start | bytes 1032200 | tf_op jit(solution)/shard_map/ppermute | solution.py:548
  67.4 20.2 %collective-permute-start.22 = (bf16[4,336,128]{2,1,0:T(8,128)(2,1)S(1)}, bf16[4,336,128]{2,1,0:T(8,128)(2,1)S(1)}, u32[]{:S(2)}, u32[]{:S(2)}) collective-permute-start(bf16[4,336,128]{2,1,0:T(8,128)(2,1)S(1)} %collective-permute-done.16), channel_id=1, source_target_pairs={{0,1},{1,0},{2,3},{3,2},{4,5},{5,4},{6,7},{7,6},{8,24},{9,25},{10,... | collective-permute-start | bytes 1032200 | tf_op jit(solution)/shard_map/ppermute | solution.py:548
  87.5 4.9 %collective-permute-start.28 = (bf16[12,336,128]{2,1,0:T(8,128)(2,1)}, bf16[12,336,128]{2,1,0:T(8,128)(2,1)S(1)}, u32[]{:S(2)}, u32[]{:S(2)}) collective-permute-start(bf16[12,336,128]{2,1,0:T(8,128)(2,1)} %collective-permute-done.23.refs_3_), channel_id=1, source_target_pairs={{0,8},{1,9},{2,10},{3,11},{4,12},{5,13},{6,14},{7,15},{8,0},{9,1},... | collective-permute-start | bytes 3096584 | tf_op jit(solution)/shard_map/ppermute | solution.py:548
  87.6 4.8 %collective-permute-start.17 = (bf16[8,336,128]{2,1,0:T(8,128)(2,1)}, bf16[8,336,128]{2,1,0:T(8,128)(2,1)S(1)}, u32[]{:S(2)}, u32[]{:S(2)}) collective-permute-start(bf16[8,336,128]{2,1,0:T(8,128)(2,1)} %copy-done.4), channel_id=1, source_target_pairs={{0,8},{1,9},{2,10},{3,11},{4,12},{5,13},{6,14},{7,15},{8,0},{9,1},... | collective-permute-start | bytes 2064392 | tf_op jit(solution)/shard_map/ppermute | solution.py:548
  88.1 4.3 %collective-permute-start.26 = (bf16[4,336,128]{2,1,0:T(8,128)(2,1)S(1)}, bf16[4,336,128]{2,1,0:T(8,128)(2,1)S(1)}, u32[]{:S(2)}, u32[]{:S(2)}) collective-permute-start(bf16[4,336,128]{2,1,0:T(8,128)(2,1)S(1)} %collective-permute-done.21.refs_1_), channel_id=1, source_target_pairs={{0,8},{1,9},{2,10},{3,11},{4,12},{5,13},{6,14},{7,15},{8,0},{9,1},... | collective-permute-start | bytes 1032200 | tf_op jit(solution)/shard_map/ppermute | solution.py:548
  88.2 4.2 %collective-permute-start.27 = (bf16[4,336,128]{2,1,0:T(8,128)(2,1)S(1)}, bf16[4,336,128]{2,1,0:T(8,128)(2,1)S(1)}, u32[]{:S(2)}, u32[]{:S(2)}) collective-permute-start(bf16[4,336,128]{2,1,0:T(8,128)(2,1)S(1)} %collective-permute-done.22.refs_2_), channel_id=1, source_target_pairs={{0,8},{1,9},{2,10},{3,11},{4,12},{5,13},{6,14},{7,15},{8,0},{9,1},... | collective-permute-start | bytes 1032200 | tf_op jit(solution)/shard_map/ppermute | solution.py:548
  (20 other events, 41.6 us)
